TPU v7x, 128 devices: a whole 4x4x4 slice. The times are simulated.
128 devices in a mesh: fsdp: 32 (over x, y, core), ctx: 2 (over z_hi), tp: 2 (over z_lo).
Axes of the slice: x: 4, y: 4, z: 4 (z_hi: 2, z_lo: 2; z = z_hi * 2 + z_lo), core: 2. Of those that a mesh axis runs over, the one named last changes fastest.
Arguments:
- tokens: bfloat16 [32, 1024, 1536], P('fsdp', 'ctx'), may hold values from -6 to 6
- segments: int32 [32, 1024], P('fsdp'), may hold values from 0 to 2, as said below
- routes: int32 [32, 1024, 4], P('fsdp', 'ctx'), may hold values from 0 to 7, all different within a row; in each aligned block of 512 rows (0 to 511, 512 to 1023, ..., all dimensions but the last counted through in order) at most 320 rows name the same one
- attn_gain: bfloat16 [1536], P(('fsdp', 'ctx')), may hold values from 0.25 to 1.75
- w_query: bfloat16 [1536, 1536], P(('fsdp', 'ctx'), 'tp'), may hold values from -0.15625 to 0.15625
- key_matrix: bfloat16 [1536, 256], P(('fsdp', 'ctx'), 'tp'), may hold values from -0.15625 to 0.15625
- value_matrix: bfloat16 [1536, 256], P(('fsdp', 'ctx'), 'tp'), may hold values from -0.15625 to 0.15625
- w_output: bfloat16 [1536, 1536], P('tp', ('fsdp', 'ctx')), may hold values from -1.75 to 1.75
- mix_gain: bfloat16 [1536], P(('fsdp', 'ctx')), may hold values from 0.25 to 1.75
- w_router: bfloat16 [1536, 8], P(('fsdp', 'ctx')), may hold values from -0.078125 to 0.078125
- w_gate: bfloat16 [8, 1536, 768], P(None, ('fsdp', 'ctx'), 'tp'), may hold values from -0.15625 to 0.15625
- w_up: bfloat16 [8, 1536, 768], P(None, ('fsdp', 'ctx'), 'tp'), may hold values from -0.15625 to 0.15625
- w_down: bfloat16 [8, 1536, 768], P(None, ('fsdp', 'ctx'), 'tp'), may hold values from -0.21875 to 0.21875
- block_cotangent: bfloat16 [32, 1024, 1536], P('fsdp', 'ctx'), may hold values from -6 to 6
Outputs:
- block_out: bfloat16 [32, 1024, 1536], P('fsdp', 'ctx')
- tokens_grad: float32 [32, 1024, 1536], P('fsdp', 'ctx')
- grad_attn_gain: float32 [1536], P(('fsdp', 'ctx'))
- grad_query: float32 [1536, 1536], P(('fsdp', 'ctx'), 'tp')
- grad_key: float32 [1536, 256], P(('fsdp', 'ctx'), 'tp')
- grad_value: float32 [1536, 256], P(('fsdp', 'ctx'), 'tp')
- grad_output: float32 [1536, 1536], P('tp', ('fsdp', 'ctx'))
- grad_mix_gain: float32 [1536], P(('fsdp', 'ctx'))
- grad_router: float32 [1536, 8], P(('fsdp', 'ctx'))
- grad_gate: float32 [8, 1536, 768], P(None, ('fsdp', 'ctx'), 'tp')
- grad_up: float32 [8, 1536, 768], P(None, ('fsdp', 'ctx'), 'tp')
- grad_down: float32 [8, 1536, 768], P(None, ('fsdp', 'ctx'), 'tp')
Inputs may be any that keep to these rules, and one draw needn't show every extreme that they name: `segments`: segment numbers never fall along a sequence; every sequence holds documents 0, 1 and 2, the first and the last of 128 to 384 positions. `routes`: each row names 4 different experts; in the 512 rows of one index of ctx no expert is named more than 320 times.
All inputs are finite; a program needn't handle non-finite values.
Results may differ from a plain program's by a relative error of at most 0.015.
Values may be sent and summed in bfloat16 or wider, within the bound.
A program may use at most 256 MiB of HBM per device.

v0:
```python
import jax
import jax.numpy as jnp
from jax import lax
from jax.sharding import PartitionSpec as P

QUERY_HEADS = 12
KEY_VALUE_HEADS = 2
HEAD_SIZE = 128


EPS = 1e-06
ROPE_BASE = 1000000.0
NEG_FILL = -1e30


def rope_tables(positions):
    half_dim = HEAD_SIZE // 2
    frequency = ROPE_BASE ** (-jnp.arange(half_dim, dtype=jnp.float32) * (2.0 / HEAD_SIZE))
    angles = positions.astype(jnp.float32)[:, None] * frequency[None, :]
    angles = jnp.concatenate([angles, angles], axis=1)
    return (jnp.cos(angles)[:, None, :], jnp.sin(angles)[:, None, :])


def rotary_embed(value_rows, cosine_table, sine_table):
    half_dim = HEAD_SIZE // 2
    turned = jnp.concatenate([-value_rows[..., half_dim:], value_rows[..., :half_dim]], axis=-1)
    return value_rows * cosine_table + turned * sine_table


def rotate_back(grad_vals, cosine_table, sine_table):
    half_dim = HEAD_SIZE // 2
    scaled = grad_vals * sine_table
    turned = jnp.concatenate([scaled[..., half_dim:], -scaled[..., :half_dim]], axis=-1)
    return grad_vals * cosine_table + turned


def slot_tables(route_rows, experts, capacity, top_k):
    flat_routes = route_rows.reshape(-1)
    hot_slots = (flat_routes[:, None] == jnp.arange(experts, dtype=jnp.int32)[None, :]).astype(
        jnp.int32
    )
    before = jnp.cumsum(hot_slots, axis=0) - hot_slots
    slot_pos = jnp.sum(before * hot_slots, axis=1)
    slot_place = flat_routes * capacity + slot_pos
    pair_ids = jnp.arange(flat_routes.shape[0], dtype=jnp.int32)
    slot_owner = jnp.zeros((experts * capacity,), jnp.int32).at[slot_place].set(pair_ids // top_k)
    slot_pair = jnp.zeros((experts * capacity,), jnp.int32).at[slot_place].set(pair_ids)
    filled = jnp.zeros((experts * capacity,), jnp.float32).at[slot_place].set(1.0)
    return (slot_place, slot_owner, slot_pair, filled)


def body(
    tokens,
    segments,
    routes,
    attn_gain,
    w_query,
    key_matrix,
    value_matrix,
    w_output,
    mix_gain,
    w_router,
    w_gate,
    w_up,
    w_down,
    block_cotangent,
):
    f32 = jnp.float32
    bf16 = jnp.bfloat16
    local_rows = tokens.shape[1]
    model_width = tokens.shape[2]
    ctx_count = lax.axis_size("ctx")
    seq_length = local_rows * ctx_count
    q_width = w_query.shape[1]
    kv_heads = key_matrix.shape[1] // HEAD_SIZE
    heads_per_group = QUERY_HEADS // KEY_VALUE_HEADS
    experts = w_gate.shape[0]
    top_k = routes.shape[2]
    capacity = local_rows * top_k * 5 // (4 * experts)
    score_scale = HEAD_SIZE ** (-0.5)
    block_rows = min(local_rows, 512)
    block_count = local_rows // block_rows
    inputs = tokens[0].astype(f32)
    upstream = block_cotangent[0].astype(f32)
    seg_all = segments[0]
    route_rows = routes[0]
    first_row = lax.axis_index("ctx") * local_rows
    positions = first_row + jnp.arange(local_rows, dtype=jnp.int32)
    key_positions = jnp.arange(seq_length, dtype=jnp.int32)
    seg_local = lax.dynamic_slice_in_dim(seg_all, first_row, local_rows)
    cosine_table, sine_table = rope_tables(positions)
    query_full, key_full, value_full, attn_full, mix_full, router_full = (
        lax.all_gather(w_query, ("fsdp", "ctx"), axis=0, tiled=True),
        lax.all_gather(key_matrix, ("fsdp", "ctx"), axis=0, tiled=True),
        lax.all_gather(value_matrix, ("fsdp", "ctx"), axis=0, tiled=True),
        lax.all_gather(attn_gain, ("fsdp", "ctx"), axis=0, tiled=True),
        lax.all_gather(mix_gain, ("fsdp", "ctx"), axis=0, tiled=True),
        lax.all_gather(w_router, ("fsdp", "ctx"), axis=0, tiled=True),
    )
    attn_scale = attn_full.astype(f32)
    mix_scale = mix_full.astype(f32)
    inv_attn = lax.rsqrt(jnp.mean(inputs * inputs, axis=1, keepdims=True) + EPS)
    scaled_in = inputs * inv_attn
    normalized_input = (scaled_in * attn_scale).astype(bf16)
    query_rows = jnp.dot(normalized_input, query_full, preferred_element_type=f32)
    keys_raw = jnp.dot(normalized_input, key_full, preferred_element_type=f32)
    values_raw = jnp.dot(normalized_input, value_full, preferred_element_type=f32)
    q_heads = rotary_embed(
        query_rows.reshape(local_rows, q_width // HEAD_SIZE, HEAD_SIZE), cosine_table, sine_table
    ).astype(bf16)
    k_heads = rotary_embed(
        keys_raw.reshape(local_rows, kv_heads, HEAD_SIZE), cosine_table, sine_table
    ).astype(bf16)
    v_heads = values_raw.astype(bf16).reshape(local_rows, kv_heads, HEAD_SIZE)
    all_keys, all_values = (
        lax.all_gather(k_heads, "ctx", axis=0, tiled=True),
        lax.all_gather(v_heads, "ctx", axis=0, tiled=True),
    )
    q_grouped = q_heads.reshape(local_rows, kv_heads, heads_per_group, HEAD_SIZE)

    def block_scores():
        attention_scores = (
            jnp.einsum("bgad,kgd->gabk", q_grouped, all_keys, preferred_element_type=f32)
            * score_scale
        )
        allowed = (seg_local[:, None] == seg_all[None, :]) & (
            positions[:, None] >= key_positions[None, :]
        )
        return (q_grouped, jnp.where(allowed[None, None], attention_scores, NEG_FILL))

    def attend(block_index):
        unused_query, masked = block_scores()
        row_peak = jnp.max(masked, axis=-1, keepdims=True)
        expo_vals = jnp.exp(masked - row_peak)
        row_total = jnp.sum(expo_vals, axis=-1, keepdims=True)
        weights_low = (expo_vals / row_total).astype(bf16)
        mixed_out = jnp.einsum(
            "gabk,kgd->bgad", weights_low, all_values, preferred_element_type=f32
        )
        return (mixed_out.reshape(block_rows, q_width), (row_peak + jnp.log(row_total))[..., 0])

    mixed_all, log_totals = lax.map(attend, jnp.arange(block_count))
    attended = mixed_all.reshape(local_rows, q_width).astype(bf16)
    branch_part = jnp.dot(
        attended,
        lax.all_gather(w_output, ("fsdp", "ctx"), axis=1, tiled=True),
        preferred_element_type=f32,
    )
    branch = lax.psum(branch_part, "tp")
    residual = inputs + branch
    inv_mix = lax.rsqrt(jnp.mean(residual * residual, axis=1, keepdims=True) + EPS)
    scaled_mix = residual * inv_mix
    normed_mix = (scaled_mix * mix_scale).astype(bf16)
    logits = jnp.dot(normed_mix, router_full, preferred_element_type=f32)
    hot_routes = (
        route_rows[:, :, None] == jnp.arange(experts, dtype=jnp.int32)[None, None, :]
    ).astype(f32)
    chosen = jnp.sum(hot_routes * logits[:, None, :], axis=-1)
    gate_expo = jnp.exp(chosen - jnp.max(chosen, axis=1, keepdims=True))
    gate_weights = gate_expo / jnp.sum(gate_expo, axis=1, keepdims=True)
    slot_place, slot_owner, slot_pair, filled = slot_tables(route_rows, experts, capacity, top_k)
    dispatched = (normed_mix[slot_owner] * filled[:, None].astype(bf16)).reshape(
        experts, capacity, model_width
    )
    gate_all, up_all, down_all = (
        lax.all_gather(w_gate, ("fsdp", "ctx"), axis=1, tiled=True),
        lax.all_gather(w_up, ("fsdp", "ctx"), axis=1, tiled=True),
        lax.all_gather(w_down, ("fsdp", "ctx"), axis=1, tiled=True),
    )
    gate_act = jnp.einsum("ecd,edf->ecf", dispatched, gate_all, preferred_element_type=f32)
    up_act = jnp.einsum("ecd,edf->ecf", dispatched, up_all, preferred_element_type=f32)
    hidden = (jax.nn.silu(gate_act) * up_act).astype(bf16)
    result = jnp.einsum("ecf,edf->ecd", hidden, down_all, preferred_element_type=f32).reshape(
        experts * capacity, model_width
    )
    gathered_out = result[slot_place].reshape(local_rows, top_k, model_width)
    mix_part = jnp.sum(gate_weights[:, :, None] * gathered_out, axis=1)
    gate_part = jnp.sum(upstream[:, None, :] * gathered_out, axis=-1)
    mix_out, gate_back = lax.psum((mix_part, gate_part), "tp")
    block_out = (residual + mix_out).astype(bf16)
    gate_mean = jnp.sum(gate_weights * gate_back, axis=1, keepdims=True)
    chosen_grad = gate_weights * (gate_back - gate_mean)
    logit_grad = jnp.sum(chosen_grad[:, :, None] * hot_routes, axis=1).astype(bf16)
    grad_router = jnp.einsum("rd,re->de", normed_mix, logit_grad, preferred_element_type=f32)
    router_back = jnp.einsum("re,de->rd", logit_grad, router_full, preferred_element_type=f32)
    slot_gate = gate_weights.reshape(-1)[slot_pair] * filled
    slot_grad = (
        (upstream[slot_owner] * slot_gate[:, None])
        .astype(bf16)
        .reshape(experts, capacity, model_width)
    )
    gate_use, up_use, down_use = (
        lax.all_gather(w_gate, ("fsdp", "ctx"), axis=1, tiled=True),
        lax.all_gather(w_up, ("fsdp", "ctx"), axis=1, tiled=True),
        lax.all_gather(w_down, ("fsdp", "ctx"), axis=1, tiled=True),
    )
    hidden_grad = jnp.einsum("ecd,edf->ecf", slot_grad, down_use, preferred_element_type=f32)
    sigmoid_act = jax.nn.sigmoid(gate_act)
    gate_low = (
        hidden_grad * up_act * (sigmoid_act * (1.0 + gate_act * (1.0 - sigmoid_act)))
    ).astype(bf16)
    up_low = (hidden_grad * jax.nn.silu(gate_act)).astype(bf16)
    dispatch_grad = (
        jnp.einsum("ecf,edf->ecd", gate_low, gate_use, preferred_element_type=f32)
        + jnp.einsum("ecf,edf->ecd", up_low, up_use, preferred_element_type=f32)
    ).reshape(experts * capacity, model_width)
    mix_back_part = jnp.sum(
        dispatch_grad[slot_place].reshape(local_rows, top_k, model_width), axis=1
    )
    mix_back = lax.psum(mix_back_part, "tp")
    normed_grad = mix_back + router_back
    grad_mix_gain = jnp.sum(normed_grad * scaled_mix, axis=0)
    scaled_grad = normed_grad * mix_scale
    resid_grad = (
        upstream
        + inv_mix * scaled_grad
        - residual * inv_mix**3 * jnp.mean(scaled_grad * residual, axis=1, keepdims=True)
    )
    grad_down = jnp.einsum("ecd,ecf->edf", slot_grad, hidden, preferred_element_type=f32)
    grad_gate = jnp.einsum("ecd,ecf->edf", dispatched, gate_low, preferred_element_type=f32)
    grad_up = jnp.einsum("ecd,ecf->edf", dispatched, up_low, preferred_element_type=f32)
    expert_parts = (
        lax.psum_scatter(grad_gate, ("fsdp", "ctx"), scatter_dimension=1, tiled=True),
        lax.psum_scatter(grad_up, ("fsdp", "ctx"), scatter_dimension=1, tiled=True),
        lax.psum_scatter(grad_down, ("fsdp", "ctx"), scatter_dimension=1, tiled=True),
        lax.psum_scatter(grad_router, ("fsdp", "ctx"), scatter_dimension=0, tiled=True),
        lax.psum_scatter(grad_mix_gain, ("fsdp", "ctx"), scatter_dimension=0, tiled=True),
    )
    branch_low = resid_grad.astype(bf16)
    attended_grad = jnp.einsum(
        "rc,qc->rq",
        branch_low,
        lax.all_gather(w_output, ("fsdp", "ctx"), axis=1, tiled=True),
        preferred_element_type=f32,
    )
    grad_output = jnp.einsum("rq,rd->qd", attended, branch_low, preferred_element_type=f32)
    back_low = attended_grad.astype(bf16).reshape(local_rows, kv_heads, heads_per_group, HEAD_SIZE)

    def back_block(running, block_index):
        key_acc, value_acc = running
        query_block, masked = block_scores()
        prob_vals = jnp.exp(masked - log_totals[block_index][..., None])
        prob_low = prob_vals.astype(bf16)
        prob_grad = jnp.einsum("bgad,kgd->gabk", back_low, all_values, preferred_element_type=f32)
        row_dot = jnp.sum(prob_vals * prob_grad, axis=-1, keepdims=True)
        score_grad = (prob_vals * (prob_grad - row_dot)).astype(bf16)
        query_grad = (
            jnp.einsum("gabk,kgd->bgad", score_grad, all_keys, preferred_element_type=f32)
            * score_scale
        )
        key_acc = key_acc + jnp.einsum(
            "gabk,bgad->kgd", score_grad, query_block, preferred_element_type=f32
        )
        value_acc = value_acc + jnp.einsum(
            "gabk,bgad->kgd", prob_low, back_low, preferred_element_type=f32
        )
        return ((key_acc, value_acc), query_grad.reshape(block_rows, q_width))

    zero_pair = (
        jnp.zeros((seq_length, kv_heads, HEAD_SIZE), f32),
        jnp.zeros((seq_length, kv_heads, HEAD_SIZE), f32),
    )
    (key_sum, value_sum), query_parts = lax.scan(back_block, zero_pair, jnp.arange(block_count))
    key_back, value_back = (
        lax.psum_scatter(
            key_sum.astype(jnp.bfloat16), "ctx", scatter_dimension=0, tiled=True
        ).astype(jnp.float32),
        lax.psum_scatter(
            value_sum.astype(jnp.bfloat16), "ctx", scatter_dimension=0, tiled=True
        ).astype(jnp.float32),
    )
    query_low = (
        rotate_back(
            query_parts.reshape(local_rows, q_width // HEAD_SIZE, HEAD_SIZE),
            cosine_table,
            sine_table,
        )
        .astype(bf16)
        .reshape(local_rows, q_width)
    )
    key_low = (
        rotate_back(key_back * score_scale, cosine_table, sine_table)
        .astype(bf16)
        .reshape(local_rows, kv_heads * HEAD_SIZE)
    )
    value_low = value_back.astype(bf16).reshape(local_rows, kv_heads * HEAD_SIZE)
    grad_query = jnp.einsum("rd,rq->dq", normalized_input, query_low, preferred_element_type=f32)
    grad_key = jnp.einsum("rd,rq->dq", normalized_input, key_low, preferred_element_type=f32)
    grad_value = jnp.einsum("rd,rq->dq", normalized_input, value_low, preferred_element_type=f32)
    pieces = lax.all_gather(
        (w_query, key_matrix, value_matrix), ("fsdp", "ctx"), axis=0, tiled=True
    )
    normed_part = (
        jnp.einsum("rq,dq->rd", query_low, pieces[0], preferred_element_type=f32)
        + jnp.einsum("rq,dq->rd", key_low, pieces[1], preferred_element_type=f32)
        + jnp.einsum("rq,dq->rd", value_low, pieces[2], preferred_element_type=f32)
    )
    normed_back = lax.psum(normed_part.astype(jnp.bfloat16), "tp").astype(jnp.float32)
    grad_attn_gain = jnp.sum(normed_back * scaled_in, axis=0)
    scaled_back = normed_back * attn_scale
    input_grad = (
        resid_grad
        + inv_attn * scaled_back
        - inputs * inv_attn**3 * jnp.mean(scaled_back * inputs, axis=1, keepdims=True)
    )
    attn_parts = (
        lax.psum_scatter(grad_query, ("fsdp", "ctx"), scatter_dimension=0, tiled=True),
        lax.psum_scatter(grad_key, ("fsdp", "ctx"), scatter_dimension=0, tiled=True),
        lax.psum_scatter(grad_value, ("fsdp", "ctx"), scatter_dimension=0, tiled=True),
        lax.psum_scatter(grad_output, ("fsdp", "ctx"), scatter_dimension=1, tiled=True),
        lax.psum_scatter(grad_attn_gain, ("fsdp", "ctx"), scatter_dimension=0, tiled=True),
    )
    return (
        block_out[None],
        input_grad[None],
        attn_parts[4],
        attn_parts[0],
        attn_parts[1],
        attn_parts[2],
        attn_parts[3],
        expert_parts[4],
        expert_parts[3],
        expert_parts[0],
        expert_parts[1],
        expert_parts[2],
    )


def solution(mesh):
    return jax.shard_map(
        body,
        mesh=mesh,
        in_specs=(
            P("fsdp", "ctx", None),
            P("fsdp", None),
            P("fsdp", "ctx", None),
            P(("fsdp", "ctx")),
            P(("fsdp", "ctx"), "tp"),
            P(("fsdp", "ctx"), "tp"),
            P(("fsdp", "ctx"), "tp"),
            P("tp", ("fsdp", "ctx")),
            P(("fsdp", "ctx")),
            P(("fsdp", "ctx"), None),
            P(None, ("fsdp", "ctx"), "tp"),
            P(None, ("fsdp", "ctx"), "tp"),
            P(None, ("fsdp", "ctx"), "tp"),
            P("fsdp", "ctx", None),
        ),
        out_specs=(
            P("fsdp", "ctx", None),
            P("fsdp", "ctx", None),
            P(("fsdp", "ctx")),
            P(("fsdp", "ctx"), "tp"),
            P(("fsdp", "ctx"), "tp"),
            P(("fsdp", "ctx"), "tp"),
            P("tp", ("fsdp", "ctx")),
            P(("fsdp", "ctx")),
            P(("fsdp", "ctx"), None),
            P(None, ("fsdp", "ctx"), "tp"),
            P(None, ("fsdp", "ctx"), "tp"),
            P(None, ("fsdp", "ctx"), "tp"),
        ),
        check_vma=False,
    )
```

profile of v0, /device:TPU:1, one launch (start us, length us, event | category | flops | bytes accessed | tf_op | source)
XLA Modules:
  0.0 2630.2 jit_solution(170719557347172662)
XLA Ops:
  14.8 170.3 %all-reduce.9 = (bf16[1536]{0:T(1024)(128)(2,1)S(1)}, bf16[1536]{0:T(1024)(128)(2,1)S(1)}) all-reduce(bf16[1536]{0:T(1024)(128)(2,1)S(1)} %dynamic-update-slice, bf16[1536]{0:T(1024)(128)(2,1)S(1)} %dynamic-update-slice.1), channel_id=1, replica_groups=mesh['fsdp'=32,'ctx'=2,'tp'=2] {'fsdp','ctx'}, use_global_device_ids=true, to_apply=%add | all-reduce | flops 3072 | bytes 12288
  185.2 162.8 %all_gather.46 = bf16[1536,128]{1,0:T(8,128)(2,1)S(1)} all-gather(bf16[24,128]{1,0:T(8,128)(2,1)} %param.19), channel_id=1, replica_groups=mesh['fsdp'=32,'ctx'=2,'tp'=2] {'fsdp','ctx'}, dimensions={0}, use_global_device_ids=true | all-gather | bytes 399360 | tf_op jit(solution)/shard_map/all_gather | solution.py:94
  358.0 166.6 %all_gather.44 = bf16[1536,128]{1,0:T(8,128)(2,1)S(1)} all-gather(bf16[24,128]{1,0:T(8,128)(2,1)S(1)} %copy-done.66), channel_id=1, replica_groups=mesh['fsdp'=32,'ctx'=2,'tp'=2] {'fsdp','ctx'}, dimensions={0}, use_global_device_ids=true | all-gather | bytes 399360 | tf_op jit(solution)/shard_map/all_gather | solution.py:95
  557.3 164.3 %all-gather.2 = bf16[64,24,8]{1,2,0:T(8,128)(2,1)S(1)} all-gather(bf16[1,24,8]{1,2,0:T(8,128)(2,1)S(1)} %bitcast.271), channel_id=1, replica_groups=mesh['fsdp'=32,'ctx'=2,'tp'=2] {'fsdp','ctx'}, dimensions={0}, use_global_device_ids=true | all-gather | bytes 24960 | tf_op jit(solution)/shard_map/all_gather | solution.py:98
  767.7 18.0 gather_fusion
  789.2 13.6 gather_fusion.3
  836.5 73.7 %all-gather.17.cloned.1.call-done = bf16[8,1536,384]{2,1,0:T(8,128)(2,1)} async-done(((bf16[8,24,384]{2,1,0:T(8,128)(2,1)}), bf16[8,1536,384]{2,1,0:T(8,128)(2,1)}) %all-gather.17.cloned.1.call-update) | async-done | bytes 9437200 | tf_op jit(solution)/shard_map/all_gather | solution.py:168
  910.2 14.9 multiply_convert_fusion.1
  925.1 14.0 fusion.133
  939.1 19.7 gather_fusion.1
  958.8 14.7 reshape.585
  973.5 17.6 multiply_reduce_fusion
  991.1 13.4 fusion.134
  1004.5 15.8 convolution_add_fusion
  1020.3 19.7 gather_fusion.4
  1040.0 14.7 reshape.587
  1072.5 151.7 %all-reduce.18.cloned.1.call-done = (f32[512,1536]{1,0:T(8,128)}, f32[512,1536]{1,0:T(8,128)}) async-done(((f32[512,1536]{1,0:T(8,128)}, f32[512,1536]{1,0:T(8,128)}), (f32[512,1536]{1,0:T(8,128)}, f32[512,1536]{1,0:T(8,128)})) %all-reduce.18.cloned.1.call-update) | async-done | bytes 6291472 | tf_op jit(solution)/shard_map/psum | solution.py:179
  1317.3 13.9 fusion.43
  1362.7 326.4 %all-reduce.7 = (f32[1536]{0:T(1024)S(1)}, f32[1536]{0:T(1024)S(1)}, f32[1536,8]{0,1:T(8,128)S(1)}) all-reduce(f32[1536]{0:T(1024)S(1)} %get-tuple-element.72, f32[1536]{0:T(1024)S(1)} %copy-done.62, f32[1536,8]{0,1:T(8,128)S(1)} %fusion.136), channel_id=6, replica_groups=mesh['fsdp'=32,'ctx'=2,'tp'=2] {'fsdp','ctx'}, use_global_device_ids=true, to_apply=%region_29.30.clone | all-reduce | flops 15360 | bytes 122880
  1695.4 121.2 %reduce-scatter.21.cloned.1.call-done = f32[768,24]{0,1:T(8,128)} async-done(((f32[768,1536]{0,1:T(8,128)}), f32[768,24]{0,1:T(8,128)}) %reduce-scatter.21.cloned.1.call-update) | async-done | bytes 73744 | tf_op jit(solution)/shard_map/reduce_scatter | solution.py:310
  1816.7 155.8 %reduce-scatter.19.cloned.1.call-done = f32[24,768]{1,0:T(8,128)} async-done(((f32[1536,768]{1,0:T(8,128)}), f32[24,768]{1,0:T(8,128)}) %reduce-scatter.19.cloned.1.call-update) | async-done | bytes 73744 | tf_op jit(solution)/shard_map/reduce_scatter | solution.py:307
  1972.4 218.0 %reduce-scatter.27.cloned.1.call-done = f32[8,24,384]{2,1,0:T(8,128)} async-done(((f32[8,1536,384]{2,1,0:T(8,128)}), f32[8,24,384]{2,1,0:T(8,128)}) %reduce-scatter.27.cloned.1.call-update) | async-done | bytes 294928 | tf_op jit(solution)/shard_map/reduce_scatter | solution.py:225
  2190.4 216.0 %reduce-scatter.25.cloned.1.call-done = f32[8,24,384]{2,1,0:T(8,128)} async-done(((f32[8,1536,384]{2,1,0:T(8,128)}), f32[8,24,384]{2,1,0:T(8,128)}) %reduce-scatter.25.cloned.1.call-update) | async-done | bytes 294928 | tf_op jit(solution)/shard_map/reduce_scatter | solution.py:224
  2406.4 217.0 %reduce-scatter.23.cloned.1.call-done = f32[8,24,384]{2,1,0:T(8,128)} async-done(((f32[8,1536,384]{2,1,0:T(8,128)}), f32[8,24,384]{2,1,0:T(8,128)}) %reduce-scatter.23.cloned.1.call-update) | async-done | bytes 294928 | tf_op jit(solution)/shard_map/reduce_scatter | solution.py:223
  (300 shorter events, 279.8 us)
Async XLA Ops:
  7.2 524.8 %all-gather.9.cloned.1.call-start = ((), (), s32[]{:S(2)}) async-start(), calls=%async_computation.9 | async-start | bytes 2396160 | tf_op jit(solution)/shard_map/all_gather | solution.py:93
  7.9 542.0 %all-gather.11.cloned.1.call-start = ((), (), s32[]{:S(2)}) async-start(), calls=%async_computation.10 | async-start | bytes 2396160 | tf_op jit(solution)/shard_map/all_gather | solution.py:146
  8.7 753.1 %all-reduce.14.cloned.1.call-start = ((), (), s32[]{:S(2)}) async-start(), calls=%async_computation.11 | async-start | bytes 6291456 | tf_op jit(solution)/shard_map/psum | solution.py:149
  10.5 347.5 %copy-start.66 = (bf16[24,128]{1,0:T(8,128)(2,1)S(1)}, bf16[24,128]{1,0:T(8,128)(2,1)}, u32[]{:S(2)}) copy-start(bf16[24,128]{1,0:T(8,128)(2,1)} %param.20) | copy-start | bytes 18436
  11.2 525.1 %copy-start.55 = (f32[512]{0:T(512)}, f32[512]{0:T(512)S(1)}, u32[]{:S(2)}) copy-start(f32[512]{0:T(512)S(1)} %get-tuple-element.119) | copy-start | bytes 6148
  185.1 351.2 %copy-start.42 = (f32[1536]{0:T(1024)}, f32[1536]{0:T(1024)S(1)}, u32[]{:S(2)}) copy-start(f32[1536]{0:T(1024)S(1)} %convert_element_type.171) | copy-start | bytes 18436
  185.1 339.5 %copy-start.5 = (bf16[1,512,1536]{2,1,0:T(8,128)(2,1)S(1)}, bf16[1,512,1536]{2,1,0:T(8,128)(2,1)}, u32[]{:S(2)}) copy-start(bf16[1,512,1536]{2,1,0:T(8,128)(2,1)} %param.14) | copy-start | bytes 4718596
  555.0 248.1 %all-gather.15.cloned.1.call-start = ((), (), s32[]{:S(2)}) async-start(), calls=%async_computation.13 | async-start | bytes 9584640 | tf_op jit(solution)/shard_map/all_gather | solution.py:167
  555.5 268.9 %all-gather.13.cloned.1.call-start = ((), (), s32[]{:S(2)}) async-start(), calls=%async_computation.12 | async-start | bytes 9584640 | tf_op jit(solution)/shard_map/all_gather | solution.py:166
  556.1 354.1 %all-gather.17.cloned.1.call-start = ((), (), s32[]{:S(2)}) async-start(), calls=%async_computation.14 | async-start | bytes 9584640 | tf_op jit(solution)/shard_map/all_gather | solution.py:168
  556.7 667.5 %all-reduce.18.cloned.1.call-start = ((), (), s32[]{:S(2)}) async-start(), calls=%async_computation.25 | async-start | bytes 12582912 | tf_op jit(solution)/shard_map/psum | solution.py:179
  557.3 208.0 %copy-start.49 = (f32[1536]{0:T(1024)}, f32[1536]{0:T(1024)S(1)}, u32[]{:S(2)}) copy-start(f32[1536]{0:T(1024)S(1)} %convert_element_type.186) | copy-start | bytes 18436
  1067.4 213.0 %reduce-scatter.15.cloned.1.call-start = ((), (), s32[]{:S(2)}) async-start(), calls=%async_computation.15 | async-start | bytes 393216 | tf_op jit(solution)/shard_map/reduce_scatter | solution.py:265
  1263.5 35.1 %reduce-scatter.17.cloned.1.call-start = ((), (), s32[]{:S(2)}) async-start(), calls=%async_computation.16 | async-start | bytes 393216 | tf_op jit(solution)/shard_map/reduce_scatter | solution.py:268
  1274.9 85.1 %all-reduce.16.cloned.1.call-start = ((), (), s32[]{:S(2)}) async-start(), calls=%async_computation.17 | async-start | bytes 3145728 | tf_op jit(solution)/shard_map/psum | solution.py:298
  1302.3 393.1 %reduce-scatter.31.cloned.1.call-start = ((), (), s32[]{:S(2)}) async-start(), calls=%async_computation.24 | async-start | bytes 798720
  1304.5 390.9 %reduce-scatter.29.cloned.1.call-start = ((), (), s32[]{:S(2)}) async-start(), calls=%async_computation.23 | async-start | bytes 798720
  1306.2 510.4 %reduce-scatter.21.cloned.1.call-start = ((), (), s32[]{:S(2)}) async-start(), calls=%async_computation.19 | async-start | bytes 4792320 | tf_op jit(solution)/shard_map/reduce_scatter | solution.py:310
  1311.8 660.7 %reduce-scatter.19.cloned.1.call-start = ((), (), s32[]{:S(2)}) async-start(), calls=%async_computation.18 | async-start | bytes 4792320 | tf_op jit(solution)/shard_map/reduce_scatter | solution.py:307
  1316.6 873.8 %reduce-scatter.27.cloned.1.call-start = ((), (), s32[]{:S(2)}) async-start(), calls=%async_computation.22 | async-start | bytes 19169280 | tf_op jit(solution)/shard_map/reduce_scatter | solution.py:225
  1331.3 1075.1 %reduce-scatter.25.cloned.1.call-start = ((), (), s32[]{:S(2)}) async-start(), calls=%async_computation.21 | async-start | bytes 19169280 | tf_op jit(solution)/shard_map/reduce_scatter | solution.py:224
  1344.8 1278.7 %reduce-scatter.23.cloned.1.call-start = ((), (), s32[]{:S(2)}) async-start(), calls=%async_computation.20 | async-start | bytes 19169280 | tf_op jit(solution)/shard_map/reduce_scatter | solution.py:223
  1357.8 333.1 %copy-start.65 = (f32[512]{0:T(512)S(1)}, f32[512]{0:T(512)}, u32[]{:S(2)}) copy-start(f32[512]{0:T(512)} %get-tuple-element.118) | copy-start | bytes 6148
  1359.9 331.0 %copy-start.14 = (bf16[512,1536]{1,0:T(8,128)(2,1)S(1)}, bf16[512,1536]{1,0:T(8,128)(2,1)}, u32[]{:S(2)}) copy-start(bf16[512,1536]{1,0:T(8,128)(2,1)} %all-reduce.16.cloned.1.call-done) | copy-start | bytes 4718596
  (65 other events, 1853.5 us)
Sparse Core Ops, SparseCore 0:
  11.1 72.6 all-gather.8
  86.9 66.0 all-gather.10
  555.1 92.6 all-reduce.13
  651.3 87.1 all-gather.14
  742.1 82.3 all-gather.12
  828.0 82.1 all-gather.16
  1067.5 156.5 all-reduce.17
  1263.6 16.8 reduce-scatter.14
  1283.5 15.0 reduce-scatter.16
  1302.5 57.4 all-reduce.15
  1366.3 145.5 reduce-scatter.30
  1518.1 142.9 reduce-scatter.28
  1667.8 148.7 reduce-scatter.20
  1823.3 149.0 reduce-scatter.18
  1979.9 210.4 reduce-scatter.26
  2196.9 209.5 reduce-scatter.24
  2413.9 209.4 reduce-scatter.22
where the time goes:
time: 2640 us; the launch traced here: 2630 us
  waiting for transfers between devices  1180 us (45%)
  blocking collectives  1010 us (38%)
  matrix products  193 us (7%)
  local copies, waits for them, and re-layouts  163 us (6%)
  other arithmetic  71.5 us (3%)
    unnamed x2, blocking collectives  497 us
    reduce_scatter x1, waiting for transfers between devices, body(): lax.psum_scatter(grad_down, ('fsdp', 'ctx'), scatter_dimension=1, tiled=T...  218 us
    reduce_scatter x1, waiting for transfers between devices, body(): lax.psum_scatter(grad_gate, ('fsdp', 'ctx'), scatter_dimension=1, tiled=T...  217 us
    reduce_scatter x1, waiting for transfers between devices, body(): lax.psum_scatter(grad_up, ('fsdp', 'ctx'), scatter_dimension=1, tiled=True)  216 us
    all_gather x1, blocking collectives, body(): lax.all_gather(value_matrix, ('fsdp', 'ctx'), axis=0, tiled=True)  167 us
    all_gather x1, blocking collectives, body(): lax.all_gather(w_router, ('fsdp', 'ctx'), axis=0, tiled=True)  164 us
    all_gather x1, blocking collectives, body(): lax.all_gather(key_matrix, ('fsdp', 'ctx'), axis=0, tiled=True)  163 us
    reduce_scatter x1, waiting for transfers between devices, body(): lax.psum_scatter(grad_query, ('fsdp', 'ctx'), scatter_dimension=0, tiled=...  156 us
  transfers between devices with their start and end apart: 17, of which 11 were waited for; matrix products, arithmetic and copies ran while one was open for 8% of the time, Pallas kernels for 0%

commit v1 on v0

v1 whole, which is shorter than its diff:
```python
import functools

import jax
import jax.numpy as jnp
from jax import lax
from jax.experimental import pallas as pl
from jax.experimental.pallas import tpu as pltpu
from jax.sharding import Mesh
from jax.sharding import PartitionSpec as P

QUERY_HEADS = 12
KEY_VALUE_HEADS = 2
HEAD_SIZE = 128
GROUP = QUERY_HEADS // KEY_VALUE_HEADS
EPS = 1e-06
ROPE_BASE = 1000000.0
NEG_FILL = -1e30
MISC = 128
SLOTS = 320
PAD = 32
MESH = pl.DeviceIdType.MESH
ANY = pl.BlockSpec(memory_space=pl.ANY)
VMEM = pl.BlockSpec(memory_space=pltpu.VMEM)
f32 = jnp.float32
bf16 = jnp.bfloat16


def rope_tables(positions):
    half_dim = HEAD_SIZE // 2
    frequency = ROPE_BASE ** (-jnp.arange(half_dim, dtype=f32) * (2.0 / HEAD_SIZE))
    angles = positions.astype(f32)[:, None] * frequency[None, :]
    angles = jnp.concatenate([angles, angles], axis=1)
    return (jnp.cos(angles)[:, None, :], jnp.sin(angles)[:, None, :])


def rotary_embed(value_rows, cosine_table, sine_table):
    half_dim = HEAD_SIZE // 2
    turned = jnp.concatenate([-value_rows[..., half_dim:], value_rows[..., :half_dim]], axis=-1)
    return value_rows * cosine_table + turned * sine_table


def rotate_back(grad_vals, cosine_table, sine_table):
    half_dim = HEAD_SIZE // 2
    scaled = grad_vals * sine_table
    turned = jnp.concatenate([scaled[..., half_dim:], -scaled[..., :half_dim]], axis=-1)
    return grad_vals * cosine_table + turned


def place():
    return lax.axis_index("c"), lax.axis_index("h"), lax.axis_index("l")


def column_peer(core_step, z_step):
    c, h, l = place()
    z = lax.rem(h * 2 + l + z_step, 4)
    return {"c": lax.rem(c + core_step, 2), "h": z // 2, "l": lax.rem(z, 2)}


def at_z(core, z):
    return {"c": core, "h": z // 2, "l": lax.rem(z, 2)}


def greet(steps):
    barrier = pltpu.get_barrier_semaphore()
    for core_step, z_step in steps:
        pl.semaphore_signal(
            barrier, inc=1, device_id=column_peer(core_step, (4 - z_step) % 4), device_id_type=MESH
        )
    pl.semaphore_wait(barrier, len(steps))


def send(src, dst, send_sem, recv_sem, peer):
    copy = pltpu.make_async_remote_copy(
        src_ref=src,
        dst_ref=dst,
        send_sem=send_sem,
        recv_sem=recv_sem,
        device_id=peer,
        device_id_type=MESH,
    )
    copy.start()
    return copy


COLUMN = [(0, 1), (0, 2), (0, 3), (1, 0), (1, 1), (1, 2), (1, 3)]
ALONG_Z = [(0, 1), (0, 2), (0, 3)]


def spread_kernel(attn_ref, expert_ref, attn_out, expert_out, s_sem, r_sem, as_sem, ar_sem, own):
    c, h, l = place()
    me = (c * 2 + h) * 2 + l
    greet(COLUMN)
    copies = []
    own_copy = pltpu.make_async_copy(expert_ref.at[me], expert_out.at[me], own.at[0])
    own_copy.start()
    slot = c * 2 + h
    for z_step in range(4):
        if z_step == 0:
            here = pltpu.make_async_copy(attn_ref, attn_out.at[slot], own.at[1])
            pl.when(c == l)(here.start)
            there = pltpu.make_async_remote_copy(
                src_ref=attn_ref,
                dst_ref=attn_out.at[slot],
                send_sem=as_sem.at[0],
                recv_sem=ar_sem.at[slot],
                device_id=column_peer(1, 0),
                device_id_type=MESH,
            )
            pl.when(c != l)(there.start)
        else:
            z = lax.rem(h * 2 + l + z_step, 4)
            send(attn_ref, attn_out.at[slot], as_sem.at[z_step], ar_sem.at[slot], at_z(l, z))
    for i, (core_step, z_step) in enumerate(COLUMN):
        peer = column_peer(core_step, z_step)
        to = (peer["c"] * 2 + peer["h"]) * 2 + peer["l"]
        copies.append(
            send(expert_ref.at[to], expert_out.at[me], s_sem.at[i], r_sem.at[i], peer)
        )
    for source in range(4):
        mine = (c == l) & (slot == source)

        def landed(source=source):
            pltpu.make_async_remote_copy(
                src_ref=attn_ref,
                dst_ref=attn_out.at[source],
                send_sem=as_sem.at[0],
                recv_sem=ar_sem.at[source],
                device_id=column_peer(1, 0),
                device_id_type=MESH,
            ).wait_recv()

        pl.when(jnp.logical_not(mine))(landed)
    pl.when(c == l)(here.wait)
    pl.when(c != l)(there.wait_send)
    for z_step in range(1, 4):
        pltpu.make_async_remote_copy(
            src_ref=attn_ref,
            dst_ref=attn_out.at[slot],
            send_sem=as_sem.at[z_step],
            recv_sem=ar_sem.at[slot],
            device_id=column_peer(0, z_step),
            device_id_type=MESH,
        ).wait_send()
    own_copy.wait()
    for copy in copies:
        copy.wait()


def spread(attn_block, expert_pieces):
    return pl.pallas_call(
        spread_kernel,
        name="spread_weights",
        out_shape=(
            jax.ShapeDtypeStruct((4,) + attn_block.shape, attn_block.dtype),
            jax.ShapeDtypeStruct(expert_pieces.shape, expert_pieces.dtype),
        ),
        in_specs=[ANY, ANY],
        out_specs=(ANY, ANY),
        scratch_shapes=[
            pltpu.SemaphoreType.DMA((7,)),
            pltpu.SemaphoreType.DMA((7,)),
            pltpu.SemaphoreType.DMA((4,)),
            pltpu.SemaphoreType.DMA((4,)),
            pltpu.SemaphoreType.DMA((2,)),
        ],
        compiler_params=pltpu.CompilerParams(collective_id=1, has_side_effects=True),
    )(attn_block, expert_pieces)


def along_z_kernel(block_ref, out_ref, s_sem, r_sem, own):
    c, h, l = place()
    z = h * 2 + l
    greet(ALONG_Z)
    own_copy = pltpu.make_async_copy(block_ref, out_ref.at[z], own)
    own_copy.start()
    copies = [
        send(block_ref, out_ref.at[z], s_sem.at[i], r_sem.at[i], column_peer(*step))
        for i, step in enumerate(ALONG_Z)
    ]
    own_copy.wait()
    for copy in copies:
        copy.wait()


def gather_along_z(block):
    return pl.pallas_call(
        along_z_kernel,
        name="gather_keys_values",
        out_shape=jax.ShapeDtypeStruct((4,) + block.shape, block.dtype),
        in_specs=[VMEM],
        out_specs=VMEM,
        scratch_shapes=[
            pltpu.SemaphoreType.DMA((3,)),
            pltpu.SemaphoreType.DMA((3,)),
            pltpu.SemaphoreType.DMA(()),
        ],
        compiler_params=pltpu.CompilerParams(collective_id=2, has_side_effects=True),
    )(block)


def sum_along_z_kernel(parts_ref, out_ref, held, s_sem, r_sem):
    c, h, l = place()
    z = h * 2 + l
    greet(ALONG_Z)
    copies = [
        send(
            parts_ref.at[lax.rem(z + step[1], 4)],
            held.at[i],
            s_sem.at[i],
            r_sem.at[i],
            column_peer(*step),
        )
        for i, step in enumerate(ALONG_Z)
    ]
    for copy in copies:
        copy.wait()
    total = parts_ref[z].astype(f32)
    for i in range(3):
        total = total + held[i].astype(f32)
    out_ref[...] = total


def sum_along_z(parts):
    shape = parts.shape[1:]
    return pl.pallas_call(
        sum_along_z_kernel,
        name="sum_key_value_gradients",
        out_shape=jax.ShapeDtypeStruct(shape, f32),
        in_specs=[VMEM],
        out_specs=VMEM,
        scratch_shapes=[
            pltpu.VMEM((3,) + shape, parts.dtype),
            pltpu.SemaphoreType.DMA((3,)),
            pltpu.SemaphoreType.DMA((3,)),
        ],
        compiler_params=pltpu.CompilerParams(collective_id=3, has_side_effects=True),
    )(parts)


def column_gather_kernel(
    rows_ref, gate_ref, rows_out, gates_out, s_sem, r_sem, fs_sem, fr_sem, gs_sem, gr_sem, own
):
    c, h, l = place()
    z = h * 2 + l
    me = c * 4 + z
    greet(COLUMN)
    own_copies = [
        pltpu.make_async_copy(rows_ref, rows_out.at[me], own.at[0]),
        pltpu.make_async_copy(gate_ref, gates_out.at[me], own.at[1]),
    ]
    for copy in own_copies:
        copy.start()
    order = [(0, 2), (0, 1), (0, 3)]
    copies = [
        send(gate_ref, gates_out.at[me], gs_sem.at[i], gr_sem.at[i], column_peer(*step))
        for i, step in enumerate(COLUMN)
    ]
    rounds = [
        send(rows_ref, rows_out.at[me], s_sem.at[i], r_sem.at[i], column_peer(*step))
        for i, step in enumerate(order)
    ]
    other = column_peer(1, 0)
    forwards = [send(rows_ref, rows_out.at[me], fs_sem.at[3], fr_sem.at[3], other)]
    for i in (1, 2, 0):
        rounds[i].wait_recv()
        origin = c * 4 + lax.rem(z + 4 - order[i][1], 4)
        block = rows_out.at[origin]
        forwards.append(send(block, block, fs_sem.at[i], fr_sem.at[i], other))
    for copy in rounds:
        copy.wait_send()
    for copy in own_copies:
        copy.wait()
    for copy in copies + forwards:
        copy.wait()


def column_gather(rows, gates):
    return pl.pallas_call(
        column_gather_kernel,
        name="gather_normed_rows",
        out_shape=(
            jax.ShapeDtypeStruct((8,) + rows.shape, rows.dtype),
            jax.ShapeDtypeStruct((8,) + gates.shape, gates.dtype),
        ),
        in_specs=[ANY, ANY],
        out_specs=(ANY, ANY),
        scratch_shapes=[
            pltpu.SemaphoreType.DMA((3,)),
            pltpu.SemaphoreType.DMA((3,)),
            pltpu.SemaphoreType.DMA((4,)),
            pltpu.SemaphoreType.DMA((4,)),
            pltpu.SemaphoreType.DMA((7,)),
            pltpu.SemaphoreType.DMA((7,)),
            pltpu.SemaphoreType.DMA((2,)),
        ],
        compiler_params=pltpu.CompilerParams(collective_id=4, has_side_effects=True),
    )(rows, gates)


def column_sum_kernel(
    parts_ref, small_ref, out_ref, small_out, near, chip, far, cs, cr, zs, zr, ss, sr, own
):
    c, h, l = place()
    z = h * 2 + l
    me = c * 4 + z
    greet(COLUMN)
    other = column_peer(1, 0)
    order = [2, 1, 3, 0]
    near_copies = [
        send(
            parts_ref.at[(1 - c) * 4 + lax.rem(z + step, 4)],
            near.at[i],
            cs.at[i],
            cr.at[i],
            other,
        )
        for i, step in enumerate(order)
    ]
    own_copy = pltpu.make_async_copy(small_ref.at[me], small_out.at[me], own)
    own_copy.start()
    small_copies = []
    for i, step in enumerate(COLUMN):
        peer = column_peer(*step)
        to = (peer["c"] * 2 + peer["h"]) * 2 + peer["l"]
        small_copies.append(send(small_ref.at[to], small_out.at[me], ss.at[i], sr.at[i], peer))
    rows = parts_ref.shape[1]
    chunk = 32
    far_copies = []
    for i, step in enumerate(order):
        near_copies[i].wait_recv()
        mine = c * 4 + lax.rem(z + step, 4)

        def add(k, carry, i=i, mine=mine, step=step):
            here = pl.ds(pl.multiple_of(k * chunk, chunk), chunk)
            total = parts_ref[mine, here, :].astype(f32) + near[i, here, :].astype(f32)
            if step == 0:
                out_ref[here, :] = total
            else:
                chip[i, here, :] = total.astype(chip.dtype)
            return carry

        lax.fori_loop(0, rows // chunk, add, 0)
        if step:
            far_copies.append(
                send(chip.at[i], far.at[i], zs.at[i], zr.at[i], column_peer(0, step))
            )
    for copy in far_copies:
        copy.wait()

    def finish(k, carry):
        here = pl.ds(pl.multiple_of(k * chunk, chunk), chunk)
        total = out_ref[here, :]
        for i in range(3):
            total = total + far[i, here, :].astype(f32)
        out_ref[here, :] = total
        return carry

    lax.fori_loop(0, rows // chunk, finish, 0)
    for copy in near_copies:
        copy.wait_send()
    own_copy.wait()
    for copy in small_copies:
        copy.wait()


def column_sum(parts, small, number):
    rows, width = parts.shape[1:]
    return pl.pallas_call(
        column_sum_kernel,
        name="sum_over_experts",
        out_shape=(
            jax.ShapeDtypeStruct((rows, width), f32),
            jax.ShapeDtypeStruct(small.shape, small.dtype),
        ),
        in_specs=[VMEM, VMEM],
        out_specs=(VMEM, VMEM),
        scratch_shapes=[
            pltpu.VMEM((4, rows, width), parts.dtype),
            pltpu.VMEM((3, rows, width), parts.dtype),
            pltpu.VMEM((3, rows, width), parts.dtype),
            pltpu.SemaphoreType.DMA((4,)),
            pltpu.SemaphoreType.DMA((4,)),
            pltpu.SemaphoreType.DMA((3,)),
            pltpu.SemaphoreType.DMA((3,)),
            pltpu.SemaphoreType.DMA((7,)),
            pltpu.SemaphoreType.DMA((7,)),
            pltpu.SemaphoreType.DMA(()),
        ],
        compiler_params=pltpu.CompilerParams(
            collective_id=number, has_side_effects=True, vmem_limit_bytes=40 * 2**20
        ),
    )(parts, small)


def expert_return_kernel(pieces_ref, out_ref, s_sem, r_sem, own):
    c, h, l = place()
    me = (c * 2 + h) * 2 + l
    greet(COLUMN)
    own_copy = pltpu.make_async_copy(pieces_ref.at[me], out_ref.at[me], own)
    own_copy.start()
    copies = []
    for i, step in enumerate(COLUMN):
        peer = column_peer(*step)
        to = (peer["c"] * 2 + peer["h"]) * 2 + peer["l"]
        copies.append(send(pieces_ref.at[to], out_ref.at[me], s_sem.at[i], r_sem.at[i], peer))
    own_copy.wait()
    for copy in copies:
        copy.wait()


def expert_return(pieces):
    return pl.pallas_call(
        expert_return_kernel,
        name="return_expert_gradients",
        out_shape=jax.ShapeDtypeStruct(pieces.shape, pieces.dtype),
        in_specs=[ANY],
        out_specs=ANY,
        scratch_shapes=[
            pltpu.SemaphoreType.DMA((7,)),
            pltpu.SemaphoreType.DMA((7,)),
            pltpu.SemaphoreType.DMA(()),
        ],
        compiler_params=pltpu.CompilerParams(collective_id=7, has_side_effects=True),
    )(pieces)


def attn_return_kernel(pieces_ref, misc_ref, out_ref, misc_out, ps, pr, ms, mr, own):
    c, h, l = place()
    z = h * 2 + l
    greet(COLUMN)
    for target in range(4):
        owner = {"c": target // 2, "h": target % 2, "l": c}
        is_me = (owner["c"] == c) & (owner["h"] == h) & (owner["l"] == l)
        there = pltpu.make_async_remote_copy(
            src_ref=pieces_ref.at[target],
            dst_ref=out_ref.at[z],
            send_sem=ps.at[target],
            recv_sem=pr.at[z],
            device_id=owner,
            device_id_type=MESH,
        )
        here = pltpu.make_async_copy(pieces_ref.at[target], out_ref.at[z], pr.at[z])
        pl.when(jnp.logical_not(is_me))(there.start)
        pl.when(is_me)(here.start)
    for target in range(8):
        owner = {"c": target // 4, "h": (target // 2) % 2, "l": target % 2}
        is_me = (owner["c"] == c) & (owner["h"] == h) & (owner["l"] == l)
        there = pltpu.make_async_remote_copy(
            src_ref=misc_ref.at[target // 2],
            dst_ref=misc_out.at[z],
            send_sem=ms.at[target],
            recv_sem=mr.at[z],
            device_id=owner,
            device_id_type=MESH,
        )
        here = pltpu.make_async_copy(misc_ref.at[target // 2], misc_out.at[z], mr.at[z])
        pl.when((c == 0) & jnp.logical_not(is_me))(there.start)
        pl.when((c == 0) & is_me)(here.start)
    for source in range(4):
        pltpu.make_async_copy(pieces_ref.at[0], out_ref.at[source], pr.at[source]).wait()
        pltpu.make_async_copy(misc_ref.at[0], misc_out.at[source], mr.at[source]).wait()
    for target in range(4):
        owner = {"c": target // 2, "h": target % 2, "l": c}
        is_me = (owner["c"] == c) & (owner["h"] == h) & (owner["l"] == l)
        sent = pltpu.make_async_copy(pieces_ref.at[0], out_ref.at[0], ps.at[target])
        pl.when(jnp.logical_not(is_me))(sent.wait)
    for target in range(8):
        owner = {"c": target // 4, "h": (target // 2) % 2, "l": target % 2}
        is_me = (owner["c"] == c) & (owner["h"] == h) & (owner["l"] == l)
        sent = pltpu.make_async_copy(misc_ref.at[0], misc_out.at[0], ms.at[target])
        pl.when((c == 0) & jnp.logical_not(is_me))(sent.wait)


def attn_return(pieces, misc):
    return pl.pallas_call(
        attn_return_kernel,
        name="return_attention_gradients",
        out_shape=(
            jax.ShapeDtypeStruct((4,) + pieces.shape[1:], pieces.dtype),
            jax.ShapeDtypeStruct((4,) + misc.shape[1:], misc.dtype),
        ),
        in_specs=[ANY, ANY],
        out_specs=(ANY, ANY),
        scratch_shapes=[
            pltpu.SemaphoreType.DMA((4,)),
            pltpu.SemaphoreType.DMA((4,)),
            pltpu.SemaphoreType.DMA((8,)),
            pltpu.SemaphoreType.DMA((4,)),
            pltpu.SemaphoreType.DMA(()),
        ],
        compiler_params=pltpu.CompilerParams(collective_id=8, has_side_effects=True),
    )(pieces, misc)


def dot(a, b):
    return jnp.dot(a, b, preferred_element_type=f32)


def dot_nt(a, b):
    return lax.dot_general(a, b, (((1,), (1,)), ((), ())), preferred_element_type=f32)


def dot_tn(a, b):
    return lax.dot_general(a, b, (((0,), (0,)), ((), ())), preferred_element_type=f32)


def exchange_halves(own, l):
    other = lax.ppermute(own, "l", [(0, 1), (1, 0)])
    first = jnp.where(l == 0, own, other)
    second = jnp.where(l == 0, other, own)
    return jnp.concatenate([first, second], axis=0)


def body(
    tokens,
    segments,
    routes,
    attn_gain,
    w_query,
    key_matrix,
    value_matrix,
    w_output,
    mix_gain,
    w_router,
    w_gate,
    w_up,
    w_down,
    block_cotangent,
):
    c, h, l = place()
    model_width = tokens.shape[2]
    rows = tokens.shape[1] // 2
    seq_length = segments.shape[1]
    experts, part, ff_half = w_gate.shape
    q_half = w_query.shape[1]
    score_scale = HEAD_SIZE ** (-0.5)

    misc = jnp.concatenate([attn_gain[:, None], mix_gain[:, None], w_router], axis=1)
    misc = jnp.pad(misc, ((0, 0), (0, MISC - misc.shape[1])))
    attn_block = jnp.concatenate(
        [w_query, key_matrix, value_matrix, misc, w_output.T], axis=1
    )
    attn_block = jnp.pad(attn_block, ((0, PAD - part), (0, 0)))
    expert_pieces = jnp.pad(
        jnp.stack([w_gate, w_up, w_down], axis=1), ((0, 0), (0, 0), (0, PAD - part), (0, 0))
    )
    attn_col, expert_col = spread(attn_block, expert_pieces)
    attn_col = attn_col[:, :part].reshape(4 * part, attn_block.shape[1])
    expert_col = (
        expert_col[:, :, :part]
        .reshape(4, 2, 3, part, ff_half)
        .transpose(2, 0, 3, 1, 4)
        .reshape(3, 4 * part, 2 * ff_half)
    )
    kv_width = key_matrix.shape[1]
    in_width = q_half + 2 * kv_width + MISC
    w_in = lax.all_gather(attn_col[:, :in_width], ("c", "x", "y"), axis=0, tiled=True).reshape(
        2, model_width, in_width
    )
    w_out = lax.all_gather(attn_col[:, in_width:], ("c", "x", "y"), axis=0, tiled=True).reshape(
        2, model_width, q_half
    )
    expert_full = lax.all_gather(expert_col, ("x", "y"), axis=1, tiled=True)
    gate_w, up_w, down_w = expert_full[0], expert_full[1], expert_full[2]
    qkv_w = w_in[:, :, : q_half + 2 * kv_width]
    misc_full = w_in[0, :, q_half + 2 * kv_width :]
    attn_scale = misc_full[:, 0].astype(f32)
    mix_scale = misc_full[:, 1].astype(f32)
    router_w = misc_full[:, 2 : 2 + experts]

    first = l * rows
    inputs = lax.dynamic_slice_in_dim(tokens[0], first, rows).astype(f32)
    upstream_low = lax.dynamic_slice_in_dim(block_cotangent[0], first, rows)
    upstream = upstream_low.astype(f32)
    route_rows = lax.dynamic_slice_in_dim(routes[0], first, rows)
    z = h * 2 + l
    positions = z * rows + jnp.arange(rows, dtype=jnp.int32)
    key_positions = jnp.arange(seq_length, dtype=jnp.int32)
    seg_all = segments[0]
    seg_local = lax.dynamic_slice_in_dim(seg_all, z * rows, rows)
    allowed = (seg_local[:, None] == seg_all[None, :]) & (
        positions[:, None] >= key_positions[None, :]
    )
    cosine_table, sine_table = rope_tables(positions)

    inv_attn = lax.rsqrt(jnp.mean(inputs * inputs, axis=1, keepdims=True) + EPS)
    scaled_in = inputs * inv_attn
    normalized_input = (scaled_in * attn_scale).astype(bf16)
    halves = [dot(normalized_input, qkv_w[i]) for i in range(2)]
    q_heads = [
        rotary_embed(p[:, :q_half].reshape(rows, GROUP, HEAD_SIZE), cosine_table, sine_table)
        .astype(bf16)
        .transpose(1, 0, 2)
        for p in halves
    ]
    k_own = [
        rotary_embed(
            p[:, None, q_half : q_half + kv_width], cosine_table, sine_table
        ).astype(bf16)[:, 0]
        for p in halves
    ]
    v_own = [p[:, q_half + kv_width :].astype(bf16) for p in halves]
    kv_all = gather_along_z(jnp.concatenate(k_own + v_own, axis=1)).reshape(
        seq_length, 4 * kv_width
    )
    keys = [kv_all[:, i * kv_width : (i + 1) * kv_width] for i in range(2)]
    values = [kv_all[:, (2 + i) * kv_width : (3 + i) * kv_width] for i in range(2)]

    def scores_of(i):
        scores = dot_nt(q_heads[i].reshape(GROUP * rows, HEAD_SIZE), keys[i]) * score_scale
        return jnp.where(
            allowed[None], scores.reshape(GROUP, rows, seq_length), NEG_FILL
        )

    attended, log_totals = [], []
    for i in range(2):
        masked = scores_of(i)
        row_peak = jnp.max(masked, axis=-1, keepdims=True)
        expo_vals = jnp.exp(masked - row_peak)
        row_total = jnp.sum(expo_vals, axis=-1, keepdims=True)
        weights_low = (expo_vals / row_total).astype(bf16)
        mixed = dot(weights_low.reshape(GROUP * rows, seq_length), values[i])
        attended.append(
            mixed.astype(bf16)
            .reshape(GROUP, rows, HEAD_SIZE)
            .transpose(1, 0, 2)
            .reshape(rows, q_half)
        )
        log_totals.append(row_peak + jnp.log(row_total))
    branch = dot_nt(attended[0], w_out[0]) + dot_nt(attended[1], w_out[1])
    residual = inputs + branch

    inv_mix = lax.rsqrt(jnp.mean(residual * residual, axis=1, keepdims=True) + EPS)
    scaled_mix = residual * inv_mix
    normed_mix = (scaled_mix * mix_scale).astype(bf16)
    logits = dot(normed_mix, router_w)
    hot_routes = (
        route_rows[:, :, None] == jnp.arange(experts, dtype=jnp.int32)[None, None, :]
    ).astype(f32)
    chosen = jnp.sum(hot_routes * logits[:, None, :], axis=-1)
    gate_expo = jnp.exp(chosen - jnp.max(chosen, axis=1, keepdims=True))
    gate_weights = gate_expo / jnp.sum(gate_expo, axis=1, keepdims=True)
    named = jnp.sum(hot_routes, axis=1)
    gate_rows = jnp.sum(gate_weights[:, :, None] * hot_routes, axis=1)
    gate_sent = jnp.where(named > 0, gate_rows, -1.0).T

    rows_all, gates_all = column_gather(normed_mix, gate_sent)
    grads_all = lax.all_gather(
        lax.all_gather(block_cotangent[0], "h", axis=0, tiled=True), "c", axis=0, tiled=True
    )
    expert = (c * 2 + h) * 2 + l
    block = 2 * rows
    rows_all = rows_all.reshape(4, block, model_width)
    grads_all = grads_all.reshape(4, block, model_width)
    gate_own = lax.dynamic_index_in_dim(gates_all, expert, axis=1, keepdims=False).reshape(
        4, block
    )
    taken = gate_own >= 0
    taken_low = taken.astype(jnp.int32)
    slot_of = jnp.cumsum(taken_low, axis=1) - taken_low
    hot_slots = (slot_of[:, None, :] == jnp.arange(SLOTS, dtype=jnp.int32)[None, :, None]) & taken[
        :, None, :
    ]
    pick = hot_slots.astype(bf16)
    slot_gate = jnp.sum(jnp.where(hot_slots, gate_own[:, None, :], 0.0), axis=2).reshape(
        4 * SLOTS, 1
    )

    def to_slots(values_all):
        return (
            jnp.einsum("kst,ktd->ksd", pick, values_all, preferred_element_type=f32)
            .astype(bf16)
            .reshape(4 * SLOTS, model_width)
        )

    def to_rows(slot_values):
        return (
            jnp.einsum(
                "kst,ksd->ktd",
                pick,
                slot_values.astype(bf16).reshape(4, SLOTS, model_width),
                preferred_element_type=f32,
            )
            .astype(bf16)
            .reshape(8, rows, model_width)
        )

    dispatched = to_slots(rows_all)
    slot_grad = to_slots(grads_all)
    gate_act = dot(dispatched, gate_w)
    up_act = dot(dispatched, up_w)
    sigmoid_act = jax.nn.sigmoid(gate_act)
    silu_act = gate_act * sigmoid_act
    hidden = silu_act * up_act
    hidden_gated = (hidden * slot_gate).astype(bf16)
    mix_parts = to_rows(dot_nt(hidden_gated, down_w))
    hidden_grad = dot(slot_grad, down_w)
    gate_back_slots = jnp.sum(hidden * hidden_grad, axis=1).reshape(4, SLOTS)
    gate_back_rows = jnp.sum(
        jnp.where(hot_slots, gate_back_slots[:, :, None], 0.0), axis=1
    ).reshape(8, 2, rows // 2)
    hidden_grad = hidden_grad * slot_gate
    gate_low = (hidden_grad * up_act * (sigmoid_act * (1.0 + gate_act * (1.0 - sigmoid_act)))).astype(
        bf16
    )
    up_low = (hidden_grad * silu_act).astype(bf16)
    grad_down = dot_tn(slot_grad, hidden_gated).astype(bf16)
    grad_gate = dot_tn(dispatched, gate_low).astype(bf16)
    grad_up = dot_tn(dispatched, up_low).astype(bf16)
    back_parts = to_rows(dot_nt(gate_low, gate_w) + dot_nt(up_low, up_w))

    mix_back, gate_back = column_sum(back_parts, gate_back_rows, 5)
    mix_out, unused = column_sum(mix_parts, gate_back_rows, 6)
    expert_sum = lax.psum_scatter(
        jnp.stack([grad_gate, grad_up, grad_down]), ("x", "y"), scatter_dimension=1, tiled=True
    )
    block_out = exchange_halves((residual + mix_out).astype(bf16), l)

    gate_back = jnp.sum(hot_routes * gate_back.reshape(experts, rows).T[:, None, :], axis=-1)
    gate_mean = jnp.sum(gate_weights * gate_back, axis=1, keepdims=True)
    chosen_grad = gate_weights * (gate_back - gate_mean)
    logit_grad = jnp.sum(chosen_grad[:, :, None] * hot_routes, axis=1).astype(bf16)
    grad_router = dot_tn(normed_mix, logit_grad)
    normed_grad = mix_back + dot_nt(logit_grad, router_w)
    grad_mix_gain = jnp.sum(normed_grad * scaled_mix, axis=0)
    scaled_grad = normed_grad * mix_scale
    resid_grad = (
        upstream
        + inv_mix * scaled_grad
        - residual * inv_mix**3 * jnp.mean(scaled_grad * residual, axis=1, keepdims=True)
    )

    branch_low = resid_grad.astype(bf16)
    grad_out = jnp.stack([dot_tn(branch_low, attended[i]) for i in range(2)]).astype(bf16)
    query_low, key_parts, value_parts = [], [], []
    for i in range(2):
        back_low = (
            dot(branch_low, w_out[i])
            .astype(bf16)
            .reshape(rows, GROUP, HEAD_SIZE)
            .transpose(1, 0, 2)
            .reshape(GROUP * rows, HEAD_SIZE)
        )
        prob_vals = jnp.exp(scores_of(i) - log_totals[i]).reshape(GROUP * rows, seq_length)
        prob_low = prob_vals.astype(bf16)
        prob_grad = dot_nt(back_low, values[i])
        row_dot = jnp.sum(prob_vals * prob_grad, axis=-1, keepdims=True)
        score_grad = (prob_vals * (prob_grad - row_dot)).astype(bf16)
        query_grad = dot(score_grad, keys[i]) * score_scale
        key_parts.append(
            dot_tn(score_grad, q_heads[i].reshape(GROUP * rows, HEAD_SIZE)) * score_scale
        )
        value_parts.append(dot_tn(prob_low, back_low))
        query_low.append(
            rotate_back(
                query_grad.reshape(GROUP, rows, HEAD_SIZE).transpose(1, 0, 2),
                cosine_table,
                sine_table,
            )
            .astype(bf16)
            .reshape(rows, q_half)
        )
    kv_back = sum_along_z(
        jnp.concatenate(key_parts + value_parts, axis=1)
        .astype(bf16)
        .reshape(4, rows, 4 * kv_width)
    )
    grad_in, normed_back = [], 0.0
    for i in range(2):
        key_low = rotate_back(
            kv_back[:, None, i * kv_width : (i + 1) * kv_width], cosine_table, sine_table
        ).astype(bf16)[:, 0]
        value_low = kv_back[:, (2 + i) * kv_width : (3 + i) * kv_width].astype(bf16)
        back_rows = jnp.concatenate([query_low[i], key_low, value_low], axis=1)
        grad_in.append(dot_tn(normalized_input, back_rows))
        normed_back = normed_back + dot_nt(back_rows, qkv_w[i])
    grad_attn_gain = jnp.sum(normed_back * scaled_in, axis=0)
    scaled_back = normed_back * attn_scale
    input_grad = (
        resid_grad
        + inv_attn * scaled_back
        - inputs * inv_attn**3 * jnp.mean(scaled_back * inputs, axis=1, keepdims=True)
    )
    input_grad = exchange_halves(input_grad.astype(bf16), l).astype(f32)

    misc_grad = jnp.concatenate(
        [grad_attn_gain[:, None], grad_mix_gain[:, None], grad_router], axis=1
    )
    misc_grad = jnp.pad(misc_grad, ((0, 0), (0, MISC - misc_grad.shape[1])))
    misc_grad = jnp.stack([misc_grad, jnp.zeros_like(misc_grad)]).astype(bf16)
    attn_grads = jnp.concatenate([jnp.stack(grad_in).astype(bf16), misc_grad], axis=2)

    def to_columns(grads):
        chip_sum = lax.psum_scatter(grads, "c", scatter_dimension=0, tiled=True)[0]
        return lax.psum_scatter(chip_sum, ("x", "y"), scatter_dimension=0, tiled=True)

    sums = jnp.concatenate([to_columns(attn_grads), to_columns(grad_out)], axis=1).astype(f32)
    sums = sums.reshape(4, part, sums.shape[1])
    returned, misc_back = attn_return(
        sums, sums[:, :, q_half + 2 * kv_width : in_width]
    )
    returned = jnp.sum(returned, axis=0)
    misc_back = jnp.sum(misc_back, axis=0)
    expert_back = expert_return(
        expert_sum.astype(f32)
        .reshape(3, 4, part, 2, ff_half)
        .transpose(1, 3, 0, 2, 4)
        .reshape(8, 3, part, ff_half)
    )
    return (
        block_out[None],
        input_grad[None],
        misc_back[:, 0],
        returned[:, :q_half],
        returned[:, q_half : q_half + kv_width],
        returned[:, q_half + kv_width : q_half + 2 * kv_width],
        returned[:, in_width:].T,
        misc_back[:, 1],
        misc_back[:, 2 : 2 + experts],
        expert_back[:, 0],
        expert_back[:, 1],
        expert_back[:, 2],
    )


def solution(mesh):
    split = Mesh(mesh.devices.reshape(4, 4, 2, 2, 2), ("x", "y", "c", "h", "l"))
    fsdp = ("x", "y", "c")
    owner = ("x", "y", "c", "h")
    return jax.shard_map(
        body,
        mesh=split,
        in_specs=(
            P(fsdp, "h", None),
            P(fsdp, None),
            P(fsdp, "h", None),
            P(owner),
            P(owner, "l"),
            P(owner, "l"),
            P(owner, "l"),
            P("l", owner),
            P(owner),
            P(owner, None),
            P(None, owner, "l"),
            P(None, owner, "l"),
            P(None, owner, "l"),
            P(fsdp, "h", None),
        ),
        out_specs=(
            P(fsdp, "h", None),
            P(fsdp, "h", None),
            P(owner),
            P(owner, "l"),
            P(owner, "l"),
            P(owner, "l"),
            P("l", owner),
            P(owner),
            P(owner, None),
            P(None, owner, "l"),
            P(None, owner, "l"),
            P(None, owner, "l"),
        ),
        check_vma=False,
    )
```

time: 2640 us -> 795 us (0.30)
  blocking collectives: 1010 us -> 0 us
  waiting for transfers between devices: 1180 us -> 287 us
  Pallas kernels: 0 us -> 225 us
  local copies, waits for them, and re-layouts: 163 us -> 60 us
  matrix products: 193 us -> 135 us
    reduce_scatter x7 -> x5, waiting for transfers between devices: 941 us -> 178 us  [the longest x2 135 us: to_columns(): lax.psum_scatter(chip_sum, ('x', 'y'), scatter_dimension=0, tiled=True)]
    all_gather x5 -> x0, blocking collectives: 506 us -> none  [the longest x1 167 us: body(): lax.all_gather(value_matrix, ('fsdp', 'ctx'), axis=0, tiled=True)]
    unnamed x2 -> x0, blocking collectives: 497 us -> none
    pallas_call x0 -> x8, Pallas kernels: none -> 225 us  [the longest x2 84.4 us: column_sum(): pl.pallas_call(column_sum_kernel, name='sum_over_experts', out_shape=(jax...]
    psum x3 -> x0, waiting for transfers between devices: 152 us -> none  [the longest x1 152 us: body(): mix_out, gate_back = lax.psum((mix_part, gate_part), 'tp')]
    gather x5 -> x0, local copies, waits for them, and re-layouts: 81.3 us -> none  [the longest x1 19.7 us: body(): gathered_out = result[slot_place].reshape(local_rows, top_k, model_width)]
    dot_general x30 -> x40, matrix products: 193 us -> 135 us  [the longest x12 46.5 us: dot_nt(): lax.dot_general(a, b, (((1,), (1,)), ((), ())), preferred_element_type=f32)]
    reduce_sum x6 -> x7, other arithmetic: 37.6 us -> 5.02 us  [the longest x2 1.8 us: body(): row_total = jnp.sum(expo_vals, axis=-1, keepdims=True)]
  transfers between devices with their start and end apart: 17 -> 12, of which waited for: 11 -> 8; matrix products, arithmetic and copies ran while one was open for 8% -> 22% of each run, Pallas kernels for 0% -> 16%
where the time goes in v1:
time: 795 us; the launch traced here: 786 us
  waiting for transfers between devices  287 us (36%)
  Pallas kernels  225 us (28%)
  matrix products  135 us (17%)
  other arithmetic  60.8 us (8%)
  local copies, waits for them, and re-layouts  60 us (8%)
  between operations  16.1 us (2%)
    reduce_scatter x2, waiting for transfers between devices, to_columns(): lax.psum_scatter(chip_sum, ('x', 'y'), scatter_dimension=0, tiled=True)  135 us
    pallas_call x2, Pallas kernels, column_sum(): pl.pallas_call(column_sum_kernel, name='sum_over_experts', out_shape=(jax...  84.4 us
    all_gather x1, waiting for transfers between devices, body(): lax.all_gather(attn_col[:, :in_width], ('c', 'x', 'y'), axis=0, tiled=True)  48 us
    dot_general x12, matrix products, dot_nt(): lax.dot_general(a, b, (((1,), (1,)), ((), ())), preferred_element_type=f32)  46.5 us
    pallas_call x1, Pallas kernels, column_gather(): pl.pallas_call(column_gather_kernel, name='gather_normed_rows', out_shape...  44.8 us
    dot_general x12, matrix products, dot(): return jnp.dot(a, b, preferred_element_type=f32)  43 us
    reduce_scatter x1, waiting for transfers between devices, body(): lax.psum_scatter(jnp.stack([grad_gate, grad_up, grad_down]), ('x', 'y'),...  42.7 us
    ppermute x2, waiting for transfers between devices, exchange_halves(): other = lax.ppermute(own, 'l', [(0, 1), (1, 0)])  29.2 us
  transfers between devices with their start and end apart: 12, of which 8 were waited for; matrix products, arithmetic and copies ran while one was open for 22% of the time, Pallas kernels for 16%

profile of v1, /device:TPU:1, one launch (start us, length us, event | category | flops | bytes accessed | tf_op | source)
XLA Modules:
  0.0 786.4 jit_solution(2278695680407679565)
XLA Ops:
  15.8 27.5 %spread_weights.1 = (bf16[4,32,1920]{2,1,0:T(8,128)(2,1)}, bf16[8,3,32,384]{3,2,1,0:T(8,128)(2,1)}) custom-call(bf16[32,1920]{1,0:T(8,128)(2,1)} %pad.20.attn_ref, bf16[8,3,32,384]{3,2,1,0:T(8,128)(2,1)} %fusion.86.expert_ref), custom_call_target="tpu_custom_call" | custom-call | tf_op jit(solution)/shard_map/spread_weights/pallas_call | solution.py:150
  45.9 23.2 %all-gather.14.cloned.1.call-done = bf16[1,1024,1536]{2,1,0:T(8,128)(2,1)} async-done(((bf16[1,512,1536]{2,1,0:T(8,128)(2,1)}), bf16[1,1024,1536]{2,1,0:T(8,128)(2,1)}) %all-gather.14.cloned.1.call-update) | async-done | bytes 3145744 | tf_op jit(solution)/shard_map/all_gather | solution.py:649
  75.0 48.0 %all-gather.8.cloned.1.call-done = bf16[3072,1152]{1,0:T(8,128)(2,1)} async-done(((bf16[96,1152]{1,0:T(8,128)(2,1)}), bf16[3072,1152]{1,0:T(8,128)(2,1)}) %all-gather.8.cloned.1.call-update) | async-done | bytes 7077904 | tf_op jit(solution)/shard_map/all_gather | solution.py:557
  144.6 18.1 %gather_keys_values.1 = bf16[4,256,512]{2,1,0:T(8,128)(2,1)} custom-call(bf16[256,512]{1,0:T(8,128)(2,1)} %pad_maximum_fusion.5.block_ref), custom_call_target="tpu_custom_call" | custom-call | tf_op jit(solution)/shard_map/gather_keys_values/pallas_call | solution.py:186
  192.2 44.8 %gather_normed_rows.1 = (bf16[8,256,1536]{2,1,0:T(8,128)(2,1)}, f32[8,8,256]{2,1,0:T(8,128)}) custom-call(bf16[256,1536]{1,0:T(8,128)(2,1)} %copy-done.6, f32[8,256]{1,0:T(8,128)} %select_bitcast_fusion.2.gate_ref), custom_call_target="tpu_custom_call" | custom-call | tf_op jit(solution)/shard_map/gather_normed_rows/pallas_call | solution.py:278
  241.9 7.1 convolution_convert_fusion.3
  253.1 6.7 all-gather.12.cloned.1.call-done
  259.8 6.5 fusion.30
  269.9 9.9 %multiply_reduce_fusion.2 = (f32[1280]{0:T(1024)S(1)}, f32[1280,768]{0,1:T(8,128)}) fusion(f32[1280,768]{0,1:T(8,128)S(1)} %fusion.30, f32[1280,768]{0,1:T(8,128)S(1)} %fusion.29, bf16[1280,1536]{1,0:T(8,128)(2,1)} %bitcast.340, bf16[3,1536,768]{2,1,0:T(8,128)(2,1)S(1)} %copy-done.66), kind=kOutput, calls=%fused_computation.30 | convolution fusion | flops 3026778880 | bytes 18093056 | tf_op jit(solution)/shard_map/dot_general | solution.py:496
  281.2 5.7 multiply_convert_fusion.2
  287.0 7.1 convolution_convert_fusion
  303.5 6.2 fusion.1
  313.4 43.1 %sum_over_experts.2 = (f32[256,1536]{1,0:T(8,128)S(1)}, f32[8,2,128]{2,1,0:T(2,128)}) custom-call(bf16[8,256,1536]{2,1,0:T(8,128)(2,1)S(1)} %bitcast.260, f32[8,2,128]{2,1,0:T(2,128)S(1)} %reshape.623.small_ref), custom_call_target="tpu_custom_call" | custom-call | tf_op jit(solution)/shard_map/sum_over_experts/pallas_call | solution.py:368
  356.5 41.4 %sum_over_experts.3 = (f32[256,1536]{1,0:T(8,128)S(1)}, f32[8,2,128]{2,1,0:T(2,128)S(1)}) custom-call(bf16[8,256,1536]{2,1,0:T(8,128)(2,1)S(1)} %bitcast.261, f32[8,2,128]{2,1,0:T(2,128)S(1)} %reshape.623.small_ref), custom_call_target="tpu_custom_call" | custom-call | tf_op jit(solution)/shard_map/sum_over_experts/pallas_call | solution.py:368
  455.0 16.7 %sum_key_value_gradients.1 = f32[256,512]{1,0:T(8,128)} custom-call(bf16[4,256,512]{2,1,0:T(8,128)(2,1)} %pad_maximum_fusion.2.parts_ref), custom_call_target="tpu_custom_call" | custom-call | tf_op jit(solution)/shard_map/sum_key_value_gradients/pallas_call | solution.py:225
  495.9 6.2 fusion.16
  513.5 5.8 copy.228
  523.9 13.8 %collective-permute-done = bf16[256,1536]{1,0:T(8,128)(2,1)S(1)} collective-permute-done((bf16[256,1536]{1,0:T(8,128)(2,1)}, bf16[256,1536]{1,0:T(8,128)(2,1)S(1)}, u32[]{:S(2)}, u32[]{:S(2)}) %collective-permute-start) | collective-permute-done | bytes 786464 | tf_op jit(solution)/shard_map/ppermute | solution.py:508
  539.1 15.4 %collective-permute-done.1 = bf16[256,1536]{1,0:T(8,128)(2,1)S(1)} collective-permute-done((bf16[256,1536]{1,0:T(8,128)(2,1)S(1)}, bf16[256,1536]{1,0:T(8,128)(2,1)S(1)}, u32[]{:S(2)}, u32[]{:S(2)}) %collective-permute-start.1) | collective-permute-done | bytes 786464 | tf_op jit(solution)/shard_map/ppermute | solution.py:508
  556.7 42.7 %reduce-scatter.14.cloned.1.call-done = bf16[3,96,768]{2,1,0:T(8,128)(2,1)} async-done(((bf16[3,1536,768]{2,1,0:T(8,128)(2,1)}), bf16[3,96,768]{2,1,0:T(8,128)(2,1)}) %reduce-scatter.14.cloned.1.call-update) | async-done | bytes 442384 | tf_op jit(solution)/shard_map/reduce_scatter | solution.py:714
  601.9 16.5 %return_expert_gradients.1 = f32[8,3,24,384]{3,2,1,0:T(8,128)} custom-call(f32[8,3,24,384]{3,2,1,0:T(8,128)} %bitcast.285), custom_call_target="tpu_custom_call" | custom-call | tf_op jit(solution)/shard_map/return_expert_gradients/pallas_call | solution.py:412
  620.5 56.3 %reduce-scatter.12.cloned.1.call-done = bf16[96,768]{1,0:T(8,128)(2,1)} async-done(((bf16[1536,768]{1,0:T(8,128)(2,1)}), bf16[96,768]{1,0:T(8,128)(2,1)}) %reduce-scatter.12.cloned.1.call-update) | async-done | bytes 147472 | tf_op jit(solution)/shard_map/reduce_scatter | solution.py:795
  676.7 79.1 %reduce-scatter.16.cloned.1.call-done = bf16[96,1152]{1,0:T(8,128)(2,1)} async-done(((bf16[1536,1152]{1,0:T(8,128)(2,1)}), bf16[96,1152]{1,0:T(8,128)(2,1)}) %reduce-scatter.16.cloned.1.call-update) | async-done | bytes 221200 | tf_op jit(solution)/shard_map/reduce_scatter | solution.py:795
  757.8 16.5 %return_attention_gradients.1 = (f32[4,24,1920]{2,1,0:T(8,128)}, f32[4,24,128]{2,1,0:T(8,128)}) custom-call(f32[4,24,1920]{2,1,0:T(8,128)} %copy-done.20, f32[4,24,128]{2,1,0:T(8,128)} %slice.287.misc_ref), custom_call_target="tpu_custom_call" | custom-call | tf_op jit(solution)/shard_map/return_attention_gradients/pallas_call | solution.py:475
  (347 shorter events, 206.0 us)
Async XLA Ops:
  7.2 66.5 %copy-start = (s32[1,512,4]{1,2,0:T(4,128)S(1)}, s32[1,512,4]{1,2,0:T(4,128)}, u32[]{:S(2)}) copy-start(s32[1,512,4]{1,2,0:T(4,128)} %param.16) | copy-start | bytes 24580
  7.2 62.0 %all-gather.14.cloned.1.call-start = ((), (), s32[]{:S(2)}) async-start(), calls=%async_computation.12 | async-start | bytes 4718592 | tf_op jit(solution)/shard_map/all_gather | solution.py:649
  7.9 115.1 %all-gather.8.cloned.1.call-start = ((), (), s32[]{:S(2)}) async-start(), calls=%async_computation.5 | async-start | bytes 7299072 | tf_op jit(solution)/shard_map/all_gather | solution.py:557
  43.3 25.9 %copy-start.41 = (bf16[8,3,32,384]{3,2,1,0:T(8,128)(2,1)S(1)}, bf16[8,3,32,384]{3,2,1,0:T(8,128)(2,1)}, u32[]{:S(2)}) copy-start(bf16[8,3,32,384]{3,2,1,0:T(8,128)(2,1)} %get-tuple-element.24) | copy-start | bytes 1769476
  45.1 137.5 %all-gather.10.cloned.1.call-start = ((), (), s32[]{:S(2)}) async-start(), calls=%async_computation.6 | async-start | bytes 4866048 | tf_op jit(solution)/shard_map/all_gather | solution.py:560
  45.9 196.0 %all-gather.16.cloned.1.call-start = ((), (), s32[]{:S(2)}) async-start(), calls=%async_computation.13 | async-start | bytes 9437184 | tf_op jit(solution)/shard_map/all_gather | solution.py:648
  69.2 190.6 %all-gather.12.cloned.1.call-start = ((), (), s32[]{:S(2)}) async-start(), calls=%async_computation.7 | async-start | bytes 7520256 | tf_op jit(solution)/shard_map/all_gather | solution.py:563
  70.8 442.0 %reduce-scatter.10.cloned.1.call-start = ((), (), s32[]{:S(2)}) async-start(), calls=%async_computation.9 | async-start | bytes 7077888 | tf_op jit(solution)/shard_map/reduce_scatter | solution.py:794
  74.3 54.3 %copy-start.63 = (f32[256]{0:T(256)}, f32[256]{0:T(256)S(1)}, u32[]{:S(2)}) copy-start(f32[256]{0:T(256)S(1)} %get-tuple-element.132) | copy-start | bytes 3076
  124.5 64.8 %copy-start.43 = (f32[1536]{0:T(1024)}, f32[1536]{0:T(1024)S(1)}, u32[]{:S(2)}) copy-start(f32[1536]{0:T(1024)S(1)} %get-tuple-element.70) | copy-start | bytes 18436
  281.2 16.7 %slice-start.6 = ((s8[7077888]{0:T(1024)(128)(4,1)}), s8[4194304]{0:T(1024)(128)(4,1)S(1)}, s32[]{:S(2)}) async-start(s8[7077888]{0:T(1024)(128)(4,1)} %bitcast.332), calls=%async_computation.21 | async-start | bytes 8388608
  356.5 41.5 %copy-start.55 = (f32[256]{0:T(256)S(1)}, f32[256]{0:T(256)}, u32[]{:S(2)}) copy-start(f32[256]{0:T(256)} %copy-done.54) | copy-start | bytes 3076
  356.5 41.5 %copy-start.60 = (f32[256]{0:T(256)S(1)}, f32[256]{0:T(256)}, u32[]{:S(2)}) copy-start(f32[256]{0:T(256)} %copy-done.59) | copy-start | bytes 3076
  356.5 41.5 %copy-start.44 = (f32[1536]{0:T(1024)S(1)}, f32[1536]{0:T(1024)}, u32[]{:S(2)}) copy-start(f32[1536]{0:T(1024)} %copy-done.43) | copy-start | bytes 18436
  356.5 41.5 %copy-start.58 = (f32[256]{0:T(256)S(1)}, f32[256]{0:T(256)}, u32[]{:S(2)}) copy-start(f32[256]{0:T(256)} %copy-done.57) | copy-start | bytes 3076
  410.9 102.6 %reduce-scatter.8.cloned.1.call-start = ((), (), s32[]{:S(2)}) async-start(), calls=%async_computation.8 | async-start | bytes 10616832 | tf_op jit(solution)/shard_map/reduce_scatter | solution.py:794
  452.8 18.8 %copy-start.5 = (bf16[1536,1024]{0,1:T(8,128)(2,1)S(1)}, bf16[1536,1024]{0,1:T(8,128)(2,1)}, u32[]{:S(2)}) copy-start(bf16[1536,1024]{0,1:T(8,128)(2,1)} %get-tuple-element.85) | copy-start | bytes 9437188
  495.6 103.8 %reduce-scatter.14.cloned.1.call-start = ((), (), s32[]{:S(2)}) async-start(), calls=%async_computation.11 | async-start | bytes 7520256 | tf_op jit(solution)/shard_map/reduce_scatter | solution.py:714
  512.7 164.0 %reduce-scatter.12.cloned.1.call-start = ((), (), s32[]{:S(2)}) async-start(), calls=%async_computation.10 | async-start | bytes 2506752 | tf_op jit(solution)/shard_map/reduce_scatter | solution.py:795
  513.5 242.4 %reduce-scatter.16.cloned.1.call-start = ((), (), s32[]{:S(2)}) async-start(), calls=%async_computation.14 | async-start | bytes 3760128 | tf_op jit(solution)/shard_map/reduce_scatter | solution.py:795
  519.4 18.4 %copy-start.21 = (bf16[256,1536]{1,0:T(8,128)(2,1)S(1)}, bf16[256,1536]{1,0:T(8,128)(2,1)}, u32[]{:S(2)}) copy-start(bf16[256,1536]{1,0:T(8,128)(2,1)} %get-tuple-element.91) | copy-start | bytes 2359300
  519.4 18.4 %collective-permute-start = (bf16[256,1536]{1,0:T(8,128)(2,1)}, bf16[256,1536]{1,0:T(8,128)(2,1)S(1)}, u32[]{:S(2)}, u32[]{:S(2)}) collective-permute-start(bf16[256,1536]{1,0:T(8,128)(2,1)} %get-tuple-element.91), channel_id=1, source_target_pairs={{0,1},{1,0},{2,3},{3,2},{4,5},{5,4},{6,7},{7,6},{8,9},{9,8},{10,11... | collective-permute-start | bytes 2359304 | tf_op jit(solution)/shard_map/ppermute | solution.py:508
  522.6 31.9 %collective-permute-start.1 = (bf16[256,1536]{1,0:T(8,128)(2,1)S(1)}, bf16[256,1536]{1,0:T(8,128)(2,1)S(1)}, u32[]{:S(2)}, u32[]{:S(2)}) collective-permute-start(bf16[256,1536]{1,0:T(8,128)(2,1)S(1)} %fusion.50), channel_id=1, source_target_pairs={{0,1},{1,0},{2,3},{3,2},{4,5},{5,4},{6,7},{7,6},{8,9},{9,8},{10,11... | collective-permute-start | bytes 2359304 | tf_op jit(solution)/shard_map/ppermute | solution.py:508
  601.9 177.2 %copy-start.1 = (s32[1,512,4]{1,2,0:T(4,128)S(1)}, s32[1,512,4]{1,2,0:T(4,128)}, u32[]{:S(2)}) copy-start(s32[1,512,4]{1,2,0:T(4,128)} %param.16) | copy-start | bytes 24580
  (66 other events, 265.8 us)
Sparse Core Ops, SparseCore 0:
  9.7 59.4 all-gather.13
  72.0 50.9 all-gather.7
  125.9 45.7 all-gather.9
  173.2 18.8 all-gather.15
  194.2 65.5 all-gather.11
  411.0 14.2 reduce-scatter.9
  495.7 17.4 reduce-scatter.7
  516.7 82.6 reduce-scatter.13
  603.1 73.6 reduce-scatter.11
  680.3 75.5 reduce-scatter.15

commit v2 on v1

--- a/solution.py
+++ b/solution.py
@@ -86,43 +86,212 @@
 ALONG_Z = [(0, 1), (0, 2), (0, 3)]
 
 
-def spread_kernel(attn_ref, expert_ref, attn_out, expert_out, s_sem, r_sem, as_sem, ar_sem, own):
+class Lanes:
+    def __init__(self, send_sem, recv_sem):
+        self.send_sem, self.recv_sem, self.used = send_sem, recv_sem, 0
+
+    def send(self, src, dst, peer):
+        i = self.used
+        self.used += 1
+        return send(src, dst, self.send_sem.at[i], self.recv_sem.at[i], peer)
+
+
+def lanes_scratch(count):
+    return [pltpu.SemaphoreType.DMA((count,)), pltpu.SemaphoreType.DMA((count,))]
+
+
+def chip_peer(axis, step):
+    return {axis: lax.rem(lax.axis_index(axis) + step + 4, 4)}
+
+
+def greet_chips(barrier):
+    for axis in ("x", "y"):
+        for step in (1, 3):
+            pl.semaphore_signal(
+                barrier, inc=1, device_id=chip_peer(axis, step), device_id_type=MESH
+            )
+    return 4
+
+
+def greet_column(barrier):
+    for step in COLUMN:
+        pl.semaphore_signal(barrier, inc=1, device_id=column_peer(*step), device_id_type=MESH)
+    return len(COLUMN)
+
+
+class ColumnRing:
+    def __init__(self, lanes, rows_ref, out_ref):
+        c, h, l = place()
+        self.lanes, self.rows, self.out = lanes, rows_ref, out_ref
+        self.c, self.z = c, h * 2 + l
+        self.half = rows_ref.shape[0] // 2
+        self.copies = []
+
+    def at(self, step):
+        return self.c * 4 + lax.rem(self.z + step + 4, 4)
+
+    def forward(self, step):
+        block = self.out.at[self.at(step)]
+        self.copies.append(self.lanes.send(block, block, column_peer(1, 0)))
+
+    def start(self):
+        here = self.out.at[self.at(0)]
+        self.up = self.lanes.send(self.rows, here, column_peer(0, 1))
+        self.down = self.lanes.send(self.rows, here, column_peer(0, 3))
+        self.copies.append(self.lanes.send(self.rows, here, column_peer(1, 0)))
+
+    def relay(self):
+        lower, upper = pl.ds(0, self.half), pl.ds(self.half, self.half)
+        self.up.wait_recv()
+        block = self.out.at[self.at(-1), lower]
+        self.up_far = self.lanes.send(block, block, column_peer(0, 1))
+        self.down.wait_recv()
+        block = self.out.at[self.at(1), upper]
+        self.down_far = self.lanes.send(block, block, column_peer(0, 3))
+        self.forward(-1)
+        self.forward(1)
+
+    def finish(self):
+        self.up_far.wait_recv()
+        self.down_far.wait_recv()
+        self.forward(2)
+        for copy in (self.up, self.down, self.up_far, self.down_far):
+            copy.wait_send()
+        for copy in self.copies:
+            copy.wait()
+
+
+class ChipRing:
+    def __init__(self, lanes, w_out, block, low, rows, a, b):
+        self.lanes, self.w_out, self.block = lanes, w_out, block
+        self.rows, self.a, self.b = pl.ds(low, rows), a, b
+        self.c = lax.axis_index("c")
+        self.split = 1024
+        self.sent, self.near = [], []
+
+    def ref(self, da, db, columns=None):
+        steps = {self.a: da, self.b: db}
+        x = lax.rem(lax.axis_index("x") + steps["x"] + 4, 4)
+        y = lax.rem(lax.axis_index("y") + steps["y"] + 4, 4)
+        if columns is None:
+            return self.w_out.at[self.c, x * 4 + y, self.rows]
+        return self.w_out.at[self.c, x * 4 + y, self.rows, columns]
+
+    def copy(self, src, dst, axis, step):
+        made = self.lanes.send(src, dst, chip_peer(axis, step))
+        self.sent.append(made)
+        return made
+
+    def share(self, da, db):
+        block = self.ref(da, db)
+        self.near.append(self.lanes.send(block, block, column_peer(1, 0)))
+
+    def start(self):
+        own = self.block.at[self.rows]
+        here = self.ref(0, 0)
+        self.first = [self.copy(own, here, self.a, step) for step in (1, -1)]
+        self.turn = {0: [self.copy(own, here, self.b, step) for step in (1, -1)]}
+        self.near.append(self.lanes.send(own, here, column_peer(1, 0)))
+
+    def pass_on(self, da):
+        block = self.ref(da, 0)
+        self.turn[da] = [self.copy(block, block, self.b, step) for step in (1, -1)]
+        self.share(da, 0)
+
+    def relay_first(self):
+        width = self.w_out.shape[3]
+        low, high = pl.ds(0, self.split), pl.ds(self.split, width - self.split)
+        for copy in self.first:
+            copy.wait_recv()
+        block = self.ref(-1, 0, low)
+        one = self.copy(block, block, self.a, 1)
+        block = self.ref(1, 0, high)
+        self.second = [one, self.copy(block, block, self.a, -1)]
+        self.pass_on(-1)
+        self.pass_on(1)
+
+    def relay_turn(self, da):
+        for copy in self.turn[da]:
+            copy.wait_recv()
+        step = 1 if da in (0, -1) else -1
+        block = self.ref(da, -step)
+        self.last[da] = self.copy(block, block, self.b, step)
+        self.share(da, 1)
+        self.share(da, -1)
+
+    def relay_second(self):
+        for copy in self.second:
+            copy.wait_recv()
+        self.pass_on(2)
+
+    def finish(self):
+        for da in (0, -1, 1, 2):
+            self.last[da].wait_recv()
+            self.share(da, 2)
+
+    def drain(self):
+        for copy in self.sent:
+            copy.wait_send()
+        for copy in self.near:
+            copy.wait()
+
+
+def weights_kernel(
+    part,
+    attn_ref,
+    expert_ref,
+    rows_ref,
+    w_out,
+    expert_out,
+    rows_out,
+    attn_in,
+    expert_in,
+    block,
+    s_sem,
+    r_sem,
+    as_sem,
+    ar_sem,
+    own,
+):
     c, h, l = place()
     me = (c * 2 + h) * 2 + l
-    greet(COLUMN)
-    copies = []
-    own_copy = pltpu.make_async_copy(expert_ref.at[me], expert_out.at[me], own.at[0])
+    barrier = pltpu.get_barrier_semaphore()
+    pl.semaphore_wait(barrier, greet_column(barrier) + greet_chips(barrier))
+    lanes = Lanes(s_sem, r_sem)
+    slot = c * 2 + h
+    here = pltpu.make_async_copy(attn_ref, attn_in.at[slot], own.at[1])
+    there = pltpu.make_async_remote_copy(
+        src_ref=attn_ref,
+        dst_ref=attn_in.at[slot],
+        send_sem=as_sem.at[0],
+        recv_sem=ar_sem.at[slot],
+        device_id=column_peer(1, 0),
+        device_id_type=MESH,
+    )
+    pl.when(c == l)(here.start)
+    pl.when(c != l)(there.start)
+    for z_step in range(1, 4):
+        z = lax.rem(h * 2 + l + z_step, 4)
+        send(attn_ref, attn_in.at[slot], as_sem.at[z_step], ar_sem.at[slot], at_z(l, z))
+    own_copy = pltpu.make_async_copy(expert_ref.at[me], expert_in.at[me], own.at[0])
     own_copy.start()
-    slot = c * 2 + h
-    for z_step in range(4):
-        if z_step == 0:
-            here = pltpu.make_async_copy(attn_ref, attn_out.at[slot], own.at[1])
-            pl.when(c == l)(here.start)
-            there = pltpu.make_async_remote_copy(
-                src_ref=attn_ref,
-                dst_ref=attn_out.at[slot],
-                send_sem=as_sem.at[0],
-                recv_sem=ar_sem.at[slot],
-                device_id=column_peer(1, 0),
-                device_id_type=MESH,
-            )
-            pl.when(c != l)(there.start)
-        else:
-            z = lax.rem(h * 2 + l + z_step, 4)
-            send(attn_ref, attn_out.at[slot], as_sem.at[z_step], ar_sem.at[slot], at_z(l, z))
-    for i, (core_step, z_step) in enumerate(COLUMN):
-        peer = column_peer(core_step, z_step)
+    pieces = []
+    for step in COLUMN:
+        peer = column_peer(*step)
         to = (peer["c"] * 2 + peer["h"]) * 2 + peer["l"]
-        copies.append(
-            send(expert_ref.at[to], expert_out.at[me], s_sem.at[i], r_sem.at[i], peer)
-        )
+        pieces.append(lanes.send(expert_ref.at[to], expert_in.at[me], peer))
+    own_rows = pltpu.make_async_copy(rows_ref, rows_out.at[me], own.at[2])
+    own_rows.start()
+    ring = ColumnRing(lanes, rows_ref, rows_out)
+    ring.start()
+
     for source in range(4):
         mine = (c == l) & (slot == source)
 
         def landed(source=source):
             pltpu.make_async_remote_copy(
                 src_ref=attn_ref,
-                dst_ref=attn_out.at[source],
+                dst_ref=attn_in.at[source],
                 send_sem=as_sem.at[0],
                 recv_sem=ar_sem.at[source],
                 device_id=column_peer(1, 0),
@@ -131,40 +300,87 @@
 
         pl.when(jnp.logical_not(mine))(landed)
     pl.when(c == l)(here.wait)
+    block[...] = jnp.concatenate(
+        [attn_in[i].astype(f32)[:part] for i in range(4)], axis=0
+    ).astype(block.dtype)
+    x, y = lax.axis_index("x"), lax.axis_index("y")
+    keep = pltpu.make_async_copy(block, w_out.at[c, x * 4 + y], own.at[3])
+    keep.start()
+    half = block.shape[0] // 2
+    halves = [
+        ChipRing(lanes, w_out, block, 0, half, "x", "y"),
+        ChipRing(lanes, w_out, block, half, half, "y", "x"),
+    ]
+    for ring_half in halves:
+        ring_half.last = {}
+        ring_half.start()
+
+    own_copy.wait()
+    for copy in pieces:
+        copy.wait()
+    for i in range(3):
+        for l_side in range(2):
+            expert_out[i, :, l_side * 384 : (l_side + 1) * 384] = jnp.concatenate(
+                [expert_in[2 * j + l_side, i].astype(f32)[:part] for j in range(4)], axis=0
+            ).astype(expert_out.dtype)
+
+    for ring_half in halves:
+        ring_half.relay_first()
+    for ring_half in halves:
+        ring_half.relay_turn(0)
+    for ring_half in halves:
+        ring_half.relay_second()
+    ring.relay()
+    for da in (-1, 1, 2):
+        for ring_half in halves:
+            ring_half.relay_turn(da)
+    ring.finish()
+    for ring_half in halves:
+        ring_half.finish()
+    for ring_half in halves:
+        ring_half.drain()
+    keep.wait()
+    own_rows.wait()
     pl.when(c != l)(there.wait_send)
     for z_step in range(1, 4):
         pltpu.make_async_remote_copy(
             src_ref=attn_ref,
-            dst_ref=attn_out.at[slot],
+            dst_ref=attn_in.at[slot],
             send_sem=as_sem.at[z_step],
             recv_sem=ar_sem.at[slot],
             device_id=column_peer(0, z_step),
             device_id_type=MESH,
         ).wait_send()
-    own_copy.wait()
-    for copy in copies:
-        copy.wait()
-
-
-def spread(attn_block, expert_pieces):
+
+
+def gather_weights(attn_block, expert_pieces, rows, part):
+    width = attn_block.shape[1]
+    ff_half = expert_pieces.shape[3]
     return pl.pallas_call(
-        spread_kernel,
-        name="spread_weights",
+        functools.partial(weights_kernel, part),
+        name="gather_weights",
         out_shape=(
-            jax.ShapeDtypeStruct((4,) + attn_block.shape, attn_block.dtype),
-            jax.ShapeDtypeStruct(expert_pieces.shape, expert_pieces.dtype),
+            jax.ShapeDtypeStruct((2, 16, 4 * part, width), bf16),
+            jax.ShapeDtypeStruct((3, 4 * part, 2 * ff_half), bf16),
+            jax.ShapeDtypeStruct((8,) + rows.shape, bf16),
         ),
-        in_specs=[ANY, ANY],
-        out_specs=(ANY, ANY),
+        in_specs=[VMEM, ANY, ANY],
+        out_specs=(ANY, VMEM, ANY),
         scratch_shapes=[
-            pltpu.SemaphoreType.DMA((7,)),
-            pltpu.SemaphoreType.DMA((7,)),
+            pltpu.VMEM((4,) + attn_block.shape, bf16),
+            pltpu.VMEM(expert_pieces.shape, bf16),
+            pltpu.VMEM((4 * part, width), bf16),
+        ]
+        + lanes_scratch(90)
+        + [
             pltpu.SemaphoreType.DMA((4,)),
             pltpu.SemaphoreType.DMA((4,)),
-            pltpu.SemaphoreType.DMA((2,)),
+            pltpu.SemaphoreType.DMA((4,)),
         ],
-        compiler_params=pltpu.CompilerParams(collective_id=1, has_side_effects=True),
-    )(attn_block, expert_pieces)
+        compiler_params=pltpu.CompilerParams(
+            collective_id=1, has_side_effects=True, vmem_limit_bytes=32 * 2**20
+        ),
+    )(attn_block, expert_pieces, rows)
 
 
 def along_z_kernel(block_ref, out_ref, s_sem, r_sem, own):
@@ -237,40 +453,24 @@
     )(parts)
 
 
-def column_gather_kernel(
-    rows_ref, gate_ref, rows_out, gates_out, s_sem, r_sem, fs_sem, fr_sem, gs_sem, gr_sem, own
-):
+def column_gather_kernel(rows_ref, gate_ref, rows_out, gates_out, s_sem, r_sem, own):
     c, h, l = place()
-    z = h * 2 + l
-    me = c * 4 + z
-    greet(COLUMN)
+    me = c * 4 + h * 2 + l
+    barrier = pltpu.get_barrier_semaphore()
+    pl.semaphore_wait(barrier, greet_column(barrier))
+    lanes = Lanes(s_sem, r_sem)
+    ring = ColumnRing(lanes, rows_ref, rows_out)
+    ring.start()
     own_copies = [
         pltpu.make_async_copy(rows_ref, rows_out.at[me], own.at[0]),
         pltpu.make_async_copy(gate_ref, gates_out.at[me], own.at[1]),
     ]
     for copy in own_copies:
         copy.start()
-    order = [(0, 2), (0, 1), (0, 3)]
-    copies = [
-        send(gate_ref, gates_out.at[me], gs_sem.at[i], gr_sem.at[i], column_peer(*step))
-        for i, step in enumerate(COLUMN)
-    ]
-    rounds = [
-        send(rows_ref, rows_out.at[me], s_sem.at[i], r_sem.at[i], column_peer(*step))
-        for i, step in enumerate(order)
-    ]
-    other = column_peer(1, 0)
-    forwards = [send(rows_ref, rows_out.at[me], fs_sem.at[3], fr_sem.at[3], other)]
-    for i in (1, 2, 0):
-        rounds[i].wait_recv()
-        origin = c * 4 + lax.rem(z + 4 - order[i][1], 4)
-        block = rows_out.at[origin]
-        forwards.append(send(block, block, fs_sem.at[i], fr_sem.at[i], other))
-    for copy in rounds:
-        copy.wait_send()
-    for copy in own_copies:
-        copy.wait()
-    for copy in copies + forwards:
+    copies = [lanes.send(gate_ref, gates_out.at[me], column_peer(*step)) for step in COLUMN]
+    ring.relay()
+    ring.finish()
+    for copy in own_copies + copies:
         copy.wait()
 
 
@@ -284,15 +484,7 @@
         ),
         in_specs=[ANY, ANY],
         out_specs=(ANY, ANY),
-        scratch_shapes=[
-            pltpu.SemaphoreType.DMA((3,)),
-            pltpu.SemaphoreType.DMA((3,)),
-            pltpu.SemaphoreType.DMA((4,)),
-            pltpu.SemaphoreType.DMA((4,)),
-            pltpu.SemaphoreType.DMA((7,)),
-            pltpu.SemaphoreType.DMA((7,)),
-            pltpu.SemaphoreType.DMA((2,)),
-        ],
+        scratch_shapes=lanes_scratch(16) + [pltpu.SemaphoreType.DMA((2,))],
         compiler_params=pltpu.CompilerParams(collective_id=4, has_side_effects=True),
     )(rows, gates)
 
@@ -392,104 +584,318 @@
     )(parts, small)
 
 
-def expert_return_kernel(pieces_ref, out_ref, s_sem, r_sem, own):
+class ChipSum:
+    def __init__(self, lanes, chip, low, rows, p, q, near_p, rest_p, near_q):
+        self.lanes, self.chip = lanes, chip
+        self.rows, self.p, self.q = pl.ds(low, rows), p, q
+        self.near_p, self.rest_p, self.near_q = near_p, rest_p, near_q
+        self.sent = []
+
+    def index(self, dp, dq):
+        steps = {self.p: dp, self.q: dq}
+        x = lax.rem(lax.axis_index("x") + steps["x"] + 4, 4)
+        y = lax.rem(lax.axis_index("y") + steps["y"] + 4, 4)
+        return x * 4 + y
+
+    def copy(self, src, dst, axis, step):
+        made = self.lanes.send(src, dst, chip_peer(axis, step))
+        self.sent.append(made)
+        return made
+
+    def own(self, dp, dq):
+        return self.chip.at[self.index(dp, dq), self.rows]
+
+    def far(self):
+        self.far_copies = {}
+        for dq, step, i in ((2, 1, 0), (3, -1, 0), (1, 1, 1), (0, -1, 1)):
+            direction = 0 if step == 1 else 1
+            self.far_copies[direction, i] = self.copy(
+                self.own(2, dq), self.near_p.at[direction, i], self.p, step
+            )
+
+    def plain(self):
+        self.next_copies = {}
+        for dq, step in ((2, -1), (3, 1), (1, -1), (0, 1)):
+            self.next_to(dq, step)
+
+    def next_to(self, dq, step):
+        direction = 0 if step == 1 else 1
+        self.next_copies[direction, dq] = self.copy(
+            self.own(step, dq), self.rest_p.at[direction, dq], self.p, step
+        )
+
+    def joined(self):
+        for dq, step, i in ((2, 1, 0), (3, -1, 0), (1, 1, 1), (0, -1, 1)):
+            direction = 0 if step == 1 else 1
+            self.far_copies[direction, i].wait_recv()
+            mine = self.own(step, dq)
+            mine[...] = mine[...] + self.near_p[direction, i]
+            self.next_to(dq, step)
+
+    def collect(self, dq):
+        for direction in range(2):
+            self.next_copies[direction, dq].wait_recv()
+        mine = self.own(0, dq)
+        total = mine[...].astype(f32)
+        for direction in range(2):
+            total = total + self.rest_p[direction, dq].astype(f32)
+        mine[...] = total.astype(mine.dtype)
+
+    def far_q(self):
+        width = self.chip.shape[2]
+        self.low, self.high = pl.ds(0, 1024), pl.ds(1024, width - 1024)
+        self.collect(2)
+        block = self.index(0, 2)
+        self.far_q_copies = [
+            self.copy(
+                self.chip.at[block, self.rows, self.low], self.near_q.at[0, :, self.low], self.q, 1
+            ),
+            self.copy(
+                self.chip.at[block, self.rows, self.high], self.near_q.at[1, :, self.high], self.q, -1
+            ),
+        ]
+
+    def next_q(self):
+        self.next_q_copies = []
+        for i, (dq, columns) in enumerate(((1, self.low), (3, self.high))):
+            self.collect(dq)
+            self.far_q_copies[i].wait_recv()
+            block = self.index(0, dq)
+            self.chip[block, self.rows, columns] = (
+                self.chip[block, self.rows, columns] + self.near_q[i, :, columns]
+            )
+            self.next_q_copies.append(
+                self.copy(
+                    self.chip.at[block, self.rows],
+                    self.near_q.at[2 + i],
+                    self.q,
+                    1 if i == 0 else -1,
+                )
+            )
+
+    def total(self):
+        self.collect(0)
+        total = self.chip[self.index(0, 0), self.rows, :].astype(f32)
+        for i in range(2):
+            self.next_q_copies[i].wait_recv()
+            total = total + self.near_q[2 + i].astype(f32)
+        return total
+
+    def drain(self):
+        for copy in self.sent:
+            copy.wait_send()
+
+
+def return_kernel(
+    part,
+    misc_at,
+    in_ref,
+    out_ref,
+    expert_ref,
+    grads_out,
+    misc_out,
+    expert_out,
+    near,
+    near_p0,
+    rest_p0,
+    near_q0,
+    near_p1,
+    rest_p1,
+    near_q1,
+    pieces,
+    landed,
+    misc_landed,
+    s_sem,
+    r_sem,
+    ps,
+    pr,
+    ms,
+    mr,
+    own,
+):
     c, h, l = place()
-    me = (c * 2 + h) * 2 + l
-    greet(COLUMN)
-    own_copy = pltpu.make_async_copy(pieces_ref.at[me], out_ref.at[me], own)
+    z = h * 2 + l
+    me = c * 4 + z
+    barrier = pltpu.get_barrier_semaphore()
+    pl.semaphore_wait(barrier, greet_column(barrier) + greet_chips(barrier))
+    lanes = Lanes(s_sem, r_sem)
+    in_width = in_ref.shape[3]
+    width = near.shape[2]
+    half = near.shape[1] // 2
+    other = column_peer(1, 0)
+    x, y = lax.axis_index("x"), lax.axis_index("y")
+    sums = [
+        ChipSum(lanes, near, 0, half, "y", "x", near_p0, rest_p0, near_q0),
+        ChipSum(lanes, near, half, half, "x", "y", near_p1, rest_p1, near_q1),
+    ]
+    order = [2, 1, 3, 0]
+    arrive = {}
+    for step in order:
+        for which in range(2):
+            for dq in range(4):
+                block = sums[which].index(step, dq)
+                rows = pl.ds(which * half, half)
+                arrive[step, which, dq] = [
+                    lanes.send(
+                        in_ref.at[1 - c, block, rows],
+                        near.at[block, rows, pl.ds(0, in_width)],
+                        other,
+                    ),
+                    lanes.send(
+                        out_ref.at[1 - c, block, rows],
+                        near.at[block, rows, pl.ds(in_width, width - in_width)],
+                        other,
+                    ),
+                ]
+    own_copy = pltpu.make_async_copy(expert_ref.at[me], expert_out.at[me], own.at[0])
     own_copy.start()
-    copies = []
-    for i, step in enumerate(COLUMN):
+    expert_copies = []
+    for step in COLUMN:
         peer = column_peer(*step)
         to = (peer["c"] * 2 + peer["h"]) * 2 + peer["l"]
-        copies.append(send(pieces_ref.at[to], out_ref.at[me], s_sem.at[i], r_sem.at[i], peer))
-    own_copy.wait()
-    for copy in copies:
-        copy.wait()
-
-
-def expert_return(pieces):
-    return pl.pallas_call(
-        expert_return_kernel,
-        name="return_expert_gradients",
-        out_shape=jax.ShapeDtypeStruct(pieces.shape, pieces.dtype),
-        in_specs=[ANY],
-        out_specs=ANY,
-        scratch_shapes=[
-            pltpu.SemaphoreType.DMA((7,)),
-            pltpu.SemaphoreType.DMA((7,)),
-            pltpu.SemaphoreType.DMA(()),
-        ],
-        compiler_params=pltpu.CompilerParams(collective_id=7, has_side_effects=True),
-    )(pieces)
-
-
-def attn_return_kernel(pieces_ref, misc_ref, out_ref, misc_out, ps, pr, ms, mr, own):
-    c, h, l = place()
-    z = h * 2 + l
-    greet(COLUMN)
+        expert_copies.append(lanes.send(expert_ref.at[to], expert_out.at[me], peer))
+
+    def add_own(step, which):
+        for dq in range(4):
+            for copy in arrive[step, which, dq]:
+                copy.wait_recv()
+            block = sums[which].index(step, dq)
+            rows = pl.ds(which * half, half)
+            near[block, rows, pl.ds(0, in_width)] = (
+                near[block, rows, pl.ds(0, in_width)] + in_ref[c, block, rows, :]
+            )
+            near[block, rows, pl.ds(in_width, width - in_width)] = (
+                near[block, rows, pl.ds(in_width, width - in_width)] + out_ref[c, block, rows, :]
+            )
+
+    for which in range(2):
+        add_own(2, which)
+        sums[which].far()
+    for step in (1, 3):
+        for which in range(2):
+            add_own(step, which)
+    for each in sums:
+        each.plain()
+    for each in sums:
+        each.joined()
+    for which in range(2):
+        add_own(0, which)
+    for each in sums:
+        each.far_q()
+    for each in sums:
+        each.next_q()
+    for which in range(2):
+        total = sums[which].total()
+        for i in range(2):
+            pieces[2 * which + i] = total[i * part : (i + 1) * part]
+
+    def to_owner(target, owner, src, dst, send_sem, recv_sem, asked):
+        is_me = (owner["c"] == c) & (owner["h"] == h) & (owner["l"] == l)
+        there = pltpu.make_async_remote_copy(
+            src_ref=src,
+            dst_ref=dst,
+            send_sem=send_sem,
+            recv_sem=recv_sem,
+            device_id=owner,
+            device_id_type=MESH,
+        )
+        here = pltpu.make_async_copy(src, dst, recv_sem)
+        pl.when(asked & jnp.logical_not(is_me))(there.start)
+        pl.when(asked & is_me)(here.start)
+        return asked & jnp.logical_not(is_me), there
+
+    sent = []
+    everyone = c < 2
     for target in range(4):
         owner = {"c": target // 2, "h": target % 2, "l": c}
-        is_me = (owner["c"] == c) & (owner["h"] == h) & (owner["l"] == l)
-        there = pltpu.make_async_remote_copy(
-            src_ref=pieces_ref.at[target],
-            dst_ref=out_ref.at[z],
-            send_sem=ps.at[target],
-            recv_sem=pr.at[z],
-            device_id=owner,
-            device_id_type=MESH,
-        )
-        here = pltpu.make_async_copy(pieces_ref.at[target], out_ref.at[z], pr.at[z])
-        pl.when(jnp.logical_not(is_me))(there.start)
-        pl.when(is_me)(here.start)
-    for target in range(8):
-        owner = {"c": target // 4, "h": (target // 2) % 2, "l": target % 2}
-        is_me = (owner["c"] == c) & (owner["h"] == h) & (owner["l"] == l)
-        there = pltpu.make_async_remote_copy(
-            src_ref=misc_ref.at[target // 2],
-            dst_ref=misc_out.at[z],
-            send_sem=ms.at[target],
-            recv_sem=mr.at[z],
-            device_id=owner,
-            device_id_type=MESH,
-        )
-        here = pltpu.make_async_copy(misc_ref.at[target // 2], misc_out.at[z], mr.at[z])
-        pl.when((c == 0) & jnp.logical_not(is_me))(there.start)
-        pl.when((c == 0) & is_me)(here.start)
+        sent.append(
+            to_owner(
+                target, owner, pieces.at[target], landed.at[z], ps.at[target], pr.at[z], everyone
+            )
+        )
+    misc = pl.ds(misc_at, MISC)
+    for target in range(4):
+        owner = {"c": target // 2, "h": target % 2, "l": 1}
+        sent.append(
+            to_owner(
+                target,
+                owner,
+                pieces.at[target, :, misc],
+                misc_landed.at[z],
+                ms.at[target],
+                mr.at[z],
+                c == 0,
+            )
+        )
     for source in range(4):
-        pltpu.make_async_copy(pieces_ref.at[0], out_ref.at[source], pr.at[source]).wait()
-        pltpu.make_async_copy(misc_ref.at[0], misc_out.at[source], mr.at[source]).wait()
-    for target in range(4):
-        owner = {"c": target // 2, "h": target % 2, "l": c}
-        is_me = (owner["c"] == c) & (owner["h"] == h) & (owner["l"] == l)
-        sent = pltpu.make_async_copy(pieces_ref.at[0], out_ref.at[0], ps.at[target])
-        pl.when(jnp.logical_not(is_me))(sent.wait)
-    for target in range(8):
-        owner = {"c": target // 4, "h": (target // 2) % 2, "l": target % 2}
-        is_me = (owner["c"] == c) & (owner["h"] == h) & (owner["l"] == l)
-        sent = pltpu.make_async_copy(misc_ref.at[0], misc_out.at[0], ms.at[target])
-        pl.when((c == 0) & jnp.logical_not(is_me))(sent.wait)
-
-
-def attn_return(pieces, misc):
+        pltpu.make_async_copy(pieces.at[0], landed.at[source], pr.at[source]).wait()
+    grads_out[...] = (landed[0] + landed[1]) + (landed[2] + landed[3])
+
+    def from_core():
+        for source in range(4):
+            pltpu.make_async_copy(
+                pieces.at[0, :, misc], misc_landed.at[source], mr.at[source]
+            ).wait()
+        misc_out[...] = (misc_landed[0] + misc_landed[1]) + (misc_landed[2] + misc_landed[3])
+
+    def from_piece():
+        misc_out[...] = (landed[0, :, misc] + landed[1, :, misc]) + (
+            landed[2, :, misc] + landed[3, :, misc]
+        )
+
+    pl.when(l == 1)(from_core)
+    pl.when(l == 0)(from_piece)
+    for asked, there in sent:
+        pl.when(asked)(there.wait_send)
+    for copies in arrive.values():
+        for copy in copies:
+            copy.wait_send()
+    for each in sums:
+        each.drain()
+    own_copy.wait()
+    for copy in expert_copies:
+        copy.wait()
+
+
+def return_gradients(grad_in, grad_out, expert_pieces, part, misc_at):
+    in_width, out_width = grad_in.shape[3], grad_out.shape[3]
+    width, rows = in_width + out_width, grad_in.shape[2]
+    half = rows // 2
+    ring = [
+        pltpu.VMEM((2, 2, half, width), bf16),
+        pltpu.VMEM((2, 4, half, width), bf16),
+        pltpu.VMEM((4, half, width), bf16),
+    ]
     return pl.pallas_call(
-        attn_return_kernel,
-        name="return_attention_gradients",
+        functools.partial(return_kernel, part, misc_at),
+        name="return_gradients",
         out_shape=(
-            jax.ShapeDtypeStruct((4,) + pieces.shape[1:], pieces.dtype),
-            jax.ShapeDtypeStruct((4,) + misc.shape[1:], misc.dtype),
+            jax.ShapeDtypeStruct((part, width), f32),
+            jax.ShapeDtypeStruct((part, MISC), f32),
+            jax.ShapeDtypeStruct(expert_pieces.shape, expert_pieces.dtype),
         ),
-        in_specs=[ANY, ANY],
-        out_specs=(ANY, ANY),
-        scratch_shapes=[
+        in_specs=[VMEM, VMEM, ANY],
+        out_specs=(VMEM, VMEM, ANY),
+        scratch_shapes=[pltpu.VMEM((16, rows, width), bf16)]
+        + ring
+        + ring
+        + [
+            pltpu.VMEM((4, part, width), f32),
+            pltpu.VMEM((4, part, width), f32),
+            pltpu.VMEM((4, part, MISC), f32),
+        ]
+        + lanes_scratch(130)
+        + [
             pltpu.SemaphoreType.DMA((4,)),
             pltpu.SemaphoreType.DMA((4,)),
-            pltpu.SemaphoreType.DMA((8,)),
             pltpu.SemaphoreType.DMA((4,)),
-            pltpu.SemaphoreType.DMA(()),
+            pltpu.SemaphoreType.DMA((4,)),
+            pltpu.SemaphoreType.DMA((1,)),
         ],
-        compiler_params=pltpu.CompilerParams(collective_id=8, has_side_effects=True),
-    )(pieces, misc)
+        compiler_params=pltpu.CompilerParams(
+            collective_id=7, has_side_effects=True, vmem_limit_bytes=48 * 2**20
+        ),
+    )(grad_in, grad_out, expert_pieces)
 
 
 def dot(a, b):
@@ -544,33 +950,22 @@
     expert_pieces = jnp.pad(
         jnp.stack([w_gate, w_up, w_down], axis=1), ((0, 0), (0, 0), (0, PAD - part), (0, 0))
     )
-    attn_col, expert_col = spread(attn_block, expert_pieces)
-    attn_col = attn_col[:, :part].reshape(4 * part, attn_block.shape[1])
-    expert_col = (
-        expert_col[:, :, :part]
-        .reshape(4, 2, 3, part, ff_half)
-        .transpose(2, 0, 3, 1, 4)
-        .reshape(3, 4 * part, 2 * ff_half)
-    )
+    upstream_low = lax.dynamic_slice_in_dim(block_cotangent[0], l * rows, rows)
+    w_attn, expert_col, grads_all = gather_weights(attn_block, expert_pieces, upstream_low, part)
     kv_width = key_matrix.shape[1]
     in_width = q_half + 2 * kv_width + MISC
-    w_in = lax.all_gather(attn_col[:, :in_width], ("c", "x", "y"), axis=0, tiled=True).reshape(
-        2, model_width, in_width
-    )
-    w_out = lax.all_gather(attn_col[:, in_width:], ("c", "x", "y"), axis=0, tiled=True).reshape(
-        2, model_width, q_half
-    )
+    w_attn = w_attn.reshape(2, model_width, attn_block.shape[1])
+    w_out = w_attn[:, :, in_width:]
     expert_full = lax.all_gather(expert_col, ("x", "y"), axis=1, tiled=True)
     gate_w, up_w, down_w = expert_full[0], expert_full[1], expert_full[2]
-    qkv_w = w_in[:, :, : q_half + 2 * kv_width]
-    misc_full = w_in[0, :, q_half + 2 * kv_width :]
+    qkv_w = w_attn[:, :, : q_half + 2 * kv_width]
+    misc_full = w_attn[0, :, q_half + 2 * kv_width : in_width]
     attn_scale = misc_full[:, 0].astype(f32)
     mix_scale = misc_full[:, 1].astype(f32)
     router_w = misc_full[:, 2 : 2 + experts]
 
     first = l * rows
     inputs = lax.dynamic_slice_in_dim(tokens[0], first, rows).astype(f32)
-    upstream_low = lax.dynamic_slice_in_dim(block_cotangent[0], first, rows)
     upstream = upstream_low.astype(f32)
     route_rows = lax.dynamic_slice_in_dim(routes[0], first, rows)
     z = h * 2 + l
@@ -645,9 +1040,6 @@
     gate_sent = jnp.where(named > 0, gate_rows, -1.0).T
 
     rows_all, gates_all = column_gather(normed_mix, gate_sent)
-    grads_all = lax.all_gather(
-        lax.all_gather(block_cotangent[0], "h", axis=0, tiled=True), "c", axis=0, tiled=True
-    )
     expert = (c * 2 + h) * 2 + l
     block = 2 * rows
     rows_all = rows_all.reshape(4, block, model_width)
@@ -790,23 +1182,19 @@
     misc_grad = jnp.stack([misc_grad, jnp.zeros_like(misc_grad)]).astype(bf16)
     attn_grads = jnp.concatenate([jnp.stack(grad_in).astype(bf16), misc_grad], axis=2)
 
-    def to_columns(grads):
-        chip_sum = lax.psum_scatter(grads, "c", scatter_dimension=0, tiled=True)[0]
-        return lax.psum_scatter(chip_sum, ("x", "y"), scatter_dimension=0, tiled=True)
-
-    sums = jnp.concatenate([to_columns(attn_grads), to_columns(grad_out)], axis=1).astype(f32)
-    sums = sums.reshape(4, part, sums.shape[1])
-    returned, misc_back = attn_return(
-        sums, sums[:, :, q_half + 2 * kv_width : in_width]
-    )
-    returned = jnp.sum(returned, axis=0)
-    misc_back = jnp.sum(misc_back, axis=0)
-    expert_back = expert_return(
-        expert_sum.astype(f32)
-        .reshape(3, 4, part, 2, ff_half)
+    pieces = (
+        jnp.pad(expert_sum.reshape(3, 4, part, 2, ff_half), ((0, 0), (0, 0), (0, PAD - part), (0, 0), (0, 0)))
         .transpose(1, 3, 0, 2, 4)
-        .reshape(8, 3, part, ff_half)
-    )
+        .reshape(8, 3, PAD, ff_half)
+    )
+    returned, misc_back, expert_back = return_gradients(
+        attn_grads.reshape(2, 16, 4 * part, in_width),
+        grad_out.reshape(2, 16, 4 * part, q_half),
+        pieces,
+        part,
+        in_width - MISC,
+    )
+    expert_back = expert_back[:, :, :part].astype(f32)
     return (
         block_out[None],
         input_grad[None],

time: 795 us -> 536 us (0.67)
  waiting for transfers between devices: 287 us -> 0.04 us
  Pallas kernels: 225 us -> 267 us
  other arithmetic: 60.8 us -> 52.2 us
    reduce_scatter x4 -> x0, waiting for transfers between devices: 135 us -> none  [the longest x2 135 us: to_columns(): lax.psum_scatter(chip_sum, ('x', 'y'), scatter_dimension=0, tiled=True)]
    all_gather x4 -> x0, waiting for transfers between devices: 71.3 us -> none  [the longest x1 48 us: body(): lax.all_gather(attn_col[:, :in_width], ('c', 'x', 'y'), axis=0, tiled=True)]
    pallas_call x3 -> x2, Pallas kernels: 60.5 us -> 115 us  [the longest x1 59.7 us: return_gradients(): pl.pallas_call(functools.partial(return_kernel, part, misc_at), name='ret...]
    reduce_scatter x1, waiting for transfers between devices: 42.7 us -> 0.01 us  [body(): lax.psum_scatter(jnp.stack([grad_gate, grad_up, grad_down]), ('x', 'y'),...]
    ppermute x2, waiting for transfers between devices: 29.2 us -> 0.01 us  [exchange_halves(): other = lax.ppermute(own, 'l', [(0, 1), (1, 0)])]
    concatenate x0 -> x1, local copies, waits for them, and re-layouts: none -> 10.5 us  [body(): jnp.concatenate([jnp.stack(grad_in).astype(bf16), misc_grad], axis=2)]
    pallas_call x1, Pallas kernels: 44.8 us -> 35.1 us  [column_gather(): pl.pallas_call(column_gather_kernel, name='gather_normed_rows', out_shape...]
    unnamed x163 -> x161, local copies, waits for them, and re-layouts: 19.2 us -> 21.6 us
  transfers between devices with their start and end apart: 12 -> 4, of which waited for: 8 -> 0; matrix products, arithmetic and copies ran while one was open for 22% -> 25% of each run, Pallas kernels for 16% -> 13%
where the time goes in v2:
time: 536 us; the launch traced here: 528 us
  Pallas kernels  267 us (50%)
  matrix products  131 us (24%)
  local copies, waits for them, and re-layouts  61.3 us (11%)
  other arithmetic  52.2 us (10%)
  between operations  15.7 us (3%)
    pallas_call x2, Pallas kernels, column_sum(): pl.pallas_call(column_sum_kernel, name='sum_over_experts', out_shape=(jax...  83.3 us
    pallas_call x1, Pallas kernels, return_gradients(): pl.pallas_call(functools.partial(return_kernel, part, misc_at), name='ret...  59.7 us
    pallas_call x1, Pallas kernels, gather_weights(): pl.pallas_call(functools.partial(weights_kernel, part), name='gather_weig...  55 us
    dot_general x12, matrix products, dot_nt(): lax.dot_general(a, b, (((1,), (1,)), ((), ())), preferred_element_type=f32)  44.4 us
    dot_general x12, matrix products, dot(): return jnp.dot(a, b, preferred_element_type=f32)  42.2 us
    pallas_call x1, Pallas kernels, column_gather(): pl.pallas_call(column_gather_kernel, name='gather_normed_rows', out_shape...  35.1 us
    unnamed x161, local copies, waits for them, and re-layouts  21.6 us
    dot_general x12, matrix products, dot_tn(): lax.dot_general(a, b, (((0,), (0,)), ((), ())), preferred_element_type=f32)  21.3 us
  transfers between devices with their start and end apart: 4, of which 0 were waited for; matrix products, arithmetic and copies ran while one was open for 25% of the time, Pallas kernels for 13%

profile of v2, /device:TPU:1, one launch (start us, length us, event | category | flops | bytes accessed | tf_op | source)
XLA Modules:
  0.0 528.4 jit_solution(7309116113341351782)
XLA Ops:
  15.0 55.0 %gather_weights.1 = (bf16[2,16,96,1920]{3,2,1,0:T(8,128)(2,1)S(1)}, bf16[3,96,768]{2,1,0:T(8,128)(2,1)}, bf16[8,256,1536]{2,1,0:T(8,128)(2,1)S(1)}) custom-call(bf16[32,1920]{1,0:T(8,128)(2,1)S(1)} %pad.24.attn_ref, bf16[8,3,32,384]{3,2,1,0:T(8,128)(2,1)S(1)} %fusion.75.expert_ref, bf16[256,1536]{1,0:T(8,128)(2,1)S(1)} %dynamic-slice_bitcast_fusion.rows_ref), custom_call_target="tpu_custom_call" | custom-call | tf_op jit(solution)/shard_map/gather_weights/pallas_call | solution.py:359
  70.0 4.3 copy-done.3
  98.8 17.8 %gather_keys_values.1 = bf16[4,256,512]{2,1,0:T(8,128)(2,1)} custom-call(bf16[256,512]{1,0:T(8,128)(2,1)} %pad_maximum_fusion.5.block_ref), custom_call_target="tpu_custom_call" | custom-call | tf_op jit(solution)/shard_map/gather_keys_values/pallas_call | solution.py:402
  141.9 35.1 %gather_normed_rows.1 = (bf16[8,256,1536]{2,1,0:T(8,128)(2,1)}, f32[8,8,256]{2,1,0:T(8,128)}) custom-call(bf16[256,1536]{1,0:T(8,128)(2,1)} %copy-done.9, f32[8,256]{1,0:T(8,128)} %select_bitcast_fusion.2.gate_ref), custom_call_target="tpu_custom_call" | custom-call | tf_op jit(solution)/shard_map/gather_normed_rows/pallas_call | solution.py:478
  181.4 7.0 %convolution_convert_fusion.3 = bf16[4,320,1536]{2,1,0:T(8,128)(2,1)} fusion(bf16[4,512,1536]{2,1,0:T(8,128)(2,1)} %bitcast.282, s32[4,512]{1,0:T(4,128)S(1)} %get-tuple-element.84, pred[4,512]{1,0:T(4,128)(4,1)S(1)} %get-tuple-element.85), kind=kOutput, calls=%fused_computation.26 | convolution fusion | flops 2016542720 | bytes 10233856 | tf_op jit(solution)/shard_map/kst,ktd->ksd/dot_general | solution.py:1063
  188.4 4.1 convolution_convert_fusion.4
  192.5 6.5 %fusion.31 = f32[1280,768]{0,1:T(8,128)S(1)} fusion(bf16[1280,1536]{1,0:T(8,128)(2,1)} %bitcast.345, bf16[3,1536,768]{2,1,0:T(8,128)(2,1)} %all-gather.2.cloned.1.call-done), kind=kOutput, calls=%fused_computation.76 | convolution fusion | flops 3019898880 | bytes 10223616 | tf_op jit(solution)/shard_map/dot_general | solution.py:902
  202.6 10.1 %multiply_reduce_fusion.2 = (f32[1280]{0:T(1024)S(1)}, f32[1280,768]{0,1:T(8,128)}) fusion(f32[1280,768]{0,1:T(8,128)S(1)} %fusion.31, f32[1280,768]{0,1:T(8,128)S(1)} %fusion.30, bf16[1280,1536]{1,0:T(8,128)(2,1)} %bitcast.349, bf16[3,1536,768]{2,1,0:T(8,128)(2,1)S(1)} %copy-done.66), kind=kOutput, calls=%fused_computation.30 | convolution fusion | flops 3026778880 | bytes 18093056 | tf_op jit(solution)/shard_map/dot_general | solution.py:902
  214.0 5.7 %multiply_convert_fusion.2 = (bf16[1280,768]{0,1:T(8,128)(2,1)S(1)}, bf16[1280,768]{0,1:T(8,128)(2,1)S(1)}, bf16[1280,768]{0,1:T(8,128)(2,1)S(1)}) fusion(f32[1280,768]{0,1:T(8,128)} %get-tuple-element.146, f32[1280]{0:T(1024)S(1)} %mul.419, f32[1280,768]{0,1:T(8,128)} %copy-done.18, f32[1280,768]{0,1:T(8,128)} %copy-done.17), kind=kLoop, calls=%fused_computation.28 | loop fusion | flops 16711680 | bytes 17699840 | tf_op jit(solution)/shard_map/convert_element_type | solution.py:1098
  230.4 5.1 convolution_convert_fusion
  235.5 5.8 %convolution_convert_fusion.2 = bf16[4,512,1536]{2,1,0:T(8,128)(2,1)S(1)} fusion(bf16[4,320,1536]{2,1,0:T(8,128)(2,1)} %bitcast.352, s32[4,512]{1,0:T(4,128)S(1)} %get-tuple-element.84, pred[4,512]{1,0:T(4,128)(4,1)S(1)} %get-tuple-element.85), kind=kOutput, calls=%fused_computation.22 | convolution fusion | flops 2017722368 | bytes 10233856 | tf_op jit(solution)/shard_map/kst,ksd->ktd/dot_general | solution.py:1070
  241.3 5.7 %fusion.29 = f32[1280,1536]{1,0:T(8,128)} fusion(bf16[1280,768]{0,1:T(8,128)(2,1)S(1)} %get-tuple-element.87, bf16[3,1536,768]{2,1,0:T(8,128)(2,1)S(1)} %bitcast.343), kind=kOutput, calls=%fused_computation.74 | convolution fusion | flops 3019898880 | bytes 12189696 | tf_op jit(solution)/shard_map/dot_general | solution.py:906
  247.0 7.8 %fusion.1 = bf16[1280,1536]{1,0:T(8,128)(2,1)} fusion(f32[1280,1536]{1,0:T(8,128)} %fusion.29, bf16[1280,768]{0,1:T(8,128)(2,1)S(1)} %get-tuple-element.86, bf16[3,1536,768]{2,1,0:T(8,128)(2,1)} %all-gather.2.cloned.1.call-done), kind=kOutput, calls=%fused_computation.3 | convolution fusion | flops 3023831040 | bytes 16121856 | tf_op jit(solution)/shard_map/dot_general | solution.py:906
  254.8 5.8 %convolution_convert_fusion.1 = bf16[4,512,1536]{2,1,0:T(8,128)(2,1)S(1)} fusion(bf16[4,320,1536]{2,1,0:T(8,128)(2,1)} %bitcast.351, s32[4,512]{1,0:T(4,128)S(1)} %get-tuple-element.84, pred[4,512]{1,0:T(4,128)(4,1)S(1)} %get-tuple-element.85), kind=kOutput, calls=%fused_computation.21 | convolution fusion | flops 2017722368 | bytes 10233856 | tf_op jit(solution)/shard_map/kst,ksd->ktd/dot_general | solution.py:1070
  260.6 42.0 %sum_over_experts.2 = (f32[256,1536]{1,0:T(8,128)S(1)}, f32[8,2,128]{2,1,0:T(2,128)}) custom-call(bf16[8,256,1536]{2,1,0:T(8,128)(2,1)S(1)} %bitcast.269, f32[8,2,128]{2,1,0:T(2,128)S(1)} %reshape.618.small_ref), custom_call_target="tpu_custom_call" | custom-call | tf_op jit(solution)/shard_map/sum_over_experts/pallas_call | solution.py:560
  302.6 41.3 %sum_over_experts.3 = (f32[256,1536]{1,0:T(8,128)S(1)}, f32[8,2,128]{2,1,0:T(2,128)S(1)}) custom-call(bf16[8,256,1536]{2,1,0:T(8,128)(2,1)S(1)} %bitcast.270, f32[8,2,128]{2,1,0:T(2,128)S(1)} %reshape.618.small_ref), custom_call_target="tpu_custom_call" | custom-call | tf_op jit(solution)/shard_map/sum_over_experts/pallas_call | solution.py:560
  360.2 4.3 multiply_reduce_fusion.1
  365.2 4.6 multiply_convert_fusion.1
  369.8 4.0 convolution_multiply_fusion.1
  377.9 4.4 multiply_reduce_fusion
  382.8 4.6 multiply_convert_fusion
  394.6 16.2 %sum_key_value_gradients.1 = f32[256,512]{1,0:T(8,128)} custom-call(bf16[4,256,512]{2,1,0:T(8,128)(2,1)} %pad_maximum_fusion.2.parts_ref), custom_call_target="tpu_custom_call" | custom-call | tf_op jit(solution)/shard_map/sum_key_value_gradients/pallas_call | solution.py:441
  434.6 10.5 %copy.115 = bf16[2,1536,1152]{2,1,0:T(8,128)(2,1)} copy(bf16[2,1536,1152]{1,2,0:T(8,128)(2,1)} %fusion.2) | data formatting | bytes 14155776 | tf_op jit(solution)/shard_map/concatenate | solution.py:1183
  458.0 59.7 %return_gradients.1 = (f32[24,1920]{1,0:T(8,128)S(1)}, f32[24,128]{1,0:T(8,128)S(1)}, bf16[8,3,32,384]{3,2,1,0:T(8,128)(2,1)S(1)}) custom-call(bf16[2,16,96,1152]{3,2,1,0:T(8,128)(2,1)} %bitcast.287, bf16[2,16,96,768]{3,2,1,0:T(8,128)(2,1)S(1)} %copy-done.2, bf16[8,3,32,384]{3,2,1,0:T(8,128)(2,1)S(1)} %bitcast.271), custom_call_target="tpu_custom_call" | custom-call | tf_op jit(solution)/shard_map/return_gradients/pallas_call | solution.py:869
  (314 shorter events, 145.3 us)
Async XLA Ops:
  7.2 126.4 %copy-start = (s32[1,512,4]{1,2,0:T(4,128)S(1)}, s32[1,512,4]{1,2,0:T(4,128)}, u32[]{:S(2)}) copy-start(s32[1,512,4]{1,2,0:T(4,128)} %param.16) | copy-start | bytes 24580
  7.2 185.3 %all-gather.2.cloned.1.call-start = ((), (), s32[]{:S(2)}) async-start(), calls=%async_computation.1 | async-start | bytes 7520256 | tf_op jit(solution)/shard_map/all_gather | solution.py:959
  12.5 65.7 %copy-start.21 = (bf16[1,512,1536]{2,1,0:T(8,128)(2,1)S(1)}, bf16[1,512,1536]{2,1,0:T(8,128)(2,1)}, u32[]{:S(2)}) copy-start(bf16[1,512,1536]{2,1,0:T(8,128)(2,1)} %param.14) | copy-start | bytes 4718596
  76.9 377.5 %reduce-scatter.2.cloned.1.call-start = ((), (), s32[]{:S(2)}) async-start(), calls=%async_computation.2 | async-start | bytes 7520256 | tf_op jit(solution)/shard_map/reduce_scatter | solution.py:1106
  119.9 7.6 %copy-start.29 = (bf16[6,256,128]{2,1,0:T(8,128)(2,1)}, bf16[6,256,128]{2,1,0:T(8,128)(2,1)S(1)}, u32[]{:S(2)}) copy-start(bf16[6,256,128]{2,1,0:T(8,128)(2,1)S(1)} %copy.94) | copy-start | bytes 1179652
  133.6 6.9 %copy-start.47 = (s32[256,4]{0,1:T(4,128)}, s32[256,4]{0,1:T(4,128)S(1)}, u32[]{:S(2)}) copy-start(s32[256,4]{0,1:T(4,128)S(1)} %dynamic-slice_bitcast_fusion.1) | copy-start | bytes 12292
  139.1 41.6 %copy-start.51 = (f32[1536]{0:T(1024)S(1)}, f32[1536]{0:T(1024)}, u32[]{:S(2)}) copy-start(f32[1536]{0:T(1024)} %copy-done.50) | copy-start | bytes 18436
  139.1 41.6 %copy-start.59 = (f32[1536]{0:T(1024)S(1)}, f32[1536]{0:T(1024)}, u32[]{:S(2)}) copy-start(f32[1536]{0:T(1024)} %copy-done.58) | copy-start | bytes 18436
  139.1 41.6 %copy-start.53 = (f32[1536]{0:T(1024)S(1)}, f32[1536]{0:T(1024)}, u32[]{:S(2)}) copy-start(f32[1536]{0:T(1024)} %copy-done.52) | copy-start | bytes 18436
  139.1 41.6 %copy-start.61 = (f32[1536]{0:T(1024)S(1)}, f32[1536]{0:T(1024)}, u32[]{:S(2)}) copy-start(f32[1536]{0:T(1024)} %copy-done.60) | copy-start | bytes 18436
  181.4 7.0 %copy-start.67 = (bf16[8,256,1536]{2,1,0:T(8,128)(2,1)S(1)}, bf16[8,256,1536]{2,1,0:T(8,128)(2,1)}, u32[]{:S(2)}) copy-start(bf16[8,256,1536]{2,1,0:T(8,128)(2,1)} %get-tuple-element.25) | copy-start | bytes 18874372
  192.5 6.5 %copy-start.66 = (bf16[3,1536,768]{2,1,0:T(8,128)(2,1)S(1)}, bf16[3,1536,768]{2,1,0:T(8,128)(2,1)}, u32[]{:S(2)}) copy-start(bf16[3,1536,768]{2,1,0:T(8,128)(2,1)} %all-gather.2.cloned.1.call-done) | copy-start | bytes 21233668
  192.5 6.5 %copy-start.68 = (bf16[4,320,1536]{2,1,0:T(8,128)(2,1)S(1)}, bf16[4,320,1536]{2,1,0:T(8,128)(2,1)}, u32[]{:S(2)}) copy-start(bf16[4,320,1536]{2,1,0:T(8,128)(2,1)} %convolution_convert_fusion.4) | copy-start | bytes 11796484
  202.6 10.1 %copy-start.18 = (f32[1280,768]{0,1:T(8,128)}, f32[1280,768]{0,1:T(8,128)S(1)}, u32[]{:S(2)}) copy-start(f32[1280,768]{0,1:T(8,128)S(1)} %fusion.30) | copy-start | bytes 11796484
  223.3 7.1 %slice-start.5 = ((s8[7077888]{0:T(1024)(128)(4,1)}), s8[4194304]{0:T(1024)(128)(4,1)S(1)}, s32[]{:S(2)}) async-start(s8[7077888]{0:T(1024)(128)(4,1)} %bitcast.342), calls=%async_computation.8 | async-start | bytes 8388608
  302.6 41.4 %copy-start.48 = (s32[256,4]{0,1:T(4,128)S(1)}, s32[256,4]{0,1:T(4,128)}, u32[]{:S(2)}) copy-start(s32[256,4]{0,1:T(4,128)} %copy-done.47) | copy-start | bytes 12292
  359.0 90.5 %collective-permute-start = (bf16[256,1536]{1,0:T(8,128)(2,1)}, bf16[256,1536]{1,0:T(8,128)(2,1)}, u32[]{:S(2)}, u32[]{:S(2)}) collective-permute-start(bf16[256,1536]{1,0:T(8,128)(2,1)} %get-tuple-element.95), channel_id=1, source_target_pairs={{0,1},{1,0},{2,3},{3,2},{4,5},{5,4},{6,7},{7,6},{8,9},{9,8},{10,11... | collective-permute-start | bytes 2359304 | tf_op jit(solution)/shard_map/ppermute | solution.py:914
  369.8 6.4 %copy-start.8 = (bf16[1536,1024]{0,1:T(8,128)(2,1)S(1)}, bf16[1536,1024]{0,1:T(8,128)(2,1)}, u32[]{:S(2)}) copy-start(bf16[1536,1024]{0,1:T(8,128)(2,1)} %get-tuple-element.89) | copy-start | bytes 9437188
  369.8 6.4 %copy-start.32 = (bf16[6,256,128]{2,1,0:T(8,128)(2,1)S(1)}, bf16[6,256,128]{2,1,0:T(8,128)(2,1)}, u32[]{:S(2)}) copy-start(bf16[6,256,128]{2,1,0:T(8,128)(2,1)} %copy-done.31) | copy-start | bytes 1179652
  392.5 18.3 %copy-start.7 = (bf16[1536,1024]{0,1:T(8,128)(2,1)S(1)}, bf16[1536,1024]{0,1:T(8,128)(2,1)}, u32[]{:S(2)}) copy-start(bf16[1536,1024]{0,1:T(8,128)(2,1)} %get-tuple-element.91) | copy-start | bytes 9437188
  428.3 23.9 %collective-permute-start.1 = (bf16[256,1536]{1,0:T(8,128)(2,1)S(1)}, bf16[256,1536]{1,0:T(8,128)(2,1)S(1)}, u32[]{:S(2)}, u32[]{:S(2)}) collective-permute-start(bf16[256,1536]{1,0:T(8,128)(2,1)S(1)} %fusion.44), channel_id=1, source_target_pairs={{0,1},{1,0},{2,3},{3,2},{4,5},{5,4},{6,7},{7,6},{8,9},{9,8},{10,11... | collective-permute-start | bytes 2359304 | tf_op jit(solution)/shard_map/ppermute | solution.py:914
  434.6 10.5 %copy-start.11 = (bf16[1536,256]{1,0:T(8,128)(2,1)S(1)}, bf16[1536,256]{1,0:T(8,128)(2,1)}, u32[]{:S(2)}) copy-start(bf16[1536,256]{1,0:T(8,128)(2,1)} %copy.116) | copy-start | bytes 2359300
  434.6 10.5 %copy-start.20 = (bf16[6,256,128]{1,2,0:T(8,128)(2,1)S(1)}, bf16[6,256,128]{1,2,0:T(8,128)(2,1)}, u32[]{:S(2)}) copy-start(bf16[6,256,128]{1,2,0:T(8,128)(2,1)} %copy-done.19) | copy-start | bytes 1179652
  458.0 63.4 %copy-start.1 = (s32[1,512,4]{1,2,0:T(4,128)S(1)}, s32[1,512,4]{1,2,0:T(4,128)}, u32[]{:S(2)}) copy-start(s32[1,512,4]{1,2,0:T(4,128)} %param.16) | copy-start | bytes 24580
  (58 other events, 182.7 us)
Sparse Core Ops, SparseCore 0:
  77.0 63.7 all-gather.1
  356.4 79.8 reduce-scatter.1

commit v3 on v2

--- a/solution.py
+++ b/solution.py
@@ -119,46 +119,68 @@
     return len(COLUMN)
 
 
+def partner():
+    return {"l": 1 - lax.axis_index("l")}
+
+
+def cross():
+    return {"h": 1 - lax.axis_index("h"), "l": 1 - lax.axis_index("l")}
+
+
+def other_core():
+    return {"c": 1 - lax.axis_index("c")}
+
+
 class ColumnRing:
     def __init__(self, lanes, rows_ref, out_ref):
         c, h, l = place()
         self.lanes, self.rows, self.out = lanes, rows_ref, out_ref
-        self.c, self.z = c, h * 2 + l
-        self.half = rows_ref.shape[0] // 2
-        self.copies = []
-
-    def at(self, step):
-        return self.c * 4 + lax.rem(self.z + step + 4, 4)
-
-    def forward(self, step):
-        block = self.out.at[self.at(step)]
-        self.copies.append(self.lanes.send(block, block, column_peer(1, 0)))
+        half = rows_ref.shape[0] // 2
+        self.first, self.second = pl.ds(0, half), pl.ds(half, half)
+        self.at = {
+            "own": c * 4 + h * 2 + l,
+            "partner": c * 4 + h * 2 + 1 - l,
+            "cross": c * 4 + (1 - h) * 2 + 1 - l,
+            "far": c * 4 + (1 - h) * 2 + l,
+        }
+        self.shared = {}
+
+    def share(self, which):
+        block = self.out.at[self.at[which]]
+        self.shared[which] = self.lanes.send(block, block, other_core())
 
     def start(self):
-        here = self.out.at[self.at(0)]
-        self.up = self.lanes.send(self.rows, here, column_peer(0, 1))
-        self.down = self.lanes.send(self.rows, here, column_peer(0, 3))
-        self.copies.append(self.lanes.send(self.rows, here, column_peer(1, 0)))
+        here = self.out.at[self.at["own"]]
+        self.to_partner = self.lanes.send(self.rows, here, partner())
+        self.to_cross = self.lanes.send(self.rows, here, cross())
+        self.shared["own"] = self.lanes.send(self.rows, here, other_core())
 
     def relay(self):
-        lower, upper = pl.ds(0, self.half), pl.ds(self.half, self.half)
-        self.up.wait_recv()
-        block = self.out.at[self.at(-1), lower]
-        self.up_far = self.lanes.send(block, block, column_peer(0, 1))
-        self.down.wait_recv()
-        block = self.out.at[self.at(1), upper]
-        self.down_far = self.lanes.send(block, block, column_peer(0, 3))
-        self.forward(-1)
-        self.forward(1)
+        self.to_partner.wait_recv()
+        block = self.out.at[self.at["partner"], self.first]
+        self.far_cross = self.lanes.send(block, block, cross())
+        self.to_cross.wait_recv()
+        block = self.out.at[self.at["cross"], self.second]
+        self.far_partner = self.lanes.send(block, block, partner())
+        self.share("partner")
+        self.share("cross")
+
+    def far(self):
+        self.far_cross.wait_recv()
+        self.far_partner.wait_recv()
+        self.share("far")
+
+    def drain(self):
+        for copy in (self.to_partner, self.to_cross, self.far_cross, self.far_partner):
+            copy.wait_send()
+        for copy in self.shared.values():
+            copy.wait_send()
 
     def finish(self):
-        self.up_far.wait_recv()
-        self.down_far.wait_recv()
-        self.forward(2)
-        for copy in (self.up, self.down, self.up_far, self.down_far):
-            copy.wait_send()
-        for copy in self.copies:
-            copy.wait()
+        self.far()
+        for copy in self.shared.values():
+            copy.wait_recv()
+        self.drain()
 
 
 class ChipRing:
@@ -241,9 +263,11 @@
     attn_ref,
     expert_ref,
     rows_ref,
+    slots_ref,
     w_out,
     expert_out,
     rows_out,
+    slots_out,
     attn_in,
     expert_in,
     block,
@@ -280,8 +304,11 @@
         peer = column_peer(*step)
         to = (peer["c"] * 2 + peer["h"]) * 2 + peer["l"]
         pieces.append(lanes.send(expert_ref.at[to], expert_in.at[me], peer))
+        pieces.append(lanes.send(slots_ref.at[to], slots_out.at[me], peer))
     own_rows = pltpu.make_async_copy(rows_ref, rows_out.at[me], own.at[2])
     own_rows.start()
+    own_slots = pltpu.make_async_copy(slots_ref.at[me], slots_out.at[me], own.at[4])
+    own_slots.start()
     ring = ColumnRing(lanes, rows_ref, rows_out)
     ring.start()
 
@@ -341,6 +368,7 @@
         ring_half.drain()
     keep.wait()
     own_rows.wait()
+    own_slots.wait()
     pl.when(c != l)(there.wait_send)
     for z_step in range(1, 4):
         pltpu.make_async_remote_copy(
@@ -353,7 +381,7 @@
         ).wait_send()
 
 
-def gather_weights(attn_block, expert_pieces, rows, part):
+def gather_weights(attn_block, expert_pieces, rows, slots, part):
     width = attn_block.shape[1]
     ff_half = expert_pieces.shape[3]
     return pl.pallas_call(
@@ -363,24 +391,25 @@
             jax.ShapeDtypeStruct((2, 16, 4 * part, width), bf16),
             jax.ShapeDtypeStruct((3, 4 * part, 2 * ff_half), bf16),
             jax.ShapeDtypeStruct((8,) + rows.shape, bf16),
+            jax.ShapeDtypeStruct(slots.shape, f32),
         ),
-        in_specs=[VMEM, ANY, ANY],
-        out_specs=(ANY, VMEM, ANY),
+        in_specs=[VMEM, ANY, ANY, ANY],
+        out_specs=(ANY, VMEM, ANY, ANY),
         scratch_shapes=[
             pltpu.VMEM((4,) + attn_block.shape, bf16),
             pltpu.VMEM(expert_pieces.shape, bf16),
             pltpu.VMEM((4 * part, width), bf16),
         ]
-        + lanes_scratch(90)
+        + lanes_scratch(100)
         + [
             pltpu.SemaphoreType.DMA((4,)),
             pltpu.SemaphoreType.DMA((4,)),
-            pltpu.SemaphoreType.DMA((4,)),
+            pltpu.SemaphoreType.DMA((5,)),
         ],
         compiler_params=pltpu.CompilerParams(
             collective_id=1, has_side_effects=True, vmem_limit_bytes=32 * 2**20
         ),
-    )(attn_block, expert_pieces, rows)
+    )(attn_block, expert_pieces, rows, slots)
 
 
 def along_z_kernel(block_ref, out_ref, s_sem, r_sem, own):
@@ -453,40 +482,349 @@
     )(parts)
 
 
-def column_gather_kernel(rows_ref, gate_ref, rows_out, gates_out, s_sem, r_sem, own):
+def experts_kernel(
+    rows_ref,
+    gate_ref,
+    grads_ref,
+    slot_rows,
+    slot_columns,
+    weights_ref,
+    mix_out,
+    weight_grads,
+    back_out,
+    gate_back_out,
+    rows_all,
+    held,
+    w_gate,
+    w_up,
+    w_down,
+    picked,
+    picked_grads,
+    hidden_back,
+    hidden_gated,
+    gate_low,
+    up_low,
+    mix_stage,
+    near,
+    far,
+    nearest,
+    gates_in,
+    gate_back,
+    s_sem,
+    r_sem,
+    own,
+    stage_sem,
+    near_send,
+    near_recv,
+):
     c, h, l = place()
-    me = c * 4 + h * 2 + l
+    me = (c * 2 + h) * 2 + l
     barrier = pltpu.get_barrier_semaphore()
     pl.semaphore_wait(barrier, greet_column(barrier))
     lanes = Lanes(s_sem, r_sem)
-    ring = ColumnRing(lanes, rows_ref, rows_out)
+    rows, width = rows_ref.shape
+    slots = picked.shape[1]
+    ff = w_gate.shape[1]
+    block = 2 * rows
+
+    ring = ColumnRing(lanes, rows_ref, rows_all)
     ring.start()
-    own_copies = [
-        pltpu.make_async_copy(rows_ref, rows_out.at[me], own.at[0]),
-        pltpu.make_async_copy(gate_ref, gates_out.at[me], own.at[1]),
+    local = [
+        pltpu.make_async_copy(grads_ref, held, own.at[0]),
+        pltpu.make_async_copy(weights_ref.at[2], w_down, own.at[1]),
+        pltpu.make_async_copy(weights_ref.at[0], w_gate, own.at[2]),
+        pltpu.make_async_copy(weights_ref.at[1], w_up, own.at[3]),
+        pltpu.make_async_copy(rows_ref, rows_all.at[me], own.at[4]),
+        pltpu.make_async_copy(gate_ref.at[me], gates_in.at[me], own.at[5]),
     ]
-    for copy in own_copies:
+    for copy in local:
         copy.start()
-    copies = [lanes.send(gate_ref, gates_out.at[me], column_peer(*step)) for step in COLUMN]
+    gate_copies = []
+    for step in COLUMN:
+        peer = column_peer(*step)
+        to = (peer["c"] * 2 + peer["h"]) * 2 + peer["l"]
+        gate_copies.append(lanes.send(gate_ref.at[to], gates_in.at[me], peer))
+
+    def pick_of(k):
+        number = lax.broadcasted_iota(jnp.int32, (slots, block), 0).astype(f32)
+        return slot_rows[k] == number
+
+    def spread_of(k):
+        number = lax.broadcasted_iota(jnp.int32, (block, slots), 1).astype(f32)
+        return (slot_columns[k] == number).astype(f32).astype(bf16)
+
+    def low(mask):
+        return mask.astype(f32).astype(bf16)
+
+    def both(ref, k, columns=None):
+        if columns is None:
+            return ref[pl.ds(2 * k, 2)].reshape(block, width)
+        return ref[pl.ds(2 * k, 2), :, columns].reshape(block, -1)
+
+    wide = 512
+    narrow = 256
+
+    def at(i, size):
+        return pl.ds(pl.multiple_of(i * size, size), size)
+
+    local[0].wait()
+    local[1].wait()
+
+    def prepare(k, carry):
+        pick = low(pick_of(k))
+
+        def gather(i, carry):
+            columns = at(i, wide)
+            values = ref_dot(pick, held[pl.ds(2 * k, 2), :, columns].reshape(block, wide))
+            picked_grads[k, :, columns] = values.astype(bf16)
+            return carry
+
+        lax.fori_loop(0, width // wide, gather, 0)
+
+        def down(i, carry):
+            columns = at(i, narrow)
+            hidden_back[k, :, columns] = ref_dot(picked_grads[k], w_down[:, columns])
+            return carry
+
+        lax.fori_loop(0, ff // narrow, down, 0)
+        return carry
+
+    lax.fori_loop(0, 4, prepare, 0)
     ring.relay()
-    ring.finish()
-    for copy in own_copies + copies:
+    for copy in local[2:]:
         copy.wait()
-
-
-def column_gather(rows, gates):
+    for copy in gate_copies:
+        copy.wait()
+    ring.shared["own"].wait_recv()
+    ring.shared["partner"].wait_recv()
+
+    def expert(k, stage):
+        pick = pick_of(k)
+        pick_low = low(pick)
+        spread = spread_of(k)
+        gates = gates_in[pl.ds(2 * k, 2)]
+        gate_row = jnp.concatenate([gates[0], gates[1]], axis=1)
+        gate = jnp.sum(jnp.where(pick, gate_row, 0.0), axis=1, keepdims=True)
+
+        def gather(i, carry):
+            columns = at(i, wide)
+            values = ref_dot(pick_low, rows_all[pl.ds(2 * k, 2), :, columns].reshape(block, wide))
+            picked[k, :, columns] = values.astype(bf16)
+            return carry
+
+        lax.fori_loop(0, width // wide, gather, 0)
+
+        def hide(i, total):
+            columns = at(i, narrow)
+            gate_act = ref_dot(picked[k], w_gate[:, columns])
+            up_act = ref_dot(picked[k], w_up[:, columns])
+            back = hidden_back[k, :, columns]
+            sigmoid_act = 1.0 / (1.0 + jnp.exp(-gate_act))
+            silu_act = gate_act * sigmoid_act
+            hidden = silu_act * up_act
+            hidden_gated[k, :, columns] = (hidden * gate).astype(bf16)
+            total = total + jnp.sum(hidden * back, axis=1, keepdims=True)
+            back = back * gate
+            slope = sigmoid_act * (1.0 + gate_act * (1.0 - sigmoid_act))
+            gate_low[k, :, columns] = (back * up_act * slope).astype(bf16)
+            up_low[k, :, columns] = (back * silu_act).astype(bf16)
+            return total
+
+        gate_slots = lax.fori_loop(0, ff // narrow, hide, jnp.zeros((slots, 1), f32))
+        back_row = jnp.sum(jnp.where(pick, gate_slots, 0.0), axis=0, keepdims=True)
+        gate_back[2 * k] = back_row[:, :rows]
+        gate_back[2 * k + 1] = back_row[:, rows:]
+
+        def leave(i, carry):
+            columns = at(i, wide)
+            out = ref_dot_nt(hidden_gated[k], w_down[columns, :]).astype(bf16)
+            mix_stage[stage, :, :, columns] = (
+                ref_dot(spread, out).astype(bf16).reshape(2, rows, wide)
+            )
+            back = ref_dot_nt(gate_low[k], w_gate[columns, :])
+            back = (back + ref_dot_nt(up_low[k], w_up[columns, :])).astype(bf16)
+            held[pl.ds(2 * k, 2), :, columns] = (
+                ref_dot(spread, back).astype(bf16).reshape(2, rows, wide)
+            )
+            return carry
+
+        lax.fori_loop(0, width // wide, leave, 0)
+
+    def stage_copy(k, stage):
+        return pltpu.make_async_copy(
+            mix_stage.at[stage], mix_out.at[pl.ds(2 * k, 2)], stage_sem.at[stage]
+        )
+
+    def near_copy(side, i):
+        return pltpu.make_async_remote_copy(
+            src_ref=held.at[pl.ds(((1 - c) * 2 + side) * 2, 2)],
+            dst_ref=near.at[pl.ds(side * 2, 2)],
+            send_sem=near_send.at[i],
+            recv_sem=near_recv.at[i],
+            device_id=other_core(),
+            device_id_type=MESH,
+        )
+
+    expert((1 - c) * 2 + h, 0)
+    near_copy(h, 0).start()
+    stage_copy((1 - c) * 2 + h, 0).start()
+    ring.far()
+    expert(c * 2 + h, 1)
+    stage_copy(c * 2 + h, 1).start()
+
+    def add_near(z):
+        mine = held.at[c * 4 + z]
+
+        def add(i, carry):
+            here = at(i, 64)
+            mine[here] = mine[here] + near[z, here]
+            return carry
+
+        lax.fori_loop(0, rows // 64, add, 0)
+
+    half = rows // 2
+    first, second = pl.ds(0, half), pl.ds(half, half)
+    z = {
+        "own": h * 2 + l,
+        "partner": h * 2 + 1 - l,
+        "cross": (1 - h) * 2 + 1 - l,
+        "far": (1 - h) * 2 + l,
+    }
+
+    def block_at(which, part):
+        return held.at[c * 4 + z[which], part]
+
+    near_copy(h, 0).wait_recv()
+    add_near(z["partner"])
+    sends = []
+    early_partner = lanes.send(
+        block_at("partner", first), nearest.at[0, first], partner()
+    )
+    add_near(z["own"])
+    ring.shared["cross"].wait_recv()
+    ring.shared["far"].wait_recv()
+
+    for stage, k in ((0, (1 - c) * 2 + 1 - h), (1, c * 2 + 1 - h)):
+        stage_copy(k, stage).wait()
+        expert(k, stage)
+        stage_copy(k, stage).start()
+        if stage == 0:
+            near_copy(1 - h, 1).start()
+    gate_own = pltpu.make_async_copy(gate_back.at[me], gate_back_out.at[me], own.at[6])
+    gate_own.start()
+    for step in COLUMN:
+        peer = column_peer(*step)
+        to = (peer["c"] * 2 + peer["h"]) * 2 + peer["l"]
+        sends.append(lanes.send(gate_back.at[to], gate_back_out.at[me], peer))
+    near_copy(1 - h, 1).wait_recv()
+    add_near(z["far"])
+    far_partner = lanes.send(block_at("far", first), far.at[0], partner())
+    far_cross = lanes.send(block_at("far", second), far.at[1], cross())
+    add_near(z["cross"])
+    early_cross = lanes.send(block_at("cross", second), nearest.at[1, second], cross())
+
+    def weight_grad(values, others, target, number):
+        def rows_of(i, carry):
+            columns = at(i, narrow)
+            left = values[:, :, columns].reshape(4 * slots, narrow)
+            target[columns, :] = ref_dot_tn(left, others[...].reshape(4 * slots, ff)).astype(bf16)
+            return carry
+
+        lax.fori_loop(0, width // narrow, rows_of, 0)
+        copy = pltpu.make_async_copy(target, weight_grads.at[number], own.at[1 + number])
+        copy.start()
+        return copy
+
+    grad_copies = [weight_grad(picked_grads, hidden_gated, w_down, 2)]
+    far_partner.wait_recv()
+    mine = block_at("cross", first)
+    mine[...] = mine[...] + far[0]
+    late_cross = lanes.send(mine, nearest.at[1, first], cross())
+    far_cross.wait_recv()
+    mine = block_at("partner", second)
+    mine[...] = mine[...] + far[1]
+    late_partner = lanes.send(mine, nearest.at[0, second], partner())
+    grad_copies.append(weight_grad(picked, gate_low, w_gate, 0))
+    grad_copies.append(weight_grad(picked, up_low, w_up, 1))
+    for copy in (early_partner, early_cross, late_cross, late_partner):
+        copy.wait_recv()
+
+    def finish(i, carry):
+        here = at(i, 64)
+        total = held[c * 4 + z["own"], here].astype(f32)
+        back_out[here, :] = (
+            total + nearest[0, here].astype(f32) + nearest[1, here].astype(f32)
+        )
+        return carry
+
+    lax.fori_loop(0, rows // 64, finish, 0)
+    for copy in (early_partner, early_cross, late_cross, late_partner, far_partner, far_cross):
+        copy.wait_send()
+    for i, side in ((0, h), (1, 1 - h)):
+        near_copy(side, i).wait_send()
+    for copy in sends + grad_copies + [gate_own]:
+        copy.wait()
+    for stage, k in ((0, (1 - c) * 2 + 1 - h), (1, c * 2 + 1 - h)):
+        stage_copy(k, stage).wait()
+    ring.drain()
+
+
+def ref_dot(a, b):
+    return jnp.dot(a, b, preferred_element_type=f32)
+
+
+def ref_dot_nt(a, b):
+    return lax.dot_general(a, b, (((1,), (1,)), ((), ())), preferred_element_type=f32)
+
+
+def ref_dot_tn(a, b):
+    return lax.dot_general(a, b, (((0,), (0,)), ((), ())), preferred_element_type=f32)
+
+
+def experts_of_column(rows, gates, grads_all, slots, weights):
+    count, width = rows.shape
+    ff = weights.shape[2]
     return pl.pallas_call(
-        column_gather_kernel,
-        name="gather_normed_rows",
+        experts_kernel,
+        name="experts",
         out_shape=(
-            jax.ShapeDtypeStruct((8,) + rows.shape, rows.dtype),
-            jax.ShapeDtypeStruct((8,) + gates.shape, gates.dtype),
+            jax.ShapeDtypeStruct((8, count, width), bf16),
+            jax.ShapeDtypeStruct(weights.shape, bf16),
+            jax.ShapeDtypeStruct((count, width), f32),
+            jax.ShapeDtypeStruct(gates.shape, f32),
         ),
-        in_specs=[ANY, ANY],
-        out_specs=(ANY, ANY),
-        scratch_shapes=lanes_scratch(16) + [pltpu.SemaphoreType.DMA((2,))],
-        compiler_params=pltpu.CompilerParams(collective_id=4, has_side_effects=True),
-    )(rows, gates)
+        in_specs=[VMEM, VMEM, ANY, VMEM, VMEM, ANY],
+        out_specs=(ANY, ANY, VMEM, VMEM),
+        scratch_shapes=[
+            pltpu.VMEM((8, count, width), bf16),
+            pltpu.VMEM((8, count, width), bf16),
+            pltpu.VMEM((width, ff), bf16),
+            pltpu.VMEM((width, ff), bf16),
+            pltpu.VMEM((width, ff), bf16),
+            pltpu.VMEM((4, SLOTS, width), bf16),
+            pltpu.VMEM((4, SLOTS, width), bf16),
+            pltpu.VMEM((4, SLOTS, ff), f32),
+            pltpu.VMEM((4, SLOTS, ff), bf16),
+            pltpu.VMEM((4, SLOTS, ff), bf16),
+            pltpu.VMEM((4, SLOTS, ff), bf16),
+            pltpu.VMEM((2, 2, count, width), bf16),
+            pltpu.VMEM((4, count, width), bf16),
+            pltpu.VMEM((2, count // 2, width), bf16),
+            pltpu.VMEM((2, count, width), bf16),
+            pltpu.VMEM(gates.shape, f32),
+            pltpu.VMEM(gates.shape, f32),
+        ]
+        + lanes_scratch(32)
+        + [
+            pltpu.SemaphoreType.DMA((7,)),
+            pltpu.SemaphoreType.DMA((2,)),
+            pltpu.SemaphoreType.DMA((2,)),
+            pltpu.SemaphoreType.DMA((2,)),
+        ],
+        compiler_params=pltpu.CompilerParams(
+            collective_id=4, has_side_effects=True, vmem_limit_bytes=60 * 2**20
+        ),
+    )(rows, gates, grads_all, slots[:, None, :], slots[:, :, None], weights)
 
 
 def column_sum_kernel(
@@ -951,13 +1289,19 @@
         jnp.stack([w_gate, w_up, w_down], axis=1), ((0, 0), (0, 0), (0, PAD - part), (0, 0))
     )
     upstream_low = lax.dynamic_slice_in_dim(block_cotangent[0], l * rows, rows)
-    w_attn, expert_col, grads_all = gather_weights(attn_block, expert_pieces, upstream_low, part)
+    hot_all = routes[0][:, :, None] == jnp.arange(experts, dtype=jnp.int32)[None, None, :]
+    named = jnp.any(hot_all, axis=1)
+    slot_of = jnp.cumsum(named.astype(jnp.int32), axis=0) - 1
+    slot_of = jnp.where(named, slot_of, -1).astype(f32).T
+    slot_of = lax.dynamic_slice_in_dim(slot_of, l * rows, rows, axis=1)[:, None, :]
+    w_attn, expert_col, grads_all, slots = gather_weights(
+        attn_block, expert_pieces, upstream_low, slot_of, part
+    )
     kv_width = key_matrix.shape[1]
     in_width = q_half + 2 * kv_width + MISC
     w_attn = w_attn.reshape(2, model_width, attn_block.shape[1])
     w_out = w_attn[:, :, in_width:]
     expert_full = lax.all_gather(expert_col, ("x", "y"), axis=1, tiled=True)
-    gate_w, up_w, down_w = expert_full[0], expert_full[1], expert_full[2]
     qkv_w = w_attn[:, :, : q_half + 2 * kv_width]
     misc_full = w_attn[0, :, q_half + 2 * kv_width : in_width]
     attn_scale = misc_full[:, 0].astype(f32)
@@ -1035,77 +1379,13 @@
     chosen = jnp.sum(hot_routes * logits[:, None, :], axis=-1)
     gate_expo = jnp.exp(chosen - jnp.max(chosen, axis=1, keepdims=True))
     gate_weights = gate_expo / jnp.sum(gate_expo, axis=1, keepdims=True)
-    named = jnp.sum(hot_routes, axis=1)
-    gate_rows = jnp.sum(gate_weights[:, :, None] * hot_routes, axis=1)
-    gate_sent = jnp.where(named > 0, gate_rows, -1.0).T
-
-    rows_all, gates_all = column_gather(normed_mix, gate_sent)
-    expert = (c * 2 + h) * 2 + l
-    block = 2 * rows
-    rows_all = rows_all.reshape(4, block, model_width)
-    grads_all = grads_all.reshape(4, block, model_width)
-    gate_own = lax.dynamic_index_in_dim(gates_all, expert, axis=1, keepdims=False).reshape(
-        4, block
-    )
-    taken = gate_own >= 0
-    taken_low = taken.astype(jnp.int32)
-    slot_of = jnp.cumsum(taken_low, axis=1) - taken_low
-    hot_slots = (slot_of[:, None, :] == jnp.arange(SLOTS, dtype=jnp.int32)[None, :, None]) & taken[
-        :, None, :
-    ]
-    pick = hot_slots.astype(bf16)
-    slot_gate = jnp.sum(jnp.where(hot_slots, gate_own[:, None, :], 0.0), axis=2).reshape(
-        4 * SLOTS, 1
-    )
-
-    def to_slots(values_all):
-        return (
-            jnp.einsum("kst,ktd->ksd", pick, values_all, preferred_element_type=f32)
-            .astype(bf16)
-            .reshape(4 * SLOTS, model_width)
-        )
-
-    def to_rows(slot_values):
-        return (
-            jnp.einsum(
-                "kst,ksd->ktd",
-                pick,
-                slot_values.astype(bf16).reshape(4, SLOTS, model_width),
-                preferred_element_type=f32,
-            )
-            .astype(bf16)
-            .reshape(8, rows, model_width)
-        )
-
-    dispatched = to_slots(rows_all)
-    slot_grad = to_slots(grads_all)
-    gate_act = dot(dispatched, gate_w)
-    up_act = dot(dispatched, up_w)
-    sigmoid_act = jax.nn.sigmoid(gate_act)
-    silu_act = gate_act * sigmoid_act
-    hidden = silu_act * up_act
-    hidden_gated = (hidden * slot_gate).astype(bf16)
-    mix_parts = to_rows(dot_nt(hidden_gated, down_w))
-    hidden_grad = dot(slot_grad, down_w)
-    gate_back_slots = jnp.sum(hidden * hidden_grad, axis=1).reshape(4, SLOTS)
-    gate_back_rows = jnp.sum(
-        jnp.where(hot_slots, gate_back_slots[:, :, None], 0.0), axis=1
-    ).reshape(8, 2, rows // 2)
-    hidden_grad = hidden_grad * slot_gate
-    gate_low = (hidden_grad * up_act * (sigmoid_act * (1.0 + gate_act * (1.0 - sigmoid_act)))).astype(
-        bf16
-    )
-    up_low = (hidden_grad * silu_act).astype(bf16)
-    grad_down = dot_tn(slot_grad, hidden_gated).astype(bf16)
-    grad_gate = dot_tn(dispatched, gate_low).astype(bf16)
-    grad_up = dot_tn(dispatched, up_low).astype(bf16)
-    back_parts = to_rows(dot_nt(gate_low, gate_w) + dot_nt(up_low, up_w))
-
-    mix_back, gate_back = column_sum(back_parts, gate_back_rows, 5)
-    mix_out, unused = column_sum(mix_parts, gate_back_rows, 6)
-    expert_sum = lax.psum_scatter(
-        jnp.stack([grad_gate, grad_up, grad_down]), ("x", "y"), scatter_dimension=1, tiled=True
-    )
+    gate_rows = jnp.sum(gate_weights[:, :, None] * hot_routes, axis=1).T
+
+    mix_parts, expert_grads, mix_back, gate_back = experts_of_column(
+        normed_mix, gate_rows[:, None, :], grads_all, slots.reshape(4, 2 * rows), expert_full
+    )
+    mix_out, unused = column_sum(mix_parts, gate_back.reshape(8, 2, rows // 2), 6)
+    expert_sum = lax.psum_scatter(expert_grads, ("x", "y"), scatter_dimension=1, tiled=True)
     block_out = exchange_halves((residual + mix_out).astype(bf16), l)
 
     gate_back = jnp.sum(hot_routes * gate_back.reshape(experts, rows).T[:, None, :], axis=-1)

time: 536 us -> 480 us (0.90)
  matrix products: 131 us -> 60.5 us
  Pallas kernels: 267 us -> 284 us
  other arithmetic: 52.2 us -> 41.5 us
  local copies, waits for them, and re-layouts: 61.3 us -> 69.5 us
    pallas_call x1, Pallas kernels: 35.1 us -> 93.1 us  [experts_of_column(): pl.pallas_call(experts_kernel, name='experts', out_shape=(jax.ShapeDtypeS...]
    pallas_call x2 -> x1, Pallas kernels: 83.3 us -> 41.9 us  [column_sum(): pl.pallas_call(column_sum_kernel, name='sum_over_experts', out_shape=(jax...]
    dot_general x4 -> x0, matrix products: 22.7 us -> none  [the longest x2 11.6 us: to_rows(): jnp.einsum('kst,ksd->ktd', pick, slot_values.astype(bf16).reshape(4, SLOT...]
    dot_general x12 -> x9, matrix products: 42.2 us -> 21.9 us  [dot(): return jnp.dot(a, b, preferred_element_type=f32)]
    dot_general x12 -> x9, matrix products: 44.4 us -> 26.7 us  [dot_nt(): lax.dot_general(a, b, (((1,), (1,)), ((), ())), preferred_element_type=f32)]
    dot_general x12 -> x9, matrix products: 21.3 us -> 11.9 us  [dot_tn(): lax.dot_general(a, b, (((0,), (0,)), ((), ())), preferred_element_type=f32)]
    convert_element_type x2 -> x0, other arithmetic: 6.57 us -> none  [the longest x1 5.71 us: body(): up_low = (hidden_grad * silu_act).astype(bf16)]
    unnamed x161 -> x143, local copies, waits for them, and re-layouts: 21.6 us -> 25.1 us
  transfers between devices with their start and end apart: 4 -> 4, of which waited for: 0 -> 0; matrix products, arithmetic and copies ran while one was open for 25% -> 27% of each run, Pallas kernels for 13% -> 7%
where the time goes in v3:
time: 480 us; the launch traced here: 472 us
  Pallas kernels  284 us (59%)
  local copies, waits for them, and re-layouts  69.5 us (14%)
  matrix products  60.5 us (13%)
  other arithmetic  41.5 us (9%)
  between operations  15.4 us (3%)
    pallas_call x1, Pallas kernels, experts_of_column(): pl.pallas_call(experts_kernel, name='experts', out_shape=(jax.ShapeDtypeS...  93.1 us
    pallas_call x1, Pallas kernels, return_gradients(): pl.pallas_call(functools.partial(return_kernel, part, misc_at), name='ret...  59.5 us
    pallas_call x1, Pallas kernels, gather_weights(): pl.pallas_call(functools.partial(weights_kernel, part), name='gather_weig...  55.2 us
    pallas_call x1, Pallas kernels, column_sum(): pl.pallas_call(column_sum_kernel, name='sum_over_experts', out_shape=(jax...  41.9 us
    dot_general x9, matrix products, dot_nt(): lax.dot_general(a, b, (((1,), (1,)), ((), ())), preferred_element_type=f32)  26.7 us
    unnamed x143, local copies, waits for them, and re-layouts  25.1 us
    dot_general x9, matrix products, dot(): return jnp.dot(a, b, preferred_element_type=f32)  21.9 us
    pallas_call x1, Pallas kernels, gather_along_z(): pl.pallas_call(along_z_kernel, name='gather_keys_values', out_shape=jax.S...  17.7 us
  transfers between devices with their start and end apart: 4, of which 0 were waited for; matrix products, arithmetic and copies ran while one was open for 27% of the time, Pallas kernels for 7%

profile of v3, /device:TPU:1, one launch (start us, length us, event | category | flops | bytes accessed | tf_op | source)
XLA Modules:
  0.0 471.7 jit_solution(6642382166157826145)
XLA Ops:
  17.2 55.2 %gather_weights.1 = (bf16[2,16,96,1920]{3,2,1,0:T(8,128)(2,1)S(1)}, bf16[3,96,768]{2,1,0:T(8,128)(2,1)}, bf16[8,256,1536]{2,1,0:T(8,128)(2,1)S(1)}, f32[8,1,256]{2,1,0:T(1,128)S(1)}) custom-call(bf16[32,1920]{1,0:T(8,128)(2,1)S(1)} %pad.24.attn_ref, bf16[8,3,32,384]{3,2,1,0:T(8,128)(2,1)S(1)} %fusion.53.expert_ref, ...), custom_call_target="tpu_custom_call" | custom-call | tf_op jit(solution)/shard_map/gather_weights/pallas_call | solution.py:387
  75.0 4.3 copy-done.3
  81.6 2.9 fusion.13
  85.2 3.0 fusion.12
  103.2 17.7 %gather_keys_values.1 = bf16[4,256,512]{2,1,0:T(8,128)(2,1)} custom-call(bf16[256,512]{1,0:T(8,128)(2,1)} %pad_maximum_fusion.4.block_ref), custom_call_target="tpu_custom_call" | custom-call | tf_op jit(solution)/shard_map/gather_keys_values/pallas_call | solution.py:431
  146.6 93.1 %experts.1 = (bf16[8,256,1536]{2,1,0:T(8,128)(2,1)}, bf16[3,1536,768]{2,1,0:T(8,128)(2,1)}, f32[256,1536]{1,0:T(8,128)}, f32[8,1,256]{2,1,0:T(1,128)}) custom-call(bf16[256,1536]{1,0:T(8,128)(2,1)} %copy-done.10, f32[8,1,256]{2,1,0:T(1,128)} %broadcast_in_dim.56.gate_ref, bf16[8,256,1536]{2,1,0:T(8,128)(2,1)} %copy-done.1, f32[4,1,512]{2,1,0:T(1,128)} %bitcast.239, ...), custom_call_target="tpu_custom_call" | custom-call | tf_op jit(solution)/shard_map/experts/pallas_call | solution.py:787
  240.6 2.7 multiply_reduce_fusion.2
  243.3 2.8 copy-done.2
  246.1 41.9 %sum_over_experts.1 = (f32[256,1536]{1,0:T(8,128)S(1)}, f32[8,2,128]{2,1,0:T(2,128)}) custom-call(bf16[8,256,1536]{2,1,0:T(8,128)(2,1)S(1)} %copy-done.2, f32[8,2,128]{2,1,0:T(2,128)S(1)} %bitcast.240), custom_call_target="tpu_custom_call" | custom-call | tf_op jit(solution)/shard_map/sum_over_experts/pallas_call | solution.py:898
  289.5 3.0 fusion.34
  298.9 4.3 multiply_reduce_fusion.1
  304.1 4.4 multiply_convert_fusion.1
  308.5 4.0 convolution_multiply_fusion.1
  314.9 2.8 fusion.36
  317.6 4.3 multiply_reduce_fusion
  322.6 4.4 multiply_convert_fusion
  327.0 3.1 fusion.37
  334.3 16.6 %sum_key_value_gradients.1 = f32[256,512]{1,0:T(8,128)} custom-call(bf16[4,256,512]{2,1,0:T(8,128)(2,1)} %pad_maximum_fusion.1.parts_ref), custom_call_target="tpu_custom_call" | custom-call | tf_op jit(solution)/shard_map/sum_key_value_gradients/pallas_call | solution.py:470
  350.9 2.9 convolution_multiply_fusion
  364.5 3.1 fusion.11
  367.6 3.4 fusion.26
  374.2 3.8 fusion.1
  378.0 10.5 %copy.119 = bf16[2,1536,1152]{2,1,0:T(8,128)(2,1)} copy(bf16[2,1536,1152]{1,2,0:T(8,128)(2,1)} %fusion.1) | data formatting | bytes 14155776 | tf_op jit(solution)/shard_map/concatenate | solution.py:1463
  401.4 59.5 %return_gradients.1 = (f32[24,1920]{1,0:T(8,128)S(1)}, f32[24,128]{1,0:T(8,128)S(1)}, bf16[8,3,32,384]{3,2,1,0:T(8,128)(2,1)S(1)}) custom-call(bf16[2,16,96,1152]{3,2,1,0:T(8,128)(2,1)} %bitcast.245, bf16[2,16,96,768]{3,2,1,0:T(8,128)(2,1)S(1)} %copy-done, bf16[8,3,32,384]{3,2,1,0:T(8,128)(2,1)S(1)} %bitcast.229), custom_call_target="tpu_custom_call" | custom-call | tf_op jit(solution)/shard_map/return_gradients/pallas_call | solution.py:1207
  (278 shorter events, 102.5 us)
Async XLA Ops:
  7.2 139.4 %all-gather.2.cloned.1.call-start = ((), (), s32[]{:S(2)}) async-start(), calls=%async_computation.1 | async-start | bytes 7520256 | tf_op jit(solution)/shard_map/all_gather | solution.py:1304
  12.5 68.2 %copy-start.18 = (bf16[1,512,1536]{2,1,0:T(8,128)(2,1)S(1)}, bf16[1,512,1536]{2,1,0:T(8,128)(2,1)}, u32[]{:S(2)}) copy-start(bf16[1,512,1536]{2,1,0:T(8,128)(2,1)} %param.14) | copy-start | bytes 4718596
  75.0 4.3 copy-start.3
  79.3 13.4 %copy-start.4 = (f32[8,1,256]{2,1,0:T(1,128)}, f32[8,1,256]{2,1,0:T(1,128)S(1)}, u32[]{:S(2)}) copy-start(f32[8,1,256]{2,1,0:T(1,128)S(1)} %get-tuple-element.26) | copy-start | bytes 24580
  79.4 318.4 %reduce-scatter.2.cloned.1.call-start = ((), (), s32[]{:S(2)}) async-start(), calls=%async_computation.2 | async-start | bytes 7520256 | tf_op jit(solution)/shard_map/reduce_scatter | solution.py:1388
  80.9 4.3 copy-start.52
  85.2 4.9 %copy-start.60 = (s32[1,1024]{1,0:T(1,128)S(1)}, s32[1,1024]{1,0:T(1,128)}, u32[]{:S(2)}) copy-start(s32[1,1024]{1,0:T(1,128)} %param.15) | copy-start | bytes 12292
  90.2 4.4 slice-start.4
  124.2 7.6 %copy-start.26 = (bf16[6,256,128]{2,1,0:T(8,128)(2,1)}, bf16[6,256,128]{2,1,0:T(8,128)(2,1)S(1)}, u32[]{:S(2)}) copy-start(bf16[6,256,128]{2,1,0:T(8,128)(2,1)S(1)} %copy.97) | copy-start | bytes 1179652
  240.6 47.4 %copy-start.50 = (bf16[256,8]{0,1:T(8,128)(2,1)}, bf16[256,8]{0,1:T(8,128)(2,1)S(1)}, u32[]{:S(2)}) copy-start(bf16[256,8]{0,1:T(8,128)(2,1)S(1)} %select_reduce_fusion) | copy-start | bytes 12292
  246.1 41.9 %copy-start.31 = (bf16[1,512,1536]{2,1,0:T(8,128)(2,1)S(1)}, bf16[1,512,1536]{2,1,0:T(8,128)(2,1)}, u32[]{:S(2)}) copy-start(bf16[1,512,1536]{2,1,0:T(8,128)(2,1)} %param.27) | copy-start | bytes 4718596
  289.5 5.5 %copy-start.15 = (f32[256,1536]{1,0:T(8,128)}, f32[256,1536]{1,0:T(8,128)S(1)}, u32[]{:S(2)}) copy-start(f32[256,1536]{1,0:T(8,128)S(1)} %get-tuple-element.81) | copy-start | bytes 4718596
  298.4 94.4 %collective-permute-start = (bf16[256,1536]{1,0:T(8,128)(2,1)}, bf16[256,1536]{1,0:T(8,128)(2,1)}, u32[]{:S(2)}, u32[]{:S(2)}) collective-permute-start(bf16[256,1536]{1,0:T(8,128)(2,1)} %get-tuple-element.88), channel_id=1, source_target_pairs={{0,1},{1,0},{2,3},{3,2},{4,5},{5,4},{6,7},{7,6},{8,9},{9,8},{10,11... | collective-permute-start | bytes 2359304 | tf_op jit(solution)/shard_map/ppermute | solution.py:1252
  298.9 4.5 slice-start.2
  298.9 5.2 %slice-start.3 = ((s8[6291456]{0:T(1024)(128)(4,1)}), s8[2097152]{0:T(1024)(128)(4,1)S(1)}, s32[]{:S(2)}) async-start(s8[6291456]{0:T(1024)(128)(4,1)} %bitcast.243), calls=%async_computation.6 | async-start | bytes 4194304
  308.5 6.4 %copy-start.9 = (bf16[1536,1024]{0,1:T(8,128)(2,1)S(1)}, bf16[1536,1024]{0,1:T(8,128)(2,1)}, u32[]{:S(2)}) copy-start(bf16[1536,1024]{0,1:T(8,128)(2,1)} %get-tuple-element.82) | copy-start | bytes 9437188
  317.6 4.3 slice-start
  317.6 4.9 %slice-start.1 = ((s8[6291456]{0:T(1024)(128)(4,1)}), s8[2097152]{0:T(1024)(128)(4,1)S(1)}, s32[]{:S(2)}) async-start(s8[6291456]{0:T(1024)(128)(4,1)} %bitcast.241), calls=%async_computation.4 | async-start | bytes 4194304
  332.1 18.7 %copy-start.8 = (bf16[1536,1024]{0,1:T(8,128)(2,1)S(1)}, bf16[1536,1024]{0,1:T(8,128)(2,1)}, u32[]{:S(2)}) copy-start(bf16[1536,1024]{0,1:T(8,128)(2,1)} %get-tuple-element.84) | copy-start | bytes 9437188
  353.7 4.3 copy-start.17
  353.7 4.3 copy-start.22
  353.7 8.7 %copy-start.13 = (f32[6,256,128]{1,2,0:T(8,128)S(1)}, f32[6,256,128]{1,2,0:T(8,128)}, u32[]{:S(2)}) copy-start(f32[6,256,128]{1,2,0:T(8,128)} %copy.104) | copy-start | bytes 2359300
  371.6 24.0 %collective-permute-start.1 = (bf16[256,1536]{1,0:T(8,128)(2,1)S(1)}, bf16[256,1536]{1,0:T(8,128)(2,1)S(1)}, u32[]{:S(2)}, u32[]{:S(2)}) collective-permute-start(bf16[256,1536]{1,0:T(8,128)(2,1)S(1)} %fusion.30), channel_id=1, source_target_pairs={{0,1},{1,0},{2,3},{3,2},{4,5},{5,4},{6,7},{7,6},{8,9},{9,8},{10,11... | collective-permute-start | bytes 2359304 | tf_op jit(solution)/shard_map/ppermute | solution.py:1252
  378.0 10.5 %copy-start.12 = (bf16[1536,256]{1,0:T(8,128)(2,1)S(1)}, bf16[1536,256]{1,0:T(8,128)(2,1)}, u32[]{:S(2)}) copy-start(bf16[1536,256]{1,0:T(8,128)(2,1)} %copy.120) | copy-start | bytes 2359300
  (49 other events, 116.7 us)
Sparse Core Ops, SparseCore 0:
  79.5 63.7 all-gather.1
  295.1 78.6 reduce-scatter.1

commit v4 on v3

--- a/solution.py
+++ b/solution.py
@@ -29,21 +29,8 @@
     half_dim = HEAD_SIZE // 2
     frequency = ROPE_BASE ** (-jnp.arange(half_dim, dtype=f32) * (2.0 / HEAD_SIZE))
     angles = positions.astype(f32)[:, None] * frequency[None, :]
-    angles = jnp.concatenate([angles, angles], axis=1)
-    return (jnp.cos(angles)[:, None, :], jnp.sin(angles)[:, None, :])
-
-
-def rotary_embed(value_rows, cosine_table, sine_table):
-    half_dim = HEAD_SIZE // 2
-    turned = jnp.concatenate([-value_rows[..., half_dim:], value_rows[..., :half_dim]], axis=-1)
-    return value_rows * cosine_table + turned * sine_table
-
-
-def rotate_back(grad_vals, cosine_table, sine_table):
-    half_dim = HEAD_SIZE // 2
-    scaled = grad_vals * sine_table
-    turned = jnp.concatenate([scaled[..., half_dim:], -scaled[..., :half_dim]], axis=-1)
-    return grad_vals * cosine_table + turned
+    cosine, sine = jnp.cos(angles), jnp.sin(angles)
+    return jnp.concatenate([cosine, cosine], axis=1), jnp.concatenate([-sine, sine], axis=1)
 
 
 def place():
@@ -412,74 +399,564 @@
     )(attn_block, expert_pieces, rows, slots)
 
 
-def along_z_kernel(block_ref, out_ref, s_sem, r_sem, own):
+def ref_dot(a, b):
+    return jnp.dot(a, b, preferred_element_type=f32)
+
+
+def ref_dot_nt(a, b):
+    return lax.dot_general(a, b, (((1,), (1,)), ((), ())), preferred_element_type=f32)
+
+
+def ref_dot_tn(a, b):
+    return lax.dot_general(a, b, (((0,), (0,)), ((), ())), preferred_element_type=f32)
+
+
+def at(i, size):
+    return pl.ds(pl.multiple_of(i * size, size), size)
+
+
+def gain_rows(misc):
+    pick = lax.broadcasted_iota(jnp.int32, (16, MISC), 0)
+    pick = (pick == lax.broadcasted_iota(jnp.int32, (16, MISC), 1)).astype(f32).astype(bf16)
+    return ref_dot_nt(pick, misc)
+
+
+def turn(values, cosine, sine):
+    return values * cosine + pltpu.roll(values, HEAD_SIZE // 2, 1) * sine
+
+
+def turn_back(values, cosine, sine):
+    return values * cosine - pltpu.roll(values, HEAD_SIZE // 2, 1) * sine
+
+
+def fill_bias(bias, seg_column, seg_row, first):
+    keys, queries = bias.shape
+    chunk = 256
+
+    def fill(i, carry):
+        here = at(i, chunk)
+        key = lax.broadcasted_iota(jnp.int32, (chunk, queries), 0) + i * chunk
+        query = lax.broadcasted_iota(jnp.int32, (chunk, queries), 1) + first
+        seen = (seg_column[here, :] == seg_row[...]) & (key <= query)
+        bias[here, :] = jnp.where(seen, 0.0, NEG_FILL)
+        return carry
+
+    lax.fori_loop(0, keys // chunk, fill, 0)
+
+
+def attention_kernel(
+    x_ref,
+    w_ref,
+    cos_ref,
+    sin_ref,
+    seg_column,
+    seg_row,
+    named_ref,
+    a_out,
+    q_out,
+    kv_out,
+    o_out,
+    lse_out,
+    h1_out,
+    b_out,
+    gates_out,
+    w,
+    bias,
+    value_turned,
+    s_sem,
+    r_sem,
+    w_sem,
+):
     c, h, l = place()
     z = h * 2 + l
-    greet(ALONG_Z)
-    own_copy = pltpu.make_async_copy(block_ref, out_ref.at[z], own)
-    own_copy.start()
-    copies = [
-        send(block_ref, out_ref.at[z], s_sem.at[i], r_sem.at[i], column_peer(*step))
-        for i, step in enumerate(ALONG_Z)
-    ]
-    own_copy.wait()
-    for copy in copies:
-        copy.wait()
-
-
-def gather_along_z(block):
+    rows, width = x_ref.shape
+    q_half = w.shape[2] // 2 - (HEAD_SIZE * 2 + MISC) // 2
+    kv_at, misc_at, out_at = q_half, q_half + 2 * HEAD_SIZE, q_half + 2 * HEAD_SIZE + MISC
+    pieces = [(kv_at, out_at - kv_at), (0, q_half), (out_at, q_half)]
+    loads = []
+    for i, (start, size) in enumerate(pieces):
+        columns = pl.ds(start, size)
+        copy = pltpu.make_async_copy(
+            w_ref.at[:, :, columns], w.at[:, :, columns], w_sem.at[i]
+        )
+        copy.start()
+        loads.append(copy)
+    barrier = pltpu.get_barrier_semaphore()
+    for step in ALONG_Z:
+        pl.semaphore_signal(barrier, inc=1, device_id=column_peer(*step), device_id_type=MESH)
+    pl.semaphore_wait(barrier, len(ALONG_Z))
+    lanes = Lanes(s_sem, r_sem)
+    scale = HEAD_SIZE ** (-0.5)
+    fill_bias(bias, seg_column, seg_row, z * rows)
+    loads[0].wait()
+    gains = gain_rows(w[0, :, misc_at:out_at])
+    chunk = 32
+
+    def norm(i, carry):
+        here = at(i, chunk)
+        x = x_ref[here, :].astype(f32)
+        inverse = lax.rsqrt(jnp.mean(x * x, axis=1, keepdims=True) + EPS)
+        a_out[here, :] = (x * inverse * gains[8:9, :]).astype(bf16)
+        return carry
+
+    lax.fori_loop(0, rows // chunk, norm, 0)
+    cosine, sine = cos_ref[...], sin_ref[...]
+    head = pl.ds(0, HEAD_SIZE)
+    sends = []
+    for i in range(2):
+        kv = ref_dot(a_out[...], w[i, :, kv_at:misc_at])
+        kv_out[z, :, i * 128 : (i + 1) * 128] = turn(kv[:, :128], cosine, sine).astype(bf16)
+        kv_out[z, :, (2 + i) * 128 : (3 + i) * 128] = kv[:, 128:].astype(bf16)
+    for step in ALONG_Z:
+        sends.append(lanes.send(kv_out.at[z], kv_out.at[z], column_peer(*step)))
+    loads[1].wait()
+    for i in range(2):
+
+        def project(j, carry, i=i):
+            columns = at(j, 256)
+            q = ref_dot(a_out[...], w[i, :, columns])
+            q_out[i * GROUP + 2 * j] = turn(q[:, :128], cosine, sine).astype(bf16)
+            q_out[i * GROUP + 2 * j + 1] = turn(q[:, 128:], cosine, sine).astype(bf16)
+            return carry
+
+        lax.fori_loop(0, q_half // 256, project, 0)
+    for copy in sends:
+        copy.wait_recv()
+    keys_count = 4 * rows
+    for i in range(2):
+        values = kv_out[:, :, (2 + i) * 128 : (3 + i) * 128].reshape(keys_count, HEAD_SIZE)
+        value_turned[...] = values.T
+
+        def attend(j, carry, i=i):
+            keys = kv_out[:, :, i * 128 : (i + 1) * 128].reshape(keys_count, HEAD_SIZE)
+            scores = ref_dot_nt(keys, q_out[i * GROUP + j]) * scale + bias[...]
+            peak = jnp.max(scores, axis=0, keepdims=True)
+            expo = jnp.exp(scores - peak)
+            total = jnp.sum(expo, axis=0, keepdims=True)
+            weights = (expo * (1.0 / total)).astype(bf16)
+            mixed = ref_dot(value_turned[...], weights)
+            o_out[:, at(i * GROUP + j, HEAD_SIZE)] = mixed.T.astype(bf16)
+            lse_out[i * GROUP + j] = peak + jnp.log(total)
+            return carry
+
+        lax.fori_loop(0, GROUP, attend, 0)
+    loads[2].wait()
+
+    def leave(j, carry):
+        here = at(j, 512)
+        u = ref_dot_nt(o_out[:, :q_half], w[0, here, out_at:])
+        u = u + ref_dot_nt(o_out[:, q_half:], w[1, here, out_at:])
+        h1_out[:, here] = x_ref[:, here].astype(f32) + u
+        return carry
+
+    lax.fori_loop(0, width // 512, leave, 0)
+
+    def second(i, carry):
+        here = at(i, chunk)
+        h1 = h1_out[here, :]
+        inverse = lax.rsqrt(jnp.mean(h1 * h1, axis=1, keepdims=True) + EPS)
+        b_out[here, :] = (h1 * inverse * gains[9:10, :]).astype(bf16)
+        return carry
+
+    lax.fori_loop(0, rows // chunk, second, 0)
+    logits = ref_dot(b_out[...], w[0, :, misc_at:out_at]).T[:8]
+    named = named_ref[...] > 0
+    masked = jnp.where(named, logits, NEG_FILL)
+    expo = jnp.where(named, jnp.exp(masked - jnp.max(masked, axis=0, keepdims=True)), 0.0)
+    gates = expo / jnp.sum(expo, axis=0, keepdims=True)
+    for e in range(8):
+        gates_out[e] = gates[e : e + 1]
+    for copy in sends:
+        copy.wait_send()
+
+
+def attention(x, w_attn, cosine, sine, seg_column, seg_row, named):
+    rows, width = x.shape
+    keys = 4 * rows
+    sds = jax.ShapeDtypeStruct
     return pl.pallas_call(
-        along_z_kernel,
-        name="gather_keys_values",
-        out_shape=jax.ShapeDtypeStruct((4,) + block.shape, block.dtype),
-        in_specs=[VMEM],
-        out_specs=VMEM,
+        attention_kernel,
+        name="attention",
+        out_shape=(
+            sds((rows, width), bf16),
+            sds((QUERY_HEADS, rows, HEAD_SIZE), bf16),
+            sds((4, rows, 4 * HEAD_SIZE), bf16),
+            sds((rows, QUERY_HEADS * HEAD_SIZE), bf16),
+            sds((QUERY_HEADS, 1, rows), f32),
+            sds((rows, width), f32),
+            sds((rows, width), bf16),
+            sds((8, 1, rows), f32),
+        ),
+        in_specs=[VMEM, ANY] + [VMEM] * 5,
+        out_specs=(VMEM,) * 8,
         scratch_shapes=[
+            pltpu.VMEM(w_attn.shape, bf16),
+            pltpu.VMEM((keys, rows), f32),
+            pltpu.VMEM((HEAD_SIZE, keys), bf16),
             pltpu.SemaphoreType.DMA((3,)),
-            pltpu.SemaphoreType.DMA((3,)),
-            pltpu.SemaphoreType.DMA(()),
-        ],
-        compiler_params=pltpu.CompilerParams(collective_id=2, has_side_effects=True),
-    )(block)
-
-
-def sum_along_z_kernel(parts_ref, out_ref, held, s_sem, r_sem):
-    c, h, l = place()
-    z = h * 2 + l
-    greet(ALONG_Z)
-    copies = [
-        send(
-            parts_ref.at[lax.rem(z + step[1], 4)],
-            held.at[i],
-            s_sem.at[i],
-            r_sem.at[i],
-            column_peer(*step),
-        )
-        for i, step in enumerate(ALONG_Z)
-    ]
-    for copy in copies:
-        copy.wait()
-    total = parts_ref[z].astype(f32)
-    for i in range(3):
-        total = total + held[i].astype(f32)
-    out_ref[...] = total
-
-
-def sum_along_z(parts):
-    shape = parts.shape[1:]
-    return pl.pallas_call(
-        sum_along_z_kernel,
-        name="sum_key_value_gradients",
-        out_shape=jax.ShapeDtypeStruct(shape, f32),
-        in_specs=[VMEM],
-        out_specs=VMEM,
-        scratch_shapes=[
-            pltpu.VMEM((3,) + shape, parts.dtype),
             pltpu.SemaphoreType.DMA((3,)),
             pltpu.SemaphoreType.DMA((3,)),
         ],
-        compiler_params=pltpu.CompilerParams(collective_id=3, has_side_effects=True),
-    )(parts)
+        compiler_params=pltpu.CompilerParams(
+            collective_id=2, has_side_effects=True, vmem_limit_bytes=56 * 2**20
+        ),
+    )(x, w_attn, cosine, sine, seg_column, seg_row, named)
+
+
+def attention_back_kernel(
+    back_ref,
+    gate_back_ref,
+    gates_ref,
+    b_ref,
+    h1_ref,
+    x_ref,
+    g_ref,
+    a_ref,
+    o_ref,
+    q_ref,
+    kv_ref,
+    lse_ref,
+    cos_ref,
+    sin_ref,
+    seg_column,
+    seg_row,
+    w_ref,
+    parts_ref,
+    grad_in,
+    grad_out,
+    tokens_out,
+    block_out,
+    w,
+    bias,
+    key_turned,
+    dh1,
+    da,
+    du,
+    do,
+    back_rows,
+    key_sum,
+    value_sum,
+    kv_send,
+    kv_held,
+    stage_in,
+    stage_out,
+    misc_grad,
+    parts,
+    near,
+    far,
+    nearest,
+    s_sem,
+    r_sem,
+    w_sem,
+    stage_in_sem,
+    stage_out_sem,
+    own,
+):
+    c, h, l = place()
+    z = h * 2 + l
+    rows, width = x_ref.shape
+    q_half = w.shape[2] // 2 - (HEAD_SIZE * 2 + MISC) // 2
+    kv_at, misc_at, out_at = q_half, q_half + 2 * HEAD_SIZE, q_half + 2 * HEAD_SIZE + MISC
+    pieces = [(misc_at, w.shape[2] - misc_at), (0, misc_at)]
+    loads = []
+    for i, (start, size) in enumerate(pieces):
+        columns = pl.ds(start, size)
+        copy = pltpu.make_async_copy(
+            w_ref.at[:, :, columns], w.at[:, :, columns], w_sem.at[i]
+        )
+        copy.start()
+        loads.append(copy)
+    parts_load = pltpu.make_async_copy(parts_ref.at[pl.ds(c * 4, 4)], parts, own.at[0])
+    parts_load.start()
+    barrier = pltpu.get_barrier_semaphore()
+    pl.semaphore_wait(barrier, greet_column(barrier))
+    lanes = Lanes(s_sem, r_sem)
+    places = {
+        "own": z,
+        "partner": h * 2 + 1 - l,
+        "cross": (1 - h) * 2 + 1 - l,
+        "far": (1 - h) * 2 + l,
+    }
+    near_copies = {
+        which: lanes.send(
+            parts_ref.at[(1 - c) * 4 + places[which]], near.at[places[which]], other_core()
+        )
+        for which in ("far", "cross", "partner", "own")
+    }
+    scale = HEAD_SIZE ** (-0.5)
+    fill_bias(bias, seg_column, seg_row, z * rows)
+
+    def add_near(which):
+        near_copies[which].wait_recv()
+        k = places[which]
+
+        def add(i, carry):
+            here = at(i, 64)
+            parts[k, here] = parts[k, here] + near[k, here]
+            return carry
+
+        lax.fori_loop(0, rows // 64, add, 0)
+
+    half = rows // 2
+    first, second = pl.ds(0, half), pl.ds(half, half)
+
+    def part_at(which, some):
+        return parts.at[places[which], some]
+
+    parts_load.wait()
+    add_near("far")
+    far_partner = lanes.send(part_at("far", first), far.at[0], partner())
+    far_cross = lanes.send(part_at("far", second), far.at[1], cross())
+    add_near("cross")
+    add_near("partner")
+    early_cross = lanes.send(part_at("cross", second), nearest.at[1, second], cross())
+    early_partner = lanes.send(part_at("partner", first), nearest.at[0, first], partner())
+    add_near("own")
+
+    loads[0].wait()
+    misc = w[0, :, misc_at:out_at]
+    gains = gain_rows(misc)
+    gates = jnp.concatenate([gates_ref[e] for e in range(8)], axis=0)
+    gate_back = jnp.concatenate([gate_back_ref[e] for e in range(8)], axis=0)
+    mean = jnp.sum(gates * gate_back, axis=0, keepdims=True)
+    logit_grad = gates * (gate_back - mean)
+    logit_grad = jnp.concatenate(
+        [logit_grad, jnp.zeros((MISC - 8, rows), f32)], axis=0
+    ).T.astype(bf16)
+    chunk = 32
+
+    def norm_back(i, carry):
+        mix_sum = carry
+        here = at(i, chunk)
+        h1 = h1_ref[here, :]
+        inverse = lax.rsqrt(jnp.mean(h1 * h1, axis=1, keepdims=True) + EPS)
+        db = back_ref[here, :] + dh1[here, :]
+        mix_sum = mix_sum + jnp.sum(db * h1 * inverse, axis=0, keepdims=True)
+        dz = db * gains[9:10, :]
+        mean = jnp.mean(dz * h1, axis=1, keepdims=True)
+        value = g_ref[here, :].astype(f32) + inverse * dz - h1 * (inverse * inverse * inverse * mean)
+        dh1[here, :] = value
+        du[here, :] = value.astype(bf16)
+        return mix_sum
+
+    dh1[...] = ref_dot_nt(logit_grad, misc)
+    mix_sum = lax.fori_loop(0, rows // chunk, norm_back, jnp.zeros((1, width), f32))
+    misc_grad[...] = ref_dot_tn(b_ref[...], logit_grad)
+
+    def project(i, carry):
+        columns = at(i, 256)
+        for g in range(2):
+            do[g, :, columns] = ref_dot(
+                du[...], w[g, :, pl.ds(pl.multiple_of(out_at + i * 256, 128), 256)]
+            ).astype(bf16)
+        return carry
+
+    lax.fori_loop(0, q_half // 256, project, 0)
+
+    def stage_out_copy(g, i, slot):
+        return pltpu.make_async_copy(
+            stage_out.at[slot], grad_out.at[g, at(i, 256)], stage_out_sem.at[slot]
+        )
+
+    for g in range(2):
+
+        def out_grad(i, carry, g=g):
+            slot = lax.rem(i, 2)
+
+            @pl.when(i >= 2)
+            def _():
+                stage_out_copy(g, i - 2, slot).wait()
+
+            stage_out[slot] = ref_dot_tn(
+                du[:, at(i, 256)], o_ref[:, g * q_half : (g + 1) * q_half]
+            ).astype(bf16)
+            stage_out_copy(g, i, slot).start()
+            return carry
+
+        lax.fori_loop(0, width // 256, out_grad, 0)
+        for i in range(2):
+            stage_out_copy(g, width // 256 - 2 + i, i).wait()
+
+    far_partner.wait_recv()
+    mine = part_at("cross", first)
+    mine[...] = mine[...] + far[0]
+    late_cross = lanes.send(mine, nearest.at[1, first], cross())
+    far_cross.wait_recv()
+    mine = part_at("partner", second)
+    mine[...] = mine[...] + far[1]
+    late_partner = lanes.send(mine, nearest.at[0, second], partner())
+
+    keys_count = 4 * rows
+    kv_sends = []
+    cosine, sine = cos_ref[...], sin_ref[...]
+    for g in range(2):
+        key_turned[...] = (
+            kv_ref[:, :, g * 128 : (g + 1) * 128].reshape(keys_count, HEAD_SIZE).T
+        )
+        key_sum[...] = jnp.zeros_like(key_sum)
+        value_sum[...] = jnp.zeros_like(value_sum)
+
+        def head_back(j, carry, g=g):
+            columns = at(j, HEAD_SIZE)
+            keys = kv_ref[:, :, g * 128 : (g + 1) * 128].reshape(keys_count, HEAD_SIZE)
+            values = kv_ref[:, :, (2 + g) * 128 : (3 + g) * 128].reshape(keys_count, HEAD_SIZE)
+            query = q_ref[g * GROUP + j]
+            out_back = do[g, :, columns]
+            scores = ref_dot_nt(keys, query) * scale + bias[...]
+            prob = jnp.exp(scores - lse_ref[g * GROUP + j])
+            prob_back = ref_dot_nt(values, out_back)
+            value_sum[...] += ref_dot(prob.astype(bf16), out_back)
+            row_dot = jnp.sum(prob * prob_back, axis=0, keepdims=True)
+            score_back = (prob * (prob_back - row_dot)).astype(bf16)
+            key_sum[...] += ref_dot(score_back, query)
+            query_back = (ref_dot(key_turned[...], score_back) * scale).T
+            back_rows[g, :, columns] = turn_back(query_back, cosine, sine).astype(bf16)
+            return carry
+
+        lax.fori_loop(0, GROUP, head_back, 0)
+        kv_send[g, :, :, :128] = (key_sum[...] * scale).astype(bf16).reshape(4, rows, 128)
+        kv_send[g, :, :, 128:] = value_sum[...].astype(bf16).reshape(4, rows, 128)
+        for i, step in enumerate(ALONG_Z):
+            to = lax.rem(z + step[1], 4)
+            kv_sends.append(lanes.send(kv_send.at[g, to], kv_held.at[g, i], column_peer(*step)))
+
+    for copy in (early_partner, early_cross, late_cross, late_partner):
+        copy.wait_recv()
+
+    def total(i, carry):
+        here = at(i, 64)
+        value = parts[z, here].astype(f32)
+        value = value + nearest[0, here].astype(f32) + nearest[1, here].astype(f32)
+        block_out[l, here] = (h1_ref[here, :] + value).astype(bf16)
+        return carry
+
+    lax.fori_loop(0, rows // 64, total, 0)
+    block_send = lanes.send(block_out.at[l], block_out.at[l], partner())
+    loads[1].wait()
+    for copy in kv_sends:
+        copy.wait_recv()
+    for g in range(2):
+        own_part = kv_send[g, z].astype(f32)
+        for i in range(3):
+            own_part = own_part + kv_held[g, i].astype(f32)
+        back_rows[g, :, q_half : q_half + 128] = turn_back(
+            own_part[:, :128], cosine, sine
+        ).astype(bf16)
+        back_rows[g, :, q_half + 128 :] = own_part[:, 128:].astype(bf16)
+
+    def input_back(i, carry):
+        here = at(i, 512)
+        value = ref_dot_nt(back_rows[0], w[0, here, :misc_at])
+        da[:, here] = value + ref_dot_nt(back_rows[1], w[1, here, :misc_at])
+        return carry
+
+    lax.fori_loop(0, width // 512, input_back, 0)
+
+    def first_back(i, carry):
+        here = at(i, chunk)
+        x = x_ref[here, :].astype(f32)
+        inverse = lax.rsqrt(jnp.mean(x * x, axis=1, keepdims=True) + EPS)
+        back = da[here, :]
+        carry = carry + jnp.sum(back * x * inverse, axis=0, keepdims=True)
+        dz = back * gains[8:9, :]
+        mean = jnp.mean(dz * x, axis=1, keepdims=True)
+        value = dh1[here, :] + inverse * dz - x * (inverse * inverse * inverse * mean)
+        tokens_out[here, :] = value.astype(bf16)
+        return carry
+
+    attn_sum = lax.fori_loop(0, rows // chunk, first_back, jnp.zeros((1, width), f32))
+    number = lax.broadcasted_iota(jnp.int32, (MISC, width), 0)
+    gain_grads = jnp.where(number == 8, attn_sum, jnp.where(number == 9, mix_sum, 0.0))
+    misc_grad[...] += gain_grads.T
+
+    def stage_in_copy(g, i, slot):
+        return pltpu.make_async_copy(
+            stage_in.at[slot], grad_in.at[g, at(i, 256)], stage_in_sem.at[slot]
+        )
+
+    for g in range(2):
+
+        def in_grad(i, carry, g=g):
+            slot = lax.rem(i, 2)
+            here = at(i, 256)
+
+            @pl.when(i >= 2)
+            def _():
+                stage_in_copy(g, i - 2, slot).wait()
+
+            stage_in[slot, :, :misc_at] = ref_dot_tn(a_ref[:, here], back_rows[g]).astype(bf16)
+            if g == 0:
+                stage_in[slot, :, misc_at:] = misc_grad[here, :].astype(bf16)
+            else:
+                stage_in[slot, :, misc_at:] = jnp.zeros((256, MISC), bf16)
+            stage_in_copy(g, i, slot).start()
+            return carry
+
+        lax.fori_loop(0, width // 256, in_grad, 0)
+        for i in range(2):
+            stage_in_copy(g, width // 256 - 2 + i, i).wait()
+    block_send.wait()
+    for copy in kv_sends:
+        copy.wait_send()
+    for copy in near_copies.values():
+        copy.wait_send()
+    for copy in (early_partner, early_cross, late_cross, late_partner, far_partner, far_cross):
+        copy.wait_send()
+
+
+def attention_back(
+    back, gate_back, gates, b, h1, x, g, a, o, q, kv, lse, cosine, sine, seg_column, seg_row, w_attn, parts
+):
+    rows, width = x.shape
+    keys = 4 * rows
+    q_half = o.shape[1] // 2
+    qkv = q_half + 2 * HEAD_SIZE
+    sds = jax.ShapeDtypeStruct
+    return pl.pallas_call(
+        attention_back_kernel,
+        name="attention_back",
+        out_shape=(
+            sds((2, width, qkv + MISC), bf16),
+            sds((2, width, q_half), bf16),
+            sds((rows, width), bf16),
+            sds((2, rows, width), bf16),
+        ),
+        in_specs=[VMEM] * 16 + [ANY, ANY],
+        out_specs=(ANY, ANY, VMEM, VMEM),
+        scratch_shapes=[
+            pltpu.VMEM(w_attn.shape, bf16),
+            pltpu.VMEM((keys, rows), f32),
+            pltpu.VMEM((HEAD_SIZE, keys), bf16),
+            pltpu.VMEM((rows, width), f32),
+            pltpu.VMEM((rows, width), f32),
+            pltpu.VMEM((rows, width), bf16),
+            pltpu.VMEM((2, rows, q_half), bf16),
+            pltpu.VMEM((2, rows, qkv), bf16),
+            pltpu.VMEM((keys, HEAD_SIZE), f32),
+            pltpu.VMEM((keys, HEAD_SIZE), f32),
+            pltpu.VMEM((2, 4, rows, 2 * HEAD_SIZE), bf16),
+            pltpu.VMEM((2, 3, rows, 2 * HEAD_SIZE), bf16),
+            pltpu.VMEM((2, 256, qkv + MISC), bf16),
+            pltpu.VMEM((2, 256, q_half), bf16),
+            pltpu.VMEM((width, MISC), f32),
+            pltpu.VMEM((4, rows, width), bf16),
+            pltpu.VMEM((4, rows, width), bf16),
+            pltpu.VMEM((2, rows // 2, width), bf16),
+            pltpu.VMEM((2, rows, width), bf16),
+        ]
+        + lanes_scratch(24)
+        + [
+            pltpu.SemaphoreType.DMA((2,)),
+            pltpu.SemaphoreType.DMA((2,)),
+            pltpu.SemaphoreType.DMA((2,)),
+            pltpu.SemaphoreType.DMA((1,)),
+        ],
+        compiler_params=pltpu.CompilerParams(
+            collective_id=3, has_side_effects=True, vmem_limit_bytes=56 * 2**20
+        ),
+    )(
+        back, gate_back, gates, b, h1, x, g, a, o, q, kv, lse, cosine, sine, seg_column, seg_row, w_attn, parts
+    )
 
 
 def experts_kernel(
@@ -564,9 +1041,6 @@
     wide = 512
     narrow = 256
 
-    def at(i, size):
-        return pl.ds(pl.multiple_of(i * size, size), size)
-
     local[0].wait()
     local[1].wait()
 
@@ -767,18 +1241,6 @@
     for stage, k in ((0, (1 - c) * 2 + 1 - h), (1, c * 2 + 1 - h)):
         stage_copy(k, stage).wait()
     ring.drain()
-
-
-def ref_dot(a, b):
-    return jnp.dot(a, b, preferred_element_type=f32)
-
-
-def ref_dot_nt(a, b):
-    return lax.dot_general(a, b, (((1,), (1,)), ((), ())), preferred_element_type=f32)
-
-
-def ref_dot_tn(a, b):
-    return lax.dot_general(a, b, (((0,), (0,)), ((), ())), preferred_element_type=f32)
 
 
 def experts_of_column(rows, gates, grads_all, slots, weights):
@@ -827,101 +1289,6 @@
     )(rows, gates, grads_all, slots[:, None, :], slots[:, :, None], weights)
 
 
-def column_sum_kernel(
-    parts_ref, small_ref, out_ref, small_out, near, chip, far, cs, cr, zs, zr, ss, sr, own
-):
-    c, h, l = place()
-    z = h * 2 + l
-    me = c * 4 + z
-    greet(COLUMN)
-    other = column_peer(1, 0)
-    order = [2, 1, 3, 0]
-    near_copies = [
-        send(
-            parts_ref.at[(1 - c) * 4 + lax.rem(z + step, 4)],
-            near.at[i],
-            cs.at[i],
-            cr.at[i],
-            other,
-        )
-        for i, step in enumerate(order)
-    ]
-    own_copy = pltpu.make_async_copy(small_ref.at[me], small_out.at[me], own)
-    own_copy.start()
-    small_copies = []
-    for i, step in enumerate(COLUMN):
-        peer = column_peer(*step)
-        to = (peer["c"] * 2 + peer["h"]) * 2 + peer["l"]
-        small_copies.append(send(small_ref.at[to], small_out.at[me], ss.at[i], sr.at[i], peer))
-    rows = parts_ref.shape[1]
-    chunk = 32
-    far_copies = []
-    for i, step in enumerate(order):
-        near_copies[i].wait_recv()
-        mine = c * 4 + lax.rem(z + step, 4)
-
-        def add(k, carry, i=i, mine=mine, step=step):
-            here = pl.ds(pl.multiple_of(k * chunk, chunk), chunk)
-            total = parts_ref[mine, here, :].astype(f32) + near[i, here, :].astype(f32)
-            if step == 0:
-                out_ref[here, :] = total
-            else:
-                chip[i, here, :] = total.astype(chip.dtype)
-            return carry
-
-        lax.fori_loop(0, rows // chunk, add, 0)
-        if step:
-            far_copies.append(
-                send(chip.at[i], far.at[i], zs.at[i], zr.at[i], column_peer(0, step))
-            )
-    for copy in far_copies:
-        copy.wait()
-
-    def finish(k, carry):
-        here = pl.ds(pl.multiple_of(k * chunk, chunk), chunk)
-        total = out_ref[here, :]
-        for i in range(3):
-            total = total + far[i, here, :].astype(f32)
-        out_ref[here, :] = total
-        return carry
-
-    lax.fori_loop(0, rows // chunk, finish, 0)
-    for copy in near_copies:
-        copy.wait_send()
-    own_copy.wait()
-    for copy in small_copies:
-        copy.wait()
-
-
-def column_sum(parts, small, number):
-    rows, width = parts.shape[1:]
-    return pl.pallas_call(
-        column_sum_kernel,
-        name="sum_over_experts",
-        out_shape=(
-            jax.ShapeDtypeStruct((rows, width), f32),
-            jax.ShapeDtypeStruct(small.shape, small.dtype),
-        ),
-        in_specs=[VMEM, VMEM],
-        out_specs=(VMEM, VMEM),
-        scratch_shapes=[
-            pltpu.VMEM((4, rows, width), parts.dtype),
-            pltpu.VMEM((3, rows, width), parts.dtype),
-            pltpu.VMEM((3, rows, width), parts.dtype),
-            pltpu.SemaphoreType.DMA((4,)),
-            pltpu.SemaphoreType.DMA((4,)),
-            pltpu.SemaphoreType.DMA((3,)),
-            pltpu.SemaphoreType.DMA((3,)),
-            pltpu.SemaphoreType.DMA((7,)),
-            pltpu.SemaphoreType.DMA((7,)),
-            pltpu.SemaphoreType.DMA(()),
-        ],
-        compiler_params=pltpu.CompilerParams(
-            collective_id=number, has_side_effects=True, vmem_limit_bytes=40 * 2**20
-        ),
-    )(parts, small)
-
-
 class ChipSum:
     def __init__(self, lanes, chip, low, rows, p, q, near_p, rest_p, near_q):
         self.lanes, self.chip = lanes, chip
@@ -1030,9 +1397,11 @@
     in_ref,
     out_ref,
     expert_ref,
+    tokens_ref,
     grads_out,
     misc_out,
     expert_out,
+    tokens_out,
     near,
     near_p0,
     rest_p0,
@@ -1087,7 +1456,9 @@
                 ]
     own_copy = pltpu.make_async_copy(expert_ref.at[me], expert_out.at[me], own.at[0])
     own_copy.start()
-    expert_copies = []
+    own_tokens = pltpu.make_async_copy(tokens_ref, tokens_out.at[l], own.at[1])
+    own_tokens.start()
+    expert_copies = [lanes.send(tokens_ref, tokens_out.at[l], partner())]
     for step in COLUMN:
         peer = column_peer(*step)
         to = (peer["c"] * 2 + peer["h"]) * 2 + peer["l"]
@@ -1191,11 +1562,12 @@
     for each in sums:
         each.drain()
     own_copy.wait()
+    own_tokens.wait()
     for copy in expert_copies:
         copy.wait()
 
 
-def return_gradients(grad_in, grad_out, expert_pieces, part, misc_at):
+def return_gradients(grad_in, grad_out, expert_pieces, tokens, part, misc_at):
     in_width, out_width = grad_in.shape[3], grad_out.shape[3]
     width, rows = in_width + out_width, grad_in.shape[2]
     half = rows // 2
@@ -1211,9 +1583,10 @@
             jax.ShapeDtypeStruct((part, width), f32),
             jax.ShapeDtypeStruct((part, MISC), f32),
             jax.ShapeDtypeStruct(expert_pieces.shape, expert_pieces.dtype),
+            jax.ShapeDtypeStruct((2,) + tokens.shape, tokens.dtype),
         ),
-        in_specs=[VMEM, VMEM, ANY],
-        out_specs=(VMEM, VMEM, ANY),
+        in_specs=[VMEM, VMEM, ANY, ANY],
+        out_specs=(VMEM, VMEM, ANY, ANY),
         scratch_shapes=[pltpu.VMEM((16, rows, width), bf16)]
         + ring
         + ring
@@ -1228,31 +1601,12 @@
             pltpu.SemaphoreType.DMA((4,)),
             pltpu.SemaphoreType.DMA((4,)),
             pltpu.SemaphoreType.DMA((4,)),
-            pltpu.SemaphoreType.DMA((1,)),
+            pltpu.SemaphoreType.DMA((2,)),
         ],
         compiler_params=pltpu.CompilerParams(
             collective_id=7, has_side_effects=True, vmem_limit_bytes=48 * 2**20
         ),
-    )(grad_in, grad_out, expert_pieces)
-
-
-def dot(a, b):
-    return jnp.dot(a, b, preferred_element_type=f32)
-
-
-def dot_nt(a, b):
-    return lax.dot_general(a, b, (((1,), (1,)), ((), ())), preferred_element_type=f32)
-
-
-def dot_tn(a, b):
-    return lax.dot_general(a, b, (((0,), (0,)), ((), ())), preferred_element_type=f32)
-
-
-def exchange_halves(own, l):
-    other = lax.ppermute(own, "l", [(0, 1), (1, 0)])
-    first = jnp.where(l == 0, own, other)
-    second = jnp.where(l == 0, other, own)
-    return jnp.concatenate([first, second], axis=0)
+    )(grad_in, grad_out, expert_pieces, tokens)
 
 
 def body(
@@ -1274,12 +1628,10 @@
     c, h, l = place()
     model_width = tokens.shape[2]
     rows = tokens.shape[1] // 2
-    seq_length = segments.shape[1]
     experts, part, ff_half = w_gate.shape
     q_half = w_query.shape[1]
-    score_scale = HEAD_SIZE ** (-0.5)
-
-    misc = jnp.concatenate([attn_gain[:, None], mix_gain[:, None], w_router], axis=1)
+
+    misc = jnp.concatenate([w_router, attn_gain[:, None], mix_gain[:, None]], axis=1)
     misc = jnp.pad(misc, ((0, 0), (0, MISC - misc.shape[1])))
     attn_block = jnp.concatenate(
         [w_query, key_matrix, value_matrix, misc, w_output.T], axis=1
@@ -1288,203 +1640,84 @@
     expert_pieces = jnp.pad(
         jnp.stack([w_gate, w_up, w_down], axis=1), ((0, 0), (0, 0), (0, PAD - part), (0, 0))
     )
-    upstream_low = lax.dynamic_slice_in_dim(block_cotangent[0], l * rows, rows)
-    hot_all = routes[0][:, :, None] == jnp.arange(experts, dtype=jnp.int32)[None, None, :]
-    named = jnp.any(hot_all, axis=1)
+    kv_width = key_matrix.shape[1]
+    in_width = q_half + 2 * kv_width + MISC
+
+    z = h * 2 + l
+    inputs = lax.dynamic_slice_in_dim(tokens[0], l * rows, rows)
+    upstream = lax.dynamic_slice_in_dim(block_cotangent[0], l * rows, rows)
+    named = jnp.any(
+        routes[0][:, :, None] == jnp.arange(experts, dtype=jnp.int32)[None, None, :], axis=1
+    )
     slot_of = jnp.cumsum(named.astype(jnp.int32), axis=0) - 1
     slot_of = jnp.where(named, slot_of, -1).astype(f32).T
-    slot_of = lax.dynamic_slice_in_dim(slot_of, l * rows, rows, axis=1)[:, None, :]
+    slot_of = lax.dynamic_slice_in_dim(slot_of, l * rows, rows, axis=1)
+    named = (slot_of >= 0).astype(f32)
+    positions = z * rows + jnp.arange(rows, dtype=jnp.int32)
+    cosine, sine = rope_tables(positions)
+    seg_column = segments[0][:, None]
+    seg_row = lax.dynamic_slice_in_dim(segments[0], z * rows, rows)[None, :]
+
     w_attn, expert_col, grads_all, slots = gather_weights(
-        attn_block, expert_pieces, upstream_low, slot_of, part
+        attn_block, expert_pieces, upstream, slot_of[:, None, :], part
     )
-    kv_width = key_matrix.shape[1]
-    in_width = q_half + 2 * kv_width + MISC
     w_attn = w_attn.reshape(2, model_width, attn_block.shape[1])
-    w_out = w_attn[:, :, in_width:]
     expert_full = lax.all_gather(expert_col, ("x", "y"), axis=1, tiled=True)
-    qkv_w = w_attn[:, :, : q_half + 2 * kv_width]
-    misc_full = w_attn[0, :, q_half + 2 * kv_width : in_width]
-    attn_scale = misc_full[:, 0].astype(f32)
-    mix_scale = misc_full[:, 1].astype(f32)
-    router_w = misc_full[:, 2 : 2 + experts]
-
-    first = l * rows
-    inputs = lax.dynamic_slice_in_dim(tokens[0], first, rows).astype(f32)
-    upstream = upstream_low.astype(f32)
-    route_rows = lax.dynamic_slice_in_dim(routes[0], first, rows)
-    z = h * 2 + l
-    positions = z * rows + jnp.arange(rows, dtype=jnp.int32)
-    key_positions = jnp.arange(seq_length, dtype=jnp.int32)
-    seg_all = segments[0]
-    seg_local = lax.dynamic_slice_in_dim(seg_all, z * rows, rows)
-    allowed = (seg_local[:, None] == seg_all[None, :]) & (
-        positions[:, None] >= key_positions[None, :]
+    normed_in, q, kv, attended, lse, residual, normed_mix, gates = attention(
+        inputs, w_attn, cosine, sine, seg_column, seg_row, named
     )
-    cosine_table, sine_table = rope_tables(positions)
-
-    inv_attn = lax.rsqrt(jnp.mean(inputs * inputs, axis=1, keepdims=True) + EPS)
-    scaled_in = inputs * inv_attn
-    normalized_input = (scaled_in * attn_scale).astype(bf16)
-    halves = [dot(normalized_input, qkv_w[i]) for i in range(2)]
-    q_heads = [
-        rotary_embed(p[:, :q_half].reshape(rows, GROUP, HEAD_SIZE), cosine_table, sine_table)
-        .astype(bf16)
-        .transpose(1, 0, 2)
-        for p in halves
-    ]
-    k_own = [
-        rotary_embed(
-            p[:, None, q_half : q_half + kv_width], cosine_table, sine_table
-        ).astype(bf16)[:, 0]
-        for p in halves
-    ]
-    v_own = [p[:, q_half + kv_width :].astype(bf16) for p in halves]
-    kv_all = gather_along_z(jnp.concatenate(k_own + v_own, axis=1)).reshape(
-        seq_length, 4 * kv_width
+    mix_parts, expert_grads, mix_back, gate_back = experts_of_column(
+        normed_mix, gates, grads_all, slots.reshape(4, 2 * rows), expert_full
     )
-    keys = [kv_all[:, i * kv_width : (i + 1) * kv_width] for i in range(2)]
-    values = [kv_all[:, (2 + i) * kv_width : (3 + i) * kv_width] for i in range(2)]
-
-    def scores_of(i):
-        scores = dot_nt(q_heads[i].reshape(GROUP * rows, HEAD_SIZE), keys[i]) * score_scale
-        return jnp.where(
-            allowed[None], scores.reshape(GROUP, rows, seq_length), NEG_FILL
+    expert_sum = lax.psum_scatter(expert_grads, ("x", "y"), scatter_dimension=1, tiled=True)
+    grad_in, grad_out, tokens_back, block_out = attention_back(
+        mix_back,
+        gate_back,
+        gates,
+        normed_mix,
+        residual,
+        inputs,
+        upstream,
+        normed_in,
+        attended,
+        q,
+        kv,
+        lse,
+        cosine,
+        sine,
+        seg_column,
+        seg_row,
+        w_attn,
+        mix_parts,
+    )
+
+    pieces = (
+        jnp.pad(
+            expert_sum.reshape(3, 4, part, 2, ff_half),
+            ((0, 0), (0, 0), (0, PAD - part), (0, 0), (0, 0)),
         )
-
-    attended, log_totals = [], []
-    for i in range(2):
-        masked = scores_of(i)
-        row_peak = jnp.max(masked, axis=-1, keepdims=True)
-        expo_vals = jnp.exp(masked - row_peak)
-        row_total = jnp.sum(expo_vals, axis=-1, keepdims=True)
-        weights_low = (expo_vals / row_total).astype(bf16)
-        mixed = dot(weights_low.reshape(GROUP * rows, seq_length), values[i])
-        attended.append(
-            mixed.astype(bf16)
-            .reshape(GROUP, rows, HEAD_SIZE)
-            .transpose(1, 0, 2)
-            .reshape(rows, q_half)
-        )
-        log_totals.append(row_peak + jnp.log(row_total))
-    branch = dot_nt(attended[0], w_out[0]) + dot_nt(attended[1], w_out[1])
-    residual = inputs + branch
-
-    inv_mix = lax.rsqrt(jnp.mean(residual * residual, axis=1, keepdims=True) + EPS)
-    scaled_mix = residual * inv_mix
-    normed_mix = (scaled_mix * mix_scale).astype(bf16)
-    logits = dot(normed_mix, router_w)
-    hot_routes = (
-        route_rows[:, :, None] == jnp.arange(experts, dtype=jnp.int32)[None, None, :]
-    ).astype(f32)
-    chosen = jnp.sum(hot_routes * logits[:, None, :], axis=-1)
-    gate_expo = jnp.exp(chosen - jnp.max(chosen, axis=1, keepdims=True))
-    gate_weights = gate_expo / jnp.sum(gate_expo, axis=1, keepdims=True)
-    gate_rows = jnp.sum(gate_weights[:, :, None] * hot_routes, axis=1).T
-
-    mix_parts, expert_grads, mix_back, gate_back = experts_of_column(
-        normed_mix, gate_rows[:, None, :], grads_all, slots.reshape(4, 2 * rows), expert_full
-    )
-    mix_out, unused = column_sum(mix_parts, gate_back.reshape(8, 2, rows // 2), 6)
-    expert_sum = lax.psum_scatter(expert_grads, ("x", "y"), scatter_dimension=1, tiled=True)
-    block_out = exchange_halves((residual + mix_out).astype(bf16), l)
-
-    gate_back = jnp.sum(hot_routes * gate_back.reshape(experts, rows).T[:, None, :], axis=-1)
-    gate_mean = jnp.sum(gate_weights * gate_back, axis=1, keepdims=True)
-    chosen_grad = gate_weights * (gate_back - gate_mean)
-    logit_grad = jnp.sum(chosen_grad[:, :, None] * hot_routes, axis=1).astype(bf16)
-    grad_router = dot_tn(normed_mix, logit_grad)
-    normed_grad = mix_back + dot_nt(logit_grad, router_w)
-    grad_mix_gain = jnp.sum(normed_grad * scaled_mix, axis=0)
-    scaled_grad = normed_grad * mix_scale
-    resid_grad = (
-        upstream
-        + inv_mix * scaled_grad
-        - residual * inv_mix**3 * jnp.mean(scaled_grad * residual, axis=1, keepdims=True)
-    )
-
-    branch_low = resid_grad.astype(bf16)
-    grad_out = jnp.stack([dot_tn(branch_low, attended[i]) for i in range(2)]).astype(bf16)
-    query_low, key_parts, value_parts = [], [], []
-    for i in range(2):
-        back_low = (
-            dot(branch_low, w_out[i])
-            .astype(bf16)
-            .reshape(rows, GROUP, HEAD_SIZE)
-            .transpose(1, 0, 2)
-            .reshape(GROUP * rows, HEAD_SIZE)
-        )
-        prob_vals = jnp.exp(scores_of(i) - log_totals[i]).reshape(GROUP * rows, seq_length)
-        prob_low = prob_vals.astype(bf16)
-        prob_grad = dot_nt(back_low, values[i])
-        row_dot = jnp.sum(prob_vals * prob_grad, axis=-1, keepdims=True)
-        score_grad = (prob_vals * (prob_grad - row_dot)).astype(bf16)
-        query_grad = dot(score_grad, keys[i]) * score_scale
-        key_parts.append(
-            dot_tn(score_grad, q_heads[i].reshape(GROUP * rows, HEAD_SIZE)) * score_scale
-        )
-        value_parts.append(dot_tn(prob_low, back_low))
-        query_low.append(
-            rotate_back(
-                query_grad.reshape(GROUP, rows, HEAD_SIZE).transpose(1, 0, 2),
-                cosine_table,
-                sine_table,
-            )
-            .astype(bf16)
-            .reshape(rows, q_half)
-        )
-    kv_back = sum_along_z(
-        jnp.concatenate(key_parts + value_parts, axis=1)
-        .astype(bf16)
-        .reshape(4, rows, 4 * kv_width)
-    )
-    grad_in, normed_back = [], 0.0
-    for i in range(2):
-        key_low = rotate_back(
-            kv_back[:, None, i * kv_width : (i + 1) * kv_width], cosine_table, sine_table
-        ).astype(bf16)[:, 0]
-        value_low = kv_back[:, (2 + i) * kv_width : (3 + i) * kv_width].astype(bf16)
-        back_rows = jnp.concatenate([query_low[i], key_low, value_low], axis=1)
-        grad_in.append(dot_tn(normalized_input, back_rows))
-        normed_back = normed_back + dot_nt(back_rows, qkv_w[i])
-    grad_attn_gain = jnp.sum(normed_back * scaled_in, axis=0)
-    scaled_back = normed_back * attn_scale
-    input_grad = (
-        resid_grad
-        + inv_attn * scaled_back
-        - inputs * inv_attn**3 * jnp.mean(scaled_back * inputs, axis=1, keepdims=True)
-    )
-    input_grad = exchange_halves(input_grad.astype(bf16), l).astype(f32)
-
-    misc_grad = jnp.concatenate(
-        [grad_attn_gain[:, None], grad_mix_gain[:, None], grad_router], axis=1
-    )
-    misc_grad = jnp.pad(misc_grad, ((0, 0), (0, MISC - misc_grad.shape[1])))
-    misc_grad = jnp.stack([misc_grad, jnp.zeros_like(misc_grad)]).astype(bf16)
-    attn_grads = jnp.concatenate([jnp.stack(grad_in).astype(bf16), misc_grad], axis=2)
-
-    pieces = (
-        jnp.pad(expert_sum.reshape(3, 4, part, 2, ff_half), ((0, 0), (0, 0), (0, PAD - part), (0, 0), (0, 0)))
         .transpose(1, 3, 0, 2, 4)
         .reshape(8, 3, PAD, ff_half)
     )
-    returned, misc_back, expert_back = return_gradients(
-        attn_grads.reshape(2, 16, 4 * part, in_width),
+    returned, misc_back, expert_back, tokens_back = return_gradients(
+        grad_in.reshape(2, 16, 4 * part, in_width),
         grad_out.reshape(2, 16, 4 * part, q_half),
         pieces,
+        tokens_back,
         part,
         in_width - MISC,
     )
     expert_back = expert_back[:, :, :part].astype(f32)
     return (
-        block_out[None],
-        input_grad[None],
-        misc_back[:, 0],
+        block_out.reshape(1, 2 * rows, model_width),
+        tokens_back.reshape(1, 2 * rows, model_width).astype(f32),
+        misc_back[:, experts],
         returned[:, :q_half],
         returned[:, q_half : q_half + kv_width],
         returned[:, q_half + kv_width : q_half + 2 * kv_width],
         returned[:, in_width:].T,
-        misc_back[:, 1],
-        misc_back[:, 2 : 2 + experts],
+        misc_back[:, experts + 1],
+        misc_back[:, :experts],
         expert_back[:, 0],
         expert_back[:, 1],
         expert_back[:, 2],

time: 480 us -> 389 us (0.81); the launches traced: 472 us -> 388 us
  matrix products: 60.5 us -> 0 us
  local copies, waits for them, and re-layouts: 69.5 us -> 22.8 us
  other arithmetic: 41.5 us -> 6.37 us
  waiting for transfers between devices: 0.04 us -> 33.5 us
  Pallas kernels: 284 us -> 311 us
    dot_general x27 -> x0, matrix products: 60.5 us -> none  [the longest x9 26.7 us: dot_nt(): lax.dot_general(a, b, (((1,), (1,)), ((), ())), preferred_element_type=f32)]
    pallas_call x3 -> x2, Pallas kernels: 76.2 us -> 102 us  [the longest x1 65 us: attention_back(): pl.pallas_call(attention_back_kernel, name='attention_back', out_shape=(s...]
    all_gather x1, waiting for transfers between devices: 0.01 us -> 19.5 us  [body(): expert_full = lax.all_gather(expert_col, ('x', 'y'), axis=1, tiled=True)]
    reduce_scatter x1, waiting for transfers between devices: 0.01 us -> 14 us  [body(): lax.psum_scatter(expert_grads, ('x', 'y'), scatter_dimension=1, tiled=True)]
    unnamed x143 -> x36, local copies, waits for them, and re-layouts: 25.1 us -> 11.4 us
    convert_element_type x10 -> x3, other arithmetic: 15 us -> 2.68 us  [the longest x1 2.07 us: body(): tokens_back.reshape(1, 2 * rows, model_width).astype(f32)]
    concatenate x1 -> x0, local copies, waits for them, and re-layouts: 10.5 us -> none  [body(): jnp.concatenate([jnp.stack(grad_in).astype(bf16), misc_grad], axis=2)]
    slice x14 -> x2, local copies, waits for them, and re-layouts: 7.57 us -> 0.91 us  [the longest x1 0.7 us: body(): misc_back[:, experts + 1]]
  transfers between devices with their start and end apart: 4 -> 2, of which waited for: 0 -> 2; matrix products, arithmetic and copies ran while one was open for 27% -> 2% of each run, Pallas kernels for 7% -> 26%
where the time goes in v4:
time: 389 us; the launch traced here: 388 us
  Pallas kernels  311 us (80%)
  waiting for transfers between devices  33.5 us (9%)
  local copies, waits for them, and re-layouts  22.8 us (6%)
  between operations  14.3 us (4%)
  other arithmetic  6.37 us (2%)
    pallas_call x1, Pallas kernels, experts_of_column(): pl.pallas_call(experts_kernel, name='experts', out_shape=(jax.ShapeDtypeS...  93.5 us
    pallas_call x1, Pallas kernels, attention_back(): pl.pallas_call(attention_back_kernel, name='attention_back', out_shape=(s...  65 us
    pallas_call x1, Pallas kernels, return_gradients(): pl.pallas_call(functools.partial(return_kernel, part, misc_at), name='ret...  60.5 us
    pallas_call x1, Pallas kernels, gather_weights(): pl.pallas_call(functools.partial(weights_kernel, part), name='gather_weig...  55.2 us
    pallas_call x1, Pallas kernels, attention(): pl.pallas_call(attention_kernel, name='attention', out_shape=(sds((rows,...  36.9 us
    all_gather x1, waiting for transfers between devices, body(): expert_full = lax.all_gather(expert_col, ('x', 'y'), axis=1, tiled=True)  19.5 us
    reduce_scatter x1, waiting for transfers between devices, body(): lax.psum_scatter(expert_grads, ('x', 'y'), scatter_dimension=1, tiled=True)  14 us
    unnamed x36, local copies, waits for them, and re-layouts  11.4 us
  transfers between devices with their start and end apart: 2, of which 2 were waited for; matrix products, arithmetic and copies ran while one was open for 2% of the time, Pallas kernels for 26%

profile of v4, /device:TPU:1, one launch (start us, length us, event | category | flops | bytes accessed | tf_op | source)
XLA Modules:
  0.0 388.2 jit_solution(12782694000030876996)
XLA Ops:
  7.3 0.8 fusion.5
  8.1 0.7 copy.44
  8.9 0.7 copy.45
  9.6 0.8 copy.43
  10.4 1.1 reduce-window.6
  11.9 0.8 constant_dynamic-update-slice_fusion.3
  13.0 55.2 %gather_weights.1 = (bf16[2,16,96,1920]{3,2,1,0:T(8,128)(2,1)S(1)}, bf16[3,96,768]{2,1,0:T(8,128)(2,1)}, bf16[8,256,1536]{2,1,0:T(8,128)(2,1)S(1)}, f32[8,1,256]{2,1,0:T(1,128)S(1)}) custom-call(bf16[32,1920]{1,0:T(8,128)(2,1)S(1)} %pad.17.attn_ref, bf16[8,3,32,384]{3,2,1,0:T(8,128)(2,1)S(1)} %fusion.4.expert_ref, ...), custom_call_target="tpu_custom_call" | custom-call | tf_op jit(solution)/shard_map/gather_weights/pallas_call | solution.py:374
  68.2 4.4 %copy-done.2 = bf16[2,16,96,1920]{3,2,1,0:T(8,128)(2,1)} copy-done((bf16[2,16,96,1920]{3,2,1,0:T(8,128)(2,1)}, bf16[2,16,96,1920]{3,2,1,0:T(8,128)(2,1)S(1)}, u32[]{:S(2)}) %copy-start.2) | copy-done | bytes 11796504
  72.6 2.7 copy-done.4
  75.5 1.0 copy.47.seg_column
  76.5 1.8 broadcast_in_dim_reshape.8.slot_columns
  80.1 0.8 pad_maximum_fusion
  80.9 2.1 dynamic-slice_bitcast_fusion.1.x_ref
  83.0 36.9 %attention.1 = (bf16[256,1536]{1,0:T(8,128)(2,1)}, bf16[12,256,128]{2,1,0:T(8,128)(2,1)}, bf16[4,256,512]{2,1,0:T(8,128)(2,1)}, bf16[256,1536]{1,0:T(8,128)(2,1)...) custom-call(bf16[256,1536]{1,0:T(8,128)(2,1)} %dynamic-slice_bitcast_fusion.1., ...), custom_call_target="tpu_custom_call" | custom-call | tf_op jit(solution)/shard_map/attention/pallas_call | solution.py:577
  120.0 19.5 %all-gather.2.cloned.1.call-done.weights_ref = bf16[3,1536,768]{2,1,0:T(8,128)(2,1)} async-done(((bf16[3,96,768]{2,1,0:T(8,128)(2,1)}), bf16[3,1536,768]{2,1,0:T(8,128)(2,1)}) %all-gather.2.cloned.1.call-update) | async-done | bytes 7077904 | tf_op jit(solution)/shard_map/all_gather | solution.py:1665
  139.5 93.5 %experts.1 = (bf16[8,256,1536]{2,1,0:T(8,128)(2,1)}, bf16[3,1536,768]{2,1,0:T(8,128)(2,1)}, f32[256,1536]{1,0:T(8,128)}, f32[8,1,256]{2,1,0:T(1,128)}) custom-call(bf16[256,1536]{1,0:T(8,128)(2,1)} %get-tuple-element.37.rows_ref.b_ref, f32[8,1,256]{2,1,0:T(1,128)} %get-tuple-element.38.gate_ref.gates_ref, bf16[8,256,1536]{2,1,0:T(8,128)(2,1)} %copy-done.4, ...), custom_call_target="tpu_custom_call" | custom-call | tf_op jit(solution)/shard_map/experts/pallas_call | solution.py:1249
  233.0 65.0 %attention_back.1 = (bf16[2,1536,1152]{2,1,0:T(8,128)(2,1)}, bf16[2,1536,768]{2,1,0:T(8,128)(2,1)}, bf16[256,1536]{1,0:T(8,128)(2,1)}, bf16[2,256,1536]{2,1,0:T(8,128)(2,1)}) custom-call(f32[256,1536]{1,0:T(8,128)} %get-tuple-element.42.back_ref, f32[8,1,256]{2,1,0:T(1,128)} %get-tuple-element.43.gate_back_ref, ...), custom_call_target="tpu_custom_call" | custom-call | tf_op jit(solution)/shard_map/attention_back/pallas_call | solution.py:915
  298.0 14.0 %reduce-scatter.2.cloned.1.call-done = bf16[3,96,768]{2,1,0:T(8,128)(2,1)} async-done(((bf16[3,1536,768]{2,1,0:T(8,128)(2,1)}), bf16[3,96,768]{2,1,0:T(8,128)(2,1)}) %reduce-scatter.2.cloned.1.call-update) | async-done | bytes 442384 | tf_op jit(solution)/shard_map/reduce_scatter | solution.py:1672
  312.0 1.1 reshape.92
  313.2 60.5 %return_gradients.1 = (f32[24,1920]{1,0:T(8,128)S(1)}, f32[24,128]{1,0:T(8,128)S(1)}, bf16[8,3,32,384]{3,2,1,0:T(8,128)(2,1)S(1)}, bf16[2,256,1536]{2,1,0:T(8,128)(2,1)S(1)}) custom-call(bf16[2,16,96,1152]{3,2,1,0:T(8,128)(2,1)} %bitcast.55, bf16[2,16,96,768]{3,2,1,0:T(8,128)(2,1)} %bitcast.56, bf16[8,3,32,384]{3,2,1,0:T(8,128)(2,1)S(1)} %bitcast.51, ...), custom_call_target="tpu_custom_call" | custom-call | tf_op jit(solution)/shard_map/return_gradients/pallas_call | solution.py:1579
  376.4 0.9 slice_bitcast_fusion
  377.3 2.1 bitcast_convert_fusion
  379.4 1.1 copy.57
  380.6 0.8 copy-done.1
  (58 shorter events, 5.3 us)
Async XLA Ops:
  7.2 5.5 %copy-start = (bf16[1,512,1536]{2,1,0:T(8,128)(2,1)S(1)}, bf16[1,512,1536]{2,1,0:T(8,128)(2,1)}, u32[]{:S(2)}) copy-start(bf16[1,512,1536]{2,1,0:T(8,128)(2,1)} %param.27) | copy-start | bytes 4718596
  7.2 5.5 %copy-start.13 = (bf16[24,128]{1,0:T(8,128)(2,1)S(1)}, bf16[24,128]{1,0:T(8,128)(2,1)}, u32[]{:S(2)}) copy-start(bf16[24,128]{1,0:T(8,128)(2,1)} %param.19) | copy-start | bytes 18436
  7.2 5.6 %copy-start.14 = (bf16[24,128]{1,0:T(8,128)(2,1)S(1)}, bf16[24,128]{1,0:T(8,128)(2,1)}, u32[]{:S(2)}) copy-start(bf16[24,128]{1,0:T(8,128)(2,1)} %param.20) | copy-start | bytes 18436
  7.2 5.7 %copy-start.11 = (bf16[768,24]{0,1:T(8,128)(2,1)S(1)}, bf16[768,24]{0,1:T(8,128)(2,1)}, u32[]{:S(2)}) copy-start(bf16[768,24]{0,1:T(8,128)(2,1)} %param.21) | copy-start | bytes 110596
  7.2 5.7 %copy-start.8 = (bf16[8,24,384]{2,1,0:T(8,128)(2,1)S(1)}, bf16[8,24,384]{2,1,0:T(8,128)(2,1)}, u32[]{:S(2)}) copy-start(bf16[8,24,384]{2,1,0:T(8,128)(2,1)} %param.26) | copy-start | bytes 442372
  7.2 5.7 %copy-start.9 = (bf16[8,24,384]{2,1,0:T(8,128)(2,1)S(1)}, bf16[8,24,384]{2,1,0:T(8,128)(2,1)}, u32[]{:S(2)}) copy-start(bf16[8,24,384]{2,1,0:T(8,128)(2,1)} %param.25) | copy-start | bytes 442372
  7.2 5.7 %copy-start.10 = (bf16[8,24,384]{2,1,0:T(8,128)(2,1)S(1)}, bf16[8,24,384]{2,1,0:T(8,128)(2,1)}, u32[]{:S(2)}) copy-start(bf16[8,24,384]{2,1,0:T(8,128)(2,1)} %param.24) | copy-start | bytes 442372
  7.3 132.2 %all-gather.2.cloned.1.call-start = ((), (), s32[]{:S(2)}) async-start(), calls=%async_computation.1 | async-start | bytes 7520256 | tf_op jit(solution)/shard_map/all_gather | solution.py:1665
  12.8 62.6 %copy-start.3 = (bf16[256,1536]{1,0:T(8,128)(2,1)}, bf16[256,1536]{1,0:T(8,128)(2,1)S(1)}, u32[]{:S(2)}) copy-start(bf16[256,1536]{1,0:T(8,128)(2,1)S(1)} %dynamic-slice_bitcast_fusion.rows_ref.g_ref) | copy-start | bytes 2359300
  12.9 62.6 %copy-start.12 = (s32[1,1024]{1,0:T(1,128)S(1)}, s32[1,1024]{1,0:T(1,128)}, u32[]{:S(2)}) copy-start(s32[1,1024]{1,0:T(1,128)} %param.15) | copy-start | bytes 12292
  68.2 4.4 %copy-start.2 = (bf16[2,16,96,1920]{3,2,1,0:T(8,128)(2,1)}, bf16[2,16,96,1920]{3,2,1,0:T(8,128)(2,1)S(1)}, u32[]{:S(2)}) copy-start(bf16[2,16,96,1920]{3,2,1,0:T(8,128)(2,1)S(1)} %get-tuple-element.36) | copy-start | bytes 35389444
  72.6 2.8 copy-start.4
  75.3 5.6 %copy-start.6 = (f32[8,1,256]{2,1,0:T(1,128)}, f32[8,1,256]{2,1,0:T(1,128)S(1)}, u32[]{:S(2)}) copy-start(f32[8,1,256]{2,1,0:T(1,128)S(1)} %get-tuple-element.40) | copy-start | bytes 24580
  75.4 236.6 %reduce-scatter.2.cloned.1.call-start = ((), (), s32[]{:S(2)}) async-start(), calls=%async_computation.2 | async-start | bytes 7520256 | tf_op jit(solution)/shard_map/reduce_scatter | solution.py:1672
  298.0 15.2 %copy-start.5 = (bf16[256,1536]{1,0:T(8,128)(2,1)S(1)}, bf16[256,1536]{1,0:T(8,128)(2,1)}, u32[]{:S(2)}) copy-start(bf16[256,1536]{1,0:T(8,128)(2,1)} %get-tuple-element.55.tokens_ref) | copy-start | bytes 2359300
  377.3 2.1 copy-start.7
  379.4 2.0 copy-start.1
Sparse Core Ops, SparseCore 0:
  75.5 63.9 all-gather.1
  233.1 78.8 reduce-scatter.1
